TPU v7x, 1024 devices: a whole 8x8x8 slice. The times are simulated.
1024 devices in a mesh: cap: 64 (over z, x_hi, core), rad: 16 (over y, x_lo).
Axes of the slice: x: 8 (x_hi: 4, x_lo: 2; x = x_hi * 2 + x_lo), y: 8, z: 8, core: 2. Of those that a mesh axis runs over, the one named last changes fastest.
Arguments:
- adjoint_velocity: float32 [3, 32, 64, 128, 128], P(None, 'rad', 'cap'), may hold values from -6 to 6
- adjoint_heat: float32 [32, 64, 128, 128], P('rad', 'cap'), may hold values from -6 to 6
- forcing: float32 [3, 32, 64, 128, 128], P(None, 'rad', 'cap'), may hold values from -6 to 6
- flow_velocity: float32 [3, 32, 64, 128, 128], P(None, 'rad', 'cap'), may hold values from -4 to 4
- forward_stress: float32 [3, 32, 64, 128, 128], P(None, 'rad', 'cap'), may hold values from -6 to 6
- viscosity: float32 [32, 64, 128, 128], P('rad', 'cap'), may hold values from 0.1 to 10
- layer_mask: int32 [32], P('rad'), may hold values 0 or 1
- face_flips: int32 [64, 4], replicated, may hold values from 0 to 1, as said below
Outputs:
- new_velocity: float32 [3, 32, 64, 128, 128], P(None, 'rad', 'cap')
- new_heat: float32 [32, 64, 128, 128], P('rad', 'cap')
- viscosity_gradient: float32 [64, 128, 128], P('cap', 'rad')
Inputs may be any that keep to these rules, and one draw needn't show every extreme that they name: Equal on both sides of a shared edge: face_flips[t, 1] = face_flips[(t + 16) mod 64, 0] and face_flips[t, 3] = face_flips[(t + 1) mod 64, 2].
All inputs are finite; a program needn't handle non-finite values. No bound on the sum of `layer_mask` on one device may be relied on, other than what follows from the above.
Results may differ from a plain program's by a relative error of at most 0.00002.
Values sent between devices are 32-bit elements; how exact they have to be, the bound alone decides.
No kernel may reach another device: no remote copies, remote signals or barrier semaphores. Data moves between devices by JAX's collectives and lax.ppermute only.
A program may use at most 64 MiB of HBM per device.

v0:
```python
import jax
import jax.numpy as jnp
from jax import lax
from jax.sharding import PartitionSpec as P

ITERS = 2


relaxation = 0.8
time_step = 0.1


def extended(cells, sides, width):
    for axis, dim in sides:
        count = lax.axis_size(axis)
        ends = count - 1
        head = lax.slice_in_dim(cells, 0, width, axis=dim)
        tail = lax.slice_in_dim(cells, cells.shape[dim] - width, cells.shape[dim], axis=dim)
        cells = jnp.concatenate(
            [
                lax.ppermute(tail, axis, [(i, (i + 1) % count) for i in range(ends)]),
                cells,
                lax.ppermute(head, axis, [((i + 1) % count, i) for i in range(ends)]),
            ],
            axis=dim,
        )
    return cells


def from_behind(array, axis, by):
    count = lax.axis_size(axis)
    return lax.ppermute(array, axis, [(i, (i + by) % count) for i in range(count)])


def advance(velocity, heat_field, totals, slopes, stiffness, forcing, flow_velocity):
    operator_image = stiffness * (6.0 * velocity - totals[:3]) + velocity
    drive = jnp.stack([forcing[0], forcing[1], forcing[2] + heat_field])
    moved = velocity + relaxation * (drive - operator_image) / (6.0 * stiffness + 1.0)
    carried = 0.5 * (
        flow_velocity[0] * slopes[0] + flow_velocity[1] * slopes[1] + flow_velocity[2] * slopes[2]
    )
    warmed = heat_field + time_step * (totals[3] - 6.0 * heat_field + carried + velocity[2])
    return (moved, warmed)


def shards(
    adjoint_velocity,
    adjoint_heat,
    forcing,
    flow_velocity,
    forward_stress,
    viscosity,
    layer_mask,
    face_flips,
):
    tile_count = lax.axis_size("cap")
    quarter = tile_count // 4
    tile_index = lax.axis_index("cap")
    flip_bits = face_flips[tile_index]
    stiffness = viscosity[:, 0] * (1.0 + 4.0 * layer_mask.astype(jnp.float32))[:, None, None]
    drive_terms = forcing[:, :, 0]
    flow_local = flow_velocity[:, :, 0]
    fields_now = jnp.concatenate([adjoint_velocity[:, :, 0], adjoint_heat[None, :, 0]], 0)
    for iteration in range(ITERS):
        padded = extended(fields_now, (("rad", 1),), 1)
        from_low_row = from_behind(fields_now[:, :, -1, :], "cap", quarter)
        from_high_row = from_behind(fields_now[:, :, 0, :], "cap", -quarter)
        from_low_col = from_behind(fields_now[:, :, :, -1], "cap", 1)
        from_high_col = from_behind(fields_now[:, :, :, 0], "cap", -1)
        edge_rims = jnp.stack([from_low_row, from_high_row, from_low_col, from_high_col])
        edge_rims = jnp.where(flip_bits[:, None, None, None] == 1, edge_rims[..., ::-1], edge_rims)
        row_above = jnp.concatenate([edge_rims[0][:, :, None, :], fields_now[:, :, :-1, :]], 2)
        row_below = jnp.concatenate([fields_now[:, :, 1:, :], edge_rims[1][:, :, None, :]], 2)
        col_left = jnp.concatenate([edge_rims[2][..., None], fields_now[..., :-1]], 3)
        col_right = jnp.concatenate([fields_now[..., 1:], edge_rims[3][..., None]], 3)
        layer_below = padded[:, :-2]
        layer_above = padded[:, 2:]
        totals = row_above + row_below + col_left + col_right + layer_below + layer_above
        slopes = (
            row_below[3] - row_above[3],
            col_right[3] - col_left[3],
            layer_above[3] - layer_below[3],
        )
        moved, warmed = advance(
            fields_now[:3], fields_now[3], totals, slopes, stiffness, drive_terms, flow_local
        )
        fields_now = jnp.concatenate([moved, warmed[None]], 0)
    total_layers = fields_now.shape[1] * lax.axis_size("rad")
    partial_sum = jnp.sum(
        stiffness[None] * fields_now[:3] * forward_stress[:, :, 0], axis=(0, 1)
    ) / (3.0 * total_layers)
    partial_sum = partial_sum[None]
    summed = lax.psum(partial_sum, "rad")
    row_count = summed.shape[1] // lax.axis_size("rad")
    gradient = lax.dynamic_slice_in_dim(summed, lax.axis_index("rad") * row_count, row_count, 1)
    return (fields_now[:3][:, :, None], fields_now[3][:, None], gradient)


def solution(mesh):
    in_specs = (
        P(None, "rad", "cap", None, None),
        P("rad", "cap", None, None),
        P(None, "rad", "cap", None, None),
        P(None, "rad", "cap", None, None),
        P(None, "rad", "cap", None, None),
        P("rad", "cap", None, None),
        P("rad"),
        P(),
    )
    out_specs = (
        P(None, "rad", "cap", None, None),
        P("rad", "cap", None, None),
        P("cap", "rad", None),
    )
    return jax.shard_map(shards, mesh=mesh, in_specs=in_specs, out_specs=out_specs, check_vma=False)
```

profile of v0, /device:TPU:4, one launch (start us, length us, event | category | flops | bytes accessed | tf_op | source)
XLA Modules:
  0.0 267.6 jit_solution(5309461988646072981)
XLA Ops:
  7.2 1.0 copy.126
  8.2 1.2 copy.122
  9.4 0.8 fusion.11
  10.2 0.8 copy.128
  11.0 7.9 %collective-permute-start = (f32[4,2,128]{2,1,0:T(2,128)}, f32[4,2,128]{2,1,0:T(2,128)S(1)}, u32[]{:S(2)}, u32[]{:S(2)}) collective-permute-start(f32[4,2,128]{2,1,0:T(2,128)} %bitcast.6), channel_id=1, source_target_pairs={{0,256},{16,272},{32,288},{48,304},{64,320},{80,336},{96,352},{112... | collective-permute-start | bytes 12296 | tf_op jit(solution)/shard_map/ppermute | solution.py:32
  18.9 0.8 copy.129
  19.7 10.4 %collective-permute-start.1 = (f32[4,2,128]{2,1,0:T(2,128)}, f32[4,2,128]{2,1,0:T(2,128)S(1)}, u32[]{:S(2)}, u32[]{:S(2)}) collective-permute-start(f32[4,2,128]{2,1,0:T(2,128)} %bitcast.8), channel_id=1, source_target_pairs={{0,768},{16,784},{32,800},{48,816},{64,832},{80,848},{96,864},{112... | collective-permute-start | bytes 12296 | tf_op jit(solution)/shard_map/ppermute | solution.py:32
  30.1 0.6 fusion.68
  30.7 1.9 collective-permute-start.2
  32.6 4.5 %collective-permute-start.3 = (f32[4,2,128]{2,1,0:T(2,128)}, f32[4,2,128]{2,1,0:T(2,128)S(1)}, u32[]{:S(2)}, u32[]{:S(2)}) collective-permute-start(f32[4,2,128]{2,1,0:T(2,128)} %get-tuple-element.38), channel_id=1, source_target_pairs={{0,1008},{16,0},{32,16},{48,32},{64,48},{80,64},{96,80},{112,96},{... | collective-permute-start | bytes 12296 | tf_op jit(solution)/shard_map/ppermute | solution.py:32
  37.2 1.2 fusion.25
  38.4 4.2 %collective-permute-start.4 = (f32[4,1,128,128]{2,1,3,0:T(1,128)}, f32[4,1,128,128]{2,1,3,0:T(1,128)}, u32[]{:S(2)}, u32[]{:S(2)}) collective-permute-start(f32[4,1,128,128]{2,1,3,0:T(1,128)} %get-tuple-element.33), channel_id=1, source_target_pairs={{0,1},{1,2},{2,3},{3,4},{4,5},{5,6},{6,7},{7,8},{8,9},{9,10},{10,1... | collective-permute-start | bytes 786440 | tf_op jit(solution)/shard_map/ppermute | solution.py:21
  42.6 0.8 fusion.14
  43.6 0.8 copy-done.28
  44.4 0.6 copy-done.21
  45.1 0.7 bitcast_add_fusion.3
  46.1 1.1 fusion.16
  47.2 0.8 copy.164
  48.0 0.7 copy.165
  48.8 0.8 copy.166
  49.7 0.8 copy.167
  50.4 0.8 copy.161
  51.2 0.8 copy.162
  52.0 0.8 copy.127
  52.7 0.8 copy.134
  53.7 0.7 copy-done.31
  54.6 1.3 collective-permute-start.5
  56.1 0.3 copy.130
  56.4 0.3 copy.131
  56.7 8.3 %collective-permute-done.5 = f32[4,1,128,128]{2,1,3,0:T(1,128)} collective-permute-done((f32[4,1,128,128]{2,1,3,0:T(1,128)}, f32[4,1,128,128]{2,1,3,0:T(1,128)}, u32[]{:S(2)}, u32[]{:S(2)}) %collective-permute-start.5) | collective-permute-done | bytes 262176 | tf_op jit(solution)/shard_map/ppermute | solution.py:23
  65.0 1.9 maximum_maximum_fusion
  67.0 1.7 fusion.6
  68.8 0.5 divide_add_fusion.1
  69.4 0.4 copy-done.1
  70.1 2.4 bitcast_add_fusion.2
  72.4 1.7 fusion.71
  74.2 1.3 fusion.72
  75.5 1.0 pad_maximum_fusion.2
  76.6 1.7 fusion.8
  78.3 1.2 copy.141
  79.5 1.9 collective-permute-start.6
  81.4 1.2 copy.142
  82.6 6.2 %collective-permute-start.7 = (f32[4,2,128]{2,1,0:T(2,128)S(1)}, f32[4,2,128]{2,1,0:T(2,128)S(1)}, u32[]{:S(2)}, u32[]{:S(2)}) collective-permute-start(f32[4,2,128]{2,1,0:T(2,128)S(1)} %bitcast.251), channel_id=1, source_target_pairs={{0,768},{16,784},{32,800},{48,816},{64,832},{80,848},{96,864},{112... | collective-permute-start | bytes 12296 | tf_op jit(solution)/shard_map/ppermute | solution.py:32
  88.8 1.9 collective-permute-start.8
  90.7 4.5 %collective-permute-start.9 = (f32[4,2,128]{2,1,0:T(2,128)S(1)}, f32[4,2,128]{2,1,0:T(2,128)S(1)}, u32[]{:S(2)}, u32[]{:S(2)}) collective-permute-start(f32[4,2,128]{2,1,0:T(2,128)S(1)} %get-tuple-element.26), channel_id=1, source_target_pairs={{0,1008},{16,0},{32,16},{48,32},{64,48},{80,64},{96,80},{112,96},{... | collective-permute-start | bytes 12296 | tf_op jit(solution)/shard_map/ppermute | solution.py:32
  95.3 0.9 fusion.24
  96.2 1.3 collective-permute-start.11
  97.5 0.3 slice.301
  97.8 0.9 copy.205
  98.7 5.9 %collective-permute-start.10 = (f32[4,1,128,128]{2,1,3,0:T(1,128)}, f32[4,1,128,128]{2,1,3,0:T(1,128)}, u32[]{:S(2)}, u32[]{:S(2)}) collective-permute-start(f32[4,1,128,128]{2,1,3,0:T(1,128)} %copy.205), channel_id=1, source_target_pairs={{0,1},{1,2},{2,3},{3,4},{4,5},{5,6},{6,7},{7,8},{8,9},{9,10},{10,1... | collective-permute-start | bytes 786440 | tf_op jit(solution)/shard_map/ppermute | solution.py:21
  104.8 1.0 copy.144
  105.8 1.0 copy.146
  106.9 0.3 collective-permute-done.11
  107.2 0.5 pad_maximum_fusion.1
  107.9 1.6 collective-permute-done.10
  109.6 3.5 %fusion.2 = f32[4,2,128,128]{2,1,3,0:T(2,128)S(1)} fusion(f32[4,2,128,1]{2,1,3,0:T(2,128)S(1)} %get-tuple-element.46, f32[4,2,128,1]{2,1,3,0:T(2,128)S(1)} %get-tuple-element.47, f32[4,1,128,128]{2,1,3,0:T(1,128)} %collective-permute-done.10, f32[4,2,128,127]{2,1,3,0:T(2,128)} %get-tuple-element.22, f32[4,2,128,127]{2,1,3,0:T(2,128)} %get-tuple-element.21, ...), kind=kLoop, calls=%fused_computation.30 | loop fusion | flops 1441792 | bytes 4460544 | tf_op jit(solution)/shard_map/add | solution.py:78
  113.2 0.8 fusion.23
  114.0 0.6 multiply_bitcast_fusion
  114.9 2.7 %fusion.40 = f32[2,1,128,128]{2,0,3,1:T(2,128)S(1)} fusion(f32[3,2,128,128]{2,1,3,0:T(2,128)S(1)} %divide_add_fusion.1, f32[4,2,128,128]{2,1,3,0:T(2,128)} %copy-done.7, f32[2,1,128,128]{2,0,3,1:T(2,128)S(1)} %copy.126, f32[1,2,1,128,128]{3,1,4,2,0:T(2,128)} %copy.167, f32[1,2,128,128]{2,1,3,0:T(2,128)} %get-tuple-element.16, ...), kind=kLoop, calls=%fused_computation.92 | loop fusion | flops 1441792 | bytes 8126464 | tf_op jit(solution)/shard_map/add | solution.py:42
  117.6 0.8 copy.159
  118.4 0.9 copy.158
  119.3 139.8 %all-reduce.2.cloned.1.call-done = f32[1,128,128]{1,2,0:T(8,128)} async-done(((f32[1,128,128]{1,2,0:T(8,128)}), f32[1,128,128]{1,2,0:T(8,128)}) %all-reduce.2.cloned.1.call-update) | async-done | bytes 65552 | tf_op jit(solution)/shard_map/psum | solution.py:93
  259.2 0.9 constant_dynamic-slice_fusion
  260.1 0.7 copy.160
  (91 shorter events, 2.4 us)
Async XLA Ops:
  7.2 252.0 %all-reduce.2.cloned.1.call-start = ((), (), s32[]{:S(2)}) async-start(), calls=%async_computation | async-start | bytes 131072 | tf_op jit(solution)/shard_map/psum | solution.py:93
  11.0 43.5 %collective-permute-start = (f32[4,2,128]{2,1,0:T(2,128)}, f32[4,2,128]{2,1,0:T(2,128)S(1)}, u32[]{:S(2)}, u32[]{:S(2)}) collective-permute-start(f32[4,2,128]{2,1,0:T(2,128)} %bitcast.6), channel_id=1, source_target_pairs={{0,256},{16,272},{32,288},{48,304},{64,320},{80,336},{96,352},{112... | collective-permute-start | bytes 12296 | tf_op jit(solution)/shard_map/ppermute | solution.py:32
  19.7 36.2 %collective-permute-start.1 = (f32[4,2,128]{2,1,0:T(2,128)}, f32[4,2,128]{2,1,0:T(2,128)S(1)}, u32[]{:S(2)}, u32[]{:S(2)}) collective-permute-start(f32[4,2,128]{2,1,0:T(2,128)} %bitcast.8), channel_id=1, source_target_pairs={{0,768},{16,784},{32,800},{48,816},{64,832},{80,848},{96,864},{112... | collective-permute-start | bytes 12296 | tf_op jit(solution)/shard_map/ppermute | solution.py:32
  30.7 25.2 %collective-permute-start.2 = (f32[4,2,128]{2,1,0:T(2,128)}, f32[4,2,128]{2,1,0:T(2,128)S(1)}, u32[]{:S(2)}, u32[]{:S(2)}) collective-permute-start(f32[4,2,128]{2,1,0:T(2,128)} %get-tuple-element.37), channel_id=1, source_target_pairs={{0,16},{16,32},{32,48},{48,64},{64,80},{80,96},{96,112},{112,128},... | collective-permute-start | bytes 12296 | tf_op jit(solution)/shard_map/ppermute | solution.py:32
  32.6 23.3 %collective-permute-start.3 = (f32[4,2,128]{2,1,0:T(2,128)}, f32[4,2,128]{2,1,0:T(2,128)S(1)}, u32[]{:S(2)}, u32[]{:S(2)}) collective-permute-start(f32[4,2,128]{2,1,0:T(2,128)} %get-tuple-element.38), channel_id=1, source_target_pairs={{0,1008},{16,0},{32,16},{48,32},{64,48},{80,64},{96,80},{112,96},{... | collective-permute-start | bytes 12296 | tf_op jit(solution)/shard_map/ppermute | solution.py:32
  38.4 5.0 %copy-start.27 = (f32[3,2,1,128,128]{4,3,2,1,0:T(8,128)S(1)}, f32[3,2,1,128,128]{4,3,2,1,0:T(8,128)}, u32[]{:S(2)}) copy-start(f32[3,2,1,128,128]{4,3,2,1,0:T(8,128)} %param.10) | copy-start | bytes 1179652
  38.4 18.3 %collective-permute-start.4 = (f32[4,1,128,128]{2,1,3,0:T(1,128)}, f32[4,1,128,128]{2,1,3,0:T(1,128)}, u32[]{:S(2)}, u32[]{:S(2)}) collective-permute-start(f32[4,1,128,128]{2,1,3,0:T(1,128)} %get-tuple-element.33), channel_id=1, source_target_pairs={{0,1},{1,2},{2,3},{3,4},{4,5},{5,6},{6,7},{7,8},{8,9},{9,10},{10,1... | collective-permute-start | bytes 786440 | tf_op jit(solution)/shard_map/ppermute | solution.py:21
  43.4 1.0 copy-start.28
  44.4 0.7 copy-start.21
  45.1 0.7 copy-start.32
  45.1 0.9 copy-start.30
  47.2 19.7 %copy-start = (f32[4,2,128,127]{2,1,3,0:T(2,128)}, f32[4,2,128,127]{2,1,3,0:T(2,128)S(1)}, u32[]{:S(2)}) copy-start(f32[4,2,128,127]{2,1,3,0:T(2,128)S(1)} %get-tuple-element.29) | copy-start | bytes 1560580
  48.8 0.9 slice-start
  51.2 2.3 copy-start.29
  53.7 0.7 copy-start.31
  54.6 10.5 %collective-permute-start.5 = (f32[4,1,128,128]{2,1,3,0:T(1,128)}, f32[4,1,128,128]{2,1,3,0:T(1,128)}, u32[]{:S(2)}, u32[]{:S(2)}) collective-permute-start(f32[4,1,128,128]{2,1,3,0:T(1,128)} %get-tuple-element.34), channel_id=1, source_target_pairs={{1,0},{2,1},{3,2},{4,3},{5,4},{6,5},{7,6},{8,7},{9,8},{10,9},{11,1... | collective-permute-start | bytes 786440 | tf_op jit(solution)/shard_map/ppermute | solution.py:23
  56.7 10.3 %copy-start.2 = (f32[4,2,128,127]{2,1,3,0:T(2,128)S(1)}, f32[4,2,128,127]{2,1,3,0:T(2,128)}, u32[]{:S(2)}) copy-start(f32[4,2,128,127]{2,1,3,0:T(2,128)} %get-tuple-element.30) | copy-start | bytes 1560580
  66.9 1.7 copy-start.13
  66.9 1.7 copy-start.15
  66.9 1.7 copy-start.17
  67.0 1.7 copy-start.19
  67.0 1.7 copy-start.25
  68.6 0.8 copy-start.6
  68.7 1.2 copy-start.1
  68.7 1.2 copy-start.8
  68.7 1.3 copy-start.10
  68.7 1.3 copy-start.11
  68.7 1.3 copy-start.12
  68.8 1.3 copy-start.22
  79.5 19.2 %collective-permute-start.6 = (f32[4,2,128]{2,1,0:T(2,128)S(1)}, f32[4,2,128]{2,1,0:T(2,128)S(1)}, u32[]{:S(2)}, u32[]{:S(2)}) collective-permute-start(f32[4,2,128]{2,1,0:T(2,128)S(1)} %bitcast.252), channel_id=1, source_target_pairs={{0,256},{16,272},{32,288},{48,304},{64,320},{80,336},{96,352},{112... | collective-permute-start | bytes 12296 | tf_op jit(solution)/shard_map/ppermute | solution.py:32
  82.6 14.9 %copy-start.23 = (f32[4,2,128,128]{2,1,0,3:T(2,128)S(1)}, f32[4,2,128,128]{2,1,0,3:T(2,128)}, u32[]{:S(2)}) copy-start(f32[4,2,128,128]{2,1,0,3:T(2,128)} %pad_maximum_fusion.2) | copy-start | bytes 1572868
  82.6 21.9 %collective-permute-start.7 = (f32[4,2,128]{2,1,0:T(2,128)S(1)}, f32[4,2,128]{2,1,0:T(2,128)S(1)}, u32[]{:S(2)}, u32[]{:S(2)}) collective-permute-start(f32[4,2,128]{2,1,0:T(2,128)S(1)} %bitcast.251), channel_id=1, source_target_pairs={{0,768},{16,784},{32,800},{48,816},{64,832},{80,848},{96,864},{112... | collective-permute-start | bytes 12296 | tf_op jit(solution)/shard_map/ppermute | solution.py:32
  88.8 15.8 %collective-permute-start.8 = (f32[4,2,128]{2,1,0:T(2,128)S(1)}, f32[4,2,128]{2,1,0:T(2,128)S(1)}, u32[]{:S(2)}, u32[]{:S(2)}) collective-permute-start(f32[4,2,128]{2,1,0:T(2,128)S(1)} %get-tuple-element.25), channel_id=1, source_target_pairs={{0,16},{16,32},{32,48},{48,64},{64,80},{80,96},{96,112},{112,128},... | collective-permute-start | bytes 12296 | tf_op jit(solution)/shard_map/ppermute | solution.py:32
  90.7 13.8 %collective-permute-start.9 = (f32[4,2,128]{2,1,0:T(2,128)S(1)}, f32[4,2,128]{2,1,0:T(2,128)S(1)}, u32[]{:S(2)}, u32[]{:S(2)}) collective-permute-start(f32[4,2,128]{2,1,0:T(2,128)S(1)} %get-tuple-element.26), channel_id=1, source_target_pairs={{0,1008},{16,0},{32,16},{48,32},{64,48},{80,64},{96,80},{112,96},{... | collective-permute-start | bytes 12296 | tf_op jit(solution)/shard_map/ppermute | solution.py:32
  96.2 11.0 %collective-permute-start.11 = (f32[4,1,128,128]{2,1,0,3:T(1,128)}, f32[4,1,128,128]{2,1,0,3:T(1,128)S(1)}, u32[]{:S(2)}, u32[]{:S(2)}) collective-permute-start(f32[4,1,128,128]{2,1,0,3:T(1,128)} %fusion.24), channel_id=1, source_target_pairs={{1,0},{2,1},{3,2},{4,3},{5,4},{6,5},{7,6},{8,7},{9,8},{10,9},{11,1... | collective-permute-start | bytes 786440 | tf_op jit(solution)/shard_map/ppermute | solution.py:23
  98.7 10.8 %collective-permute-start.10 = (f32[4,1,128,128]{2,1,3,0:T(1,128)}, f32[4,1,128,128]{2,1,3,0:T(1,128)}, u32[]{:S(2)}, u32[]{:S(2)}) collective-permute-start(f32[4,1,128,128]{2,1,3,0:T(1,128)} %copy.205), channel_id=1, source_target_pairs={{0,1},{1,2},{2,3},{3,4},{4,5},{5,6},{6,7},{7,8},{8,9},{9,10},{10,1... | collective-permute-start | bytes 786440 | tf_op jit(solution)/shard_map/ppermute | solution.py:21
  106.9 2.7 %copy-start.3 = (f32[4,2,127,128]{2,1,3,0:T(2,128)S(1)}, f32[4,2,127,128]{2,1,3,0:T(2,128)}, u32[]{:S(2)}) copy-start(f32[4,2,127,128]{2,1,3,0:T(2,128)} %get-tuple-element.19) | copy-start | bytes 1560580
  106.9 2.7 %copy-start.4 = (f32[4,2,127,128]{2,1,3,0:T(2,128)S(1)}, f32[4,2,127,128]{2,1,3,0:T(2,128)}, u32[]{:S(2)}) copy-start(f32[4,2,127,128]{2,1,3,0:T(2,128)} %get-tuple-element.20) | copy-start | bytes 1560580
  106.9 2.7 %copy-start.5 = (f32[4,2,1,128]{2,1,3,0:T(2,128)S(1)}, f32[4,2,1,128]{2,1,3,0:T(2,128)}, u32[]{:S(2)}) copy-start(f32[4,2,1,128]{2,1,3,0:T(2,128)} %copy.144) | copy-start | bytes 12292
  107.2 0.7 copy-start.24
  109.5 3.6 %copy-start.14 = (f32[1,2,1,128,128]{3,1,4,2,0:T(2,128)S(1)}, f32[1,2,1,128,128]{3,1,4,2,0:T(2,128)}, u32[]{:S(2)}) copy-start(f32[1,2,1,128,128]{3,1,4,2,0:T(2,128)} %copy.161) | copy-start | bytes 393220
  109.6 3.6 %copy-start.16 = (f32[1,2,1,128,128]{3,1,4,2,0:T(2,128)S(1)}, f32[1,2,1,128,128]{3,1,4,2,0:T(2,128)}, u32[]{:S(2)}) copy-start(f32[1,2,1,128,128]{3,1,4,2,0:T(2,128)} %copy.162) | copy-start | bytes 393220
  109.6 3.6 %copy-start.18 = (f32[2,128,128]{1,0,2:T(2,128)S(1)}, f32[2,128,128]{1,0,2:T(2,128)}, u32[]{:S(2)}) copy-start(f32[2,128,128]{1,0,2:T(2,128)} %copy.127) | copy-start | bytes 393220
  109.6 3.6 %copy-start.20 = (f32[2,128,128]{1,0,2:T(2,128)S(1)}, f32[2,128,128]{1,0,2:T(2,128)}, u32[]{:S(2)}) copy-start(f32[2,128,128]{1,0,2:T(2,128)} %copy.134) | copy-start | bytes 393220
  109.6 3.6 %copy-start.26 = (f32[1,2,128,128]{2,1,3,0:T(2,128)S(1)}, f32[1,2,128,128]{2,1,3,0:T(2,128)}, u32[]{:S(2)}) copy-start(f32[1,2,128,128]{2,1,3,0:T(2,128)} %get-tuple-element.14) | copy-start | bytes 393220
  113.1 0.9 copy-start.7
  114.0 0.9 copy-start.9
Sparse Core Ops, SparseCore 0:
  114.8 144.3 all-reduce.1
where the time goes:
time: 269 us; the launch traced here: 268 us
  waiting for transfers between devices  150 us (56%)
  starting transfers between devices  52 us (19%)
  other arithmetic  26.9 us (10%)
  local copies, waits for them, and re-layouts  23.9 us (9%)
  between operations  14.6 us (5%)
    psum x1, waiting for transfers between devices, shards(): summed = lax.psum(partial_sum, 'rad')  140 us
    ppermute x8, starting transfers between devices, from_behind(): lax.ppermute(array, axis, [(i, (i + by) % count) for i in range(count)])  39.3 us
    unnamed x80, local copies, waits for them, and re-layouts  14.1 us
    ppermute x2, starting transfers between devices, extended(): lax.ppermute(tail, axis, [(i, (i + 1) % count) for i in range(ends)])  10.1 us
    ppermute x2, waiting for transfers between devices, extended(): lax.ppermute(head, axis, [((i + 1) % count, i) for i in range(ends)])  8.68 us
  transfers between devices with their start and end apart: 13, of which 4 were waited for; matrix products, arithmetic and copies ran while one was open for 9% of the time, Pallas kernels for 0%

commit v1 on v0

v1 whole, which is shorter than its diff:
```python
import jax
import jax.numpy as jnp
from jax import lax
from jax.experimental import pallas as pl
from jax.experimental.pallas import tpu as pltpu
from jax.sharding import PartitionSpec as P

RELAX = 0.8
STEP = 0.1
VMEM_BYTES = 48 * 1024 * 1024


def lanes(shape):
    return lax.broadcasted_iota(jnp.int32, shape, len(shape) - 1)


def rows(shape):
    return lax.broadcasted_iota(jnp.int32, shape, len(shape) - 2)


def shifted(plane, by, axis):
    return pltpu.roll(plane, by % plane.shape[axis], axis)


def edge_columns(planes):
    count = len(planes)
    shape = planes[0].shape
    lane = lanes(shape)
    gathered = jnp.zeros(shape, jnp.float32)
    for k, plane in enumerate(planes):
        gathered = jnp.where(lane == k, shifted(plane, k, 1), gathered)
        gathered = jnp.where(lane == count + k, shifted(plane, count + k + 1, 1), gathered)
    return gathered.T[: 2 * count]


def pack_rims(planes, row_low, row_high, col_low, col_high):
    for k, plane in enumerate(planes):
        row_low[k : k + 1, :] = plane[0:1, :]
        row_high[k : k + 1, :] = plane[-1:, :]
    columns = edge_columns(planes)
    count = len(planes)
    col_low[...] = columns[:count]
    col_high[...] = columns[count:]


def pack_kernel(velocity, heat, lower, upper, row_low, row_high, col_low, col_high):
    planes = []
    for layer, out in enumerate((lower, upper)):
        for k in range(4):
            plane = velocity[k, layer] if k < 3 else heat[layer]
            out[k] = plane
            planes.append(plane)
    pack_rims(planes, row_low, row_high, col_low, col_high)


def turned(rim, flip):
    lane = lanes(rim.shape)
    return jnp.take_along_axis(rim, jnp.where(flip == 1, rim.shape[1] - 1 - lane, lane), axis=1)


def halos(flips, from_low_row, from_high_row, from_low_col, from_high_col):
    tile = lax.axis_index("cap")
    low_row = turned(from_low_row[...], flips[tile, 0])
    high_row = turned(from_high_row[...], flips[tile, 1])
    low_col = turned(from_low_col[...], flips[tile, 2]).T
    high_col = turned(from_high_col[...], flips[tile, 3]).T
    return low_row, high_row, low_col, high_col


def lateral(plane, k, rims):
    low_row, high_row, low_col, high_col = rims
    size = plane.shape[0]
    row, lane = rows(plane.shape), lanes(plane.shape)
    above = jnp.where(row == 0, low_row[k : k + 1, :], shifted(plane, 1, 0))
    below = jnp.where(row == size - 1, high_row[k : k + 1, :], shifted(plane, -1, 0))
    left = jnp.where(lane == 0, low_col[:, k : k + 1], shifted(plane, 1, 1))
    right = jnp.where(lane == size - 1, high_col[:, k : k + 1], shifted(plane, -1, 1))
    return above, below, left, right


def cycle_layer(layer, state, below_halo, above_halo, forcing, flow, stiffness, rims):
    own = state[layer]
    new = []
    weight = RELAX / (6.0 * stiffness + 1.0)
    heat = own[3]
    for k in range(4):
        plane = own[k]
        under = below_halo[k] if layer == 0 else state[0][k]
        over = above_halo[k] if layer == 1 else state[1][k]
        up, down, left, right = lateral(plane, layer * 4 + k, rims)
        total = up + down + left + right + under + over
        if k < 3:
            image = stiffness * (6.0 * plane - total) + plane
            drive = forcing[k, layer]
            if k == 2:
                drive = drive + heat
            new.append(plane + weight * (drive - image))
        else:
            carried = 0.5 * (
                flow[0, layer] * (down - up)
                + flow[1, layer] * (right - left)
                + flow[2, layer] * (over - under)
            )
            new.append(plane + STEP * (total - 6.0 * plane + carried + own[2]))
    return new


def stiffness_of(viscosity, mask, layer):
    return viscosity[layer] * (1.0 + 4.0 * mask[layer].astype(jnp.float32))


def first_kernel(
    flips, mask, lower, upper, below_halo, above_halo, lr, hr, lc, hc, forcing, flow, viscosity,
    new_lower, new_upper, row_low, row_high, col_low, col_high,
):
    rims = halos(flips, lr, hr, lc, hc)
    state = [[ref[k] for k in range(4)] for ref in (lower, upper)]
    planes = []
    for layer, out in enumerate((new_lower, new_upper)):
        new = cycle_layer(
            layer, state, below_halo, above_halo, forcing, flow,
            stiffness_of(viscosity, mask, layer), rims,
        )
        for k in range(4):
            out[k] = new[k]
        planes += new
    pack_rims(planes, row_low, row_high, col_low, col_high)


def last_kernel(
    flips, mask, lower, upper, below_halo, above_halo, lr, hr, lc, hc, forcing, flow, viscosity,
    stress, new_velocity, new_heat, partial,
):
    rims = halos(flips, lr, hr, lc, hc)
    state = [[ref[k] for k in range(4)] for ref in (lower, upper)]
    for layer in range(2):
        stiffness = stiffness_of(viscosity, mask, layer)
        new = cycle_layer(layer, state, below_halo, above_halo, forcing, flow, stiffness, rims)
        for k in range(3):
            new_velocity[k, layer] = new[k]
        new_heat[layer] = new[3]
        share = stiffness * (
            new[0] * stress[0, layer] + new[1] * stress[1, layer] + new[2] * stress[2, layer]
        )
        if layer == 0:
            partial[...] = share
        else:
            partial[...] = (partial[...] + share) * (1.0 / 96.0)


def call(kernel, outs, scalars, arrays):
    smem = pl.BlockSpec(memory_space=pltpu.SMEM)
    vmem = pl.BlockSpec(memory_space=pltpu.VMEM)
    return pl.pallas_call(
        kernel,
        out_shape=[jax.ShapeDtypeStruct(shape, jnp.float32) for shape in outs],
        in_specs=[smem] * len(scalars) + [vmem] * len(arrays),
        out_specs=[vmem] * len(outs),
        compiler_params=pltpu.CompilerParams(vmem_limit_bytes=VMEM_BYTES),
    )(*scalars, *arrays)


def around(array, by):
    count = lax.axis_size("cap")
    return lax.ppermute(array, "cap", [(i, (i + by) % count) for i in range(count)])


def along(array, by):
    count = lax.axis_size("rad")
    return lax.ppermute(
        array, "rad", [(i, i + by) for i in range(count) if 0 <= i + by < count]
    )


def exchange(lower, upper, row_low, row_high, col_low, col_high):
    quarter = lax.axis_size("cap") // 4
    below_halo = along(upper, 1)
    above_halo = along(lower, -1)
    from_low_row = around(row_high, quarter)
    from_high_row = around(row_low, -quarter)
    from_low_col = around(col_high, 1)
    from_high_col = around(col_low, -1)
    return below_halo, above_halo, from_low_row, from_high_row, from_low_col, from_high_col


def shards(
    adjoint_velocity, adjoint_heat, forcing, flow_velocity, forward_stress, viscosity, layer_mask,
    face_flips,
):
    size = adjoint_velocity.shape[-1]
    layer_shape = (4, size, size)
    rim_shape = (8, size)
    packed = [layer_shape] * 2 + [rim_shape] * 4
    velocity, heat = adjoint_velocity[:, :, 0], adjoint_heat[:, 0]
    forces, flow, stress, visc = (
        forcing[:, :, 0], flow_velocity[:, :, 0], forward_stress[:, :, 0], viscosity[:, 0]
    )
    scalars = (face_flips, layer_mask)
    state = call(pack_kernel, packed, (), (velocity, heat))
    received = exchange(*state)
    state = call(
        first_kernel, packed, scalars, (*state[:2], *received, forces, flow, visc)
    )
    received = exchange(*state)
    new_velocity, new_heat, partial = call(
        last_kernel,
        [velocity.shape, heat.shape, (size, size)],
        scalars,
        (*state[:2], *received, forces, flow, visc, stress),
    )
    count = lax.axis_size("rad")
    pieces = lax.all_to_all(partial, "rad", 0, 0, tiled=True)
    gradient = jnp.sum(pieces.reshape(count, size // count, size), axis=0)
    return new_velocity[:, :, None], new_heat[:, None], gradient[None]


def solution(mesh):
    fields = P(None, "rad", "cap", None, None)
    scalar_field = P("rad", "cap", None, None)
    return jax.shard_map(
        shards,
        mesh=mesh,
        in_specs=(
            fields, scalar_field, fields, fields, fields, scalar_field, P("rad"), P(),
        ),
        out_specs=(fields, scalar_field, P("cap", "rad", None)),
        check_vma=False,
    )
```

time: 269 us -> 89.3 us (0.33)
  the two profiles are of different devices: /device:TPU:4 before, /device:TPU:2 now
where the time goes in v1:
time: 89.3 us; the launch traced here: 88.7 us
  starting transfers between devices  59.3 us (66%)
  blocking collectives  16.5 us (18%)
  Pallas kernels  5.26 us (6%)
  local copies, waits for them, and re-layouts  3.7 us (4%)
  waiting for transfers between devices  2.5 us (3%)
    ppermute x8, starting transfers between devices, around(): lax.ppermute(array, 'cap', [(i, (i + by) % count) for i in range(count)])  35.6 us
    ppermute x4, starting transfers between devices, along(): lax.ppermute(array, 'rad', [(i, i + by) for i in range(count) if 0 <= i +...  23.7 us
    all_to_all x1, blocking collectives, shards(): pieces = lax.all_to_all(partial, 'rad', 0, 0, tiled=True)  16.5 us
    pallas_call x3, Pallas kernels, call(): pl.pallas_call(kernel, out_shape=[jax.ShapeDtypeStruct(shape, jnp.float32...  5.26 us
    unnamed x19, local copies, waits for them, and re-layouts  3.7 us
    ppermute x8, waiting for transfers between devices, around(): lax.ppermute(array, 'cap', [(i, (i + by) % count) for i in range(count)])  2.49 us
  transfers between devices with their start and end apart: 12, of which 2 were waited for; matrix products, arithmetic and copies ran while one was open for 0% of the time, Pallas kernels for 0%

profile of v1, /device:TPU:2, one launch (start us, length us, event | category | flops | bytes accessed | tf_op | source)
XLA Modules:
  0.0 88.7 jit_solution(6315152295463251502)
XLA Ops:
  0.6 0.0 copy-start
  0.6 0.0 copy-start.4
  0.7 1.0 %copy-done.4 = f32[3,2,1,128,128]{4,3,2,1,0:T(8,128)S(1)} copy-done((f32[3,2,1,128,128]{4,3,2,1,0:T(8,128)S(1)}, f32[3,2,1,128,128]{4,3,2,1,0:T(8,128)}, u32[]{:S(2)}) %copy-start.4) | copy-done | bytes 393240
  1.7 0.0 copy-start.6
  1.7 0.9 %copy-done.6 = f32[2,1,128,128]{3,2,1,0:T(8,128)S(1)} copy-done((f32[2,1,128,128]{3,2,1,0:T(8,128)S(1)}, f32[2,1,128,128]{3,2,1,0:T(8,128)}, u32[]{:S(2)}) %copy-start.6) | copy-done | bytes 131096
  2.6 0.0 copy-start.3
  2.6 0.4 shard_map.103
  3.0 15.1 %collective-permute-start.1 = (f32[4,128,128]{2,1,0:T(8,128)S(1)}, f32[4,128,128]{2,1,0:T(8,128)S(1)}, u32[]{:S(2)}, u32[]{:S(2)}) collective-permute-start(f32[4,128,128]{2,1,0:T(8,128)S(1)} %get-tuple-element.18.lower), channel_id=1, source_target_pairs={{1,0},{2,1},{3,2},{4,3},{5,4},{6,5},{7,6},{8,7},{9,8},{10,9},{11,1... | collective-permute-start | bytes 786440 | tf_op jit(solution)/shard_map/ppermute | solution.py:170
  18.0 1.9 %collective-permute-start = (f32[4,128,128]{2,1,0:T(8,128)S(1)}, f32[4,128,128]{2,1,0:T(8,128)S(1)}, u32[]{:S(2)}, u32[]{:S(2)}) collective-permute-start(f32[4,128,128]{2,1,0:T(8,128)S(1)} %get-tuple-element.19.upper), channel_id=1, source_target_pairs={{0,1},{1,2},{2,3},{3,4},{4,5},{5,6},{6,7},{7,8},{8,9},{9,10},{10,1... | collective-permute-start | bytes 786440 | tf_op jit(solution)/shard_map/ppermute | solution.py:170
  20.0 1.9 %collective-permute-start.2 = (f32[8,128]{1,0:T(8,128)S(1)}, f32[8,128]{1,0:T(8,128)S(1)}, u32[]{:S(2)}, u32[]{:S(2)}) collective-permute-start(f32[8,128]{1,0:T(8,128)S(1)} %get-tuple-element.20), channel_id=1, source_target_pairs={{0,256},{16,272},{32,288},{48,304},{64,320},{80,336},{96,352},{112... | collective-permute-start | bytes 12296 | tf_op jit(solution)/shard_map/ppermute | solution.py:165
  21.9 0.0 copy-start.8
  21.9 6.1 %collective-permute-start.3 = (f32[8,128]{1,0:T(8,128)S(1)}, f32[8,128]{1,0:T(8,128)S(1)}, u32[]{:S(2)}, u32[]{:S(2)}) collective-permute-start(f32[8,128]{1,0:T(8,128)S(1)} %get-tuple-element.21), channel_id=1, source_target_pairs={{0,768},{16,784},{32,800},{48,816},{64,832},{80,848},{96,864},{112... | collective-permute-start | bytes 12296 | tf_op jit(solution)/shard_map/ppermute | solution.py:165
  28.0 1.9 %collective-permute-start.4 = (f32[8,128]{1,0:T(8,128)S(1)}, f32[8,128]{1,0:T(8,128)S(1)}, u32[]{:S(2)}, u32[]{:S(2)}) collective-permute-start(f32[8,128]{1,0:T(8,128)S(1)} %get-tuple-element.22), channel_id=1, source_target_pairs={{0,16},{16,32},{32,48},{48,64},{64,80},{80,96},{96,112},{112,128},... | collective-permute-start | bytes 12296 | tf_op jit(solution)/shard_map/ppermute | solution.py:165
  30.0 0.0 collective-permute-done.2.lr
  30.0 7.9 %collective-permute-start.5 = (f32[8,128]{1,0:T(8,128)S(1)}, f32[8,128]{1,0:T(8,128)S(1)}, u32[]{:S(2)}, u32[]{:S(2)}) collective-permute-start(f32[8,128]{1,0:T(8,128)S(1)} %get-tuple-element.23), channel_id=1, source_target_pairs={{0,1008},{16,0},{32,16},{48,32},{64,48},{80,64},{96,80},{112,96},{... | collective-permute-start | bytes 12296 | tf_op jit(solution)/shard_map/ppermute | solution.py:165
  37.9 0.0 copy-done.8
  37.9 0.1 copy.12.flips
  38.0 0.0 collective-permute-done.3.hr
  38.0 0.0 collective-permute-done.4.lc
  38.0 1.2 %collective-permute-done.5.hc = f32[8,128]{1,0:T(8,128)S(1)} collective-permute-done((f32[8,128]{1,0:T(8,128)S(1)}, f32[8,128]{1,0:T(8,128)S(1)}, u32[]{:S(2)}, u32[]{:S(2)}) %collective-permute-start.5) | collective-permute-done | bytes 4128 | tf_op jit(solution)/shard_map/ppermute | solution.py:165
  39.2 0.0 collective-permute-done.1.above_halo
  39.2 0.0 collective-permute-done.below_halo
  39.2 0.0 copy-start.7
  39.2 0.0 copy-done
  39.2 0.0 copy-done.3
  39.2 0.6 copy-done.7
  39.8 0.0 copy-start.1
  39.8 1.0 %copy-done.1 = f32[3,2,1,128,128]{4,3,2,1,0:T(8,128)S(1)} copy-done((f32[3,2,1,128,128]{4,3,2,1,0:T(8,128)S(1)}, f32[3,2,1,128,128]{4,3,2,1,0:T(8,128)}, u32[]{:S(2)}) %copy-start.1) | copy-done | bytes 393240
  40.8 0.0 copy-start.2
  40.8 0.0 copy-start.5
  40.8 2.2 %shard_map.104 = (f32[4,128,128]{2,1,0:T(8,128)S(1)}, f32[4,128,128]{2,1,0:T(8,128)S(1)}, f32[8,128]{1,0:T(8,128)S(1)}, f32[8,128]{1,0:T(8,128)S(1)}, f32[8,128]{1,0:T(8,128)S(1)}, /*index=5*/f32[8,128]{1,0:T(8,128)S(1)}) custom-call(s32[64,4]{1,0:T(8,128)S(1)} %copy.12.flips, s32[2]{0:T(128)S(1)} %copy-done.7, f32[4,128,128]{2,1,0:T(8,128)S(1)} %get-tuple-element.18.lower, ...), custom_call_target="tpu_custom_call" | custom-call | tf_op jit(solution)/shard_map/pallas_call | solution.py:154
  43.0 3.8 %collective-permute-start.7 = (f32[4,128,128]{2,1,0:T(8,128)S(1)}, f32[4,128,128]{2,1,0:T(8,128)S(1)}, u32[]{:S(2)}, u32[]{:S(2)}) collective-permute-start(f32[4,128,128]{2,1,0:T(8,128)S(1)} %get-tuple-element.24.lower), channel_id=1, source_target_pairs={{1,0},{2,1},{3,2},{4,3},{5,4},{6,5},{7,6},{8,7},{9,8},{10,9},{11,1... | collective-permute-start | bytes 786440 | tf_op jit(solution)/shard_map/ppermute | solution.py:170
  46.9 2.9 %collective-permute-start.6 = (f32[4,128,128]{2,1,0:T(8,128)S(1)}, f32[4,128,128]{2,1,0:T(8,128)S(1)}, u32[]{:S(2)}, u32[]{:S(2)}) collective-permute-start(f32[4,128,128]{2,1,0:T(8,128)S(1)} %get-tuple-element.25.upper), channel_id=1, source_target_pairs={{0,1},{1,2},{2,3},{3,4},{4,5},{5,6},{6,7},{7,8},{8,9},{9,10},{10,1... | collective-permute-start | bytes 786440 | tf_op jit(solution)/shard_map/ppermute | solution.py:170
  49.8 1.9 %collective-permute-start.8 = (f32[8,128]{1,0:T(8,128)S(1)}, f32[8,128]{1,0:T(8,128)S(1)}, u32[]{:S(2)}, u32[]{:S(2)}) collective-permute-start(f32[8,128]{1,0:T(8,128)S(1)} %get-tuple-element.26), channel_id=1, source_target_pairs={{0,256},{16,272},{32,288},{48,304},{64,320},{80,336},{96,352},{112... | collective-permute-start | bytes 12296 | tf_op jit(solution)/shard_map/ppermute | solution.py:165
  51.7 6.0 %collective-permute-start.9 = (f32[8,128]{1,0:T(8,128)S(1)}, f32[8,128]{1,0:T(8,128)S(1)}, u32[]{:S(2)}, u32[]{:S(2)}) collective-permute-start(f32[8,128]{1,0:T(8,128)S(1)} %get-tuple-element.27), channel_id=1, source_target_pairs={{0,768},{16,784},{32,800},{48,816},{64,832},{80,848},{96,864},{112... | collective-permute-start | bytes 12296 | tf_op jit(solution)/shard_map/ppermute | solution.py:165
  57.7 1.9 %collective-permute-start.10 = (f32[8,128]{1,0:T(8,128)S(1)}, f32[8,128]{1,0:T(8,128)S(1)}, u32[]{:S(2)}, u32[]{:S(2)}) collective-permute-start(f32[8,128]{1,0:T(8,128)S(1)} %get-tuple-element.28), channel_id=1, source_target_pairs={{0,16},{16,32},{32,48},{48,64},{64,80},{80,96},{96,112},{112,128},... | collective-permute-start | bytes 12296 | tf_op jit(solution)/shard_map/ppermute | solution.py:165
  59.7 0.0 collective-permute-done.8.lr
  59.7 7.9 %collective-permute-start.11 = (f32[8,128]{1,0:T(8,128)S(1)}, f32[8,128]{1,0:T(8,128)S(1)}, u32[]{:S(2)}, u32[]{:S(2)}) collective-permute-start(f32[8,128]{1,0:T(8,128)S(1)} %get-tuple-element.29), channel_id=1, source_target_pairs={{0,1008},{16,0},{32,16},{48,32},{64,48},{80,64},{96,80},{112,96},{... | collective-permute-start | bytes 12296 | tf_op jit(solution)/shard_map/ppermute | solution.py:165
  67.5 0.0 collective-permute-done.9.hr
  67.6 0.0 collective-permute-done.10.lc
  67.6 1.3 %collective-permute-done.11.hc = f32[8,128]{1,0:T(8,128)S(1)} collective-permute-done((f32[8,128]{1,0:T(8,128)S(1)}, f32[8,128]{1,0:T(8,128)S(1)}, u32[]{:S(2)}, u32[]{:S(2)}) %collective-permute-start.11) | collective-permute-done | bytes 4128 | tf_op jit(solution)/shard_map/ppermute | solution.py:165
  68.9 0.0 collective-permute-done.7.above_halo
  68.9 0.0 collective-permute-done.6.below_halo
  68.9 0.0 copy-done.2
  68.9 0.0 copy-done.5
  68.9 2.7 %shard_map.105 = (f32[3,2,128,128]{3,2,1,0:T(8,128)}, f32[2,128,128]{2,1,0:T(8,128)}, f32[128,128]{1,0:T(8,128)S(1)}) custom-call(s32[64,4]{1,0:T(8,128)S(1)} %copy.12.flips, s32[2]{0:T(128)S(1)} %copy-done.7, f32[4,128,128]{2,1,0:T(8,128)S(1)} %get-tuple-element.24.lower, f32[4,128,128]{2,1,0:T(8,128)S(1)} %get-tuple-element.25.upper, ...), custom_call_target="tpu_custom_call" | custom-call | tf_op jit(solution)/shard_map/pallas_call | solution.py:154
  71.6 16.5 %all_to_all.9 = f32[16,8,128]{2,1,0:T(8,128)S(1)} all-to-all(f32[16,8,128]{2,1,0:T(8,128)S(1)} %bitcast.23), channel_id=1, replica_groups=mesh['cap'=64,'rad'=16] {'rad'}, dimensions={0} | all-to-all | bytes 131072 | tf_op jit(solution)/shard_map/all_to_all | solution.py:212
  88.1 0.6 reduce_sum.9
Async XLA Ops:
  0.6 38.5 %copy-start = (f32[3,2,1,128,128]{4,3,2,1,0:T(8,128)S(1)}, f32[3,2,1,128,128]{4,3,2,1,0:T(8,128)}, u32[]{:S(2)}) copy-start(f32[3,2,1,128,128]{4,3,2,1,0:T(8,128)} %param.10) | copy-start | bytes 1179652
  0.6 1.0 %copy-start.4 = (f32[3,2,1,128,128]{4,3,2,1,0:T(8,128)S(1)}, f32[3,2,1,128,128]{4,3,2,1,0:T(8,128)}, u32[]{:S(2)}) copy-start(f32[3,2,1,128,128]{4,3,2,1,0:T(8,128)} %param.8) | copy-start | bytes 1179652
  1.7 0.9 %copy-start.6 = (f32[2,1,128,128]{3,2,1,0:T(8,128)S(1)}, f32[2,1,128,128]{3,2,1,0:T(8,128)}, u32[]{:S(2)}) copy-start(f32[2,1,128,128]{3,2,1,0:T(8,128)} %param.9) | copy-start | bytes 393220
  2.6 36.6 %copy-start.3 = (f32[2,1,128,128]{3,2,1,0:T(8,128)S(1)}, f32[2,1,128,128]{3,2,1,0:T(8,128)}, u32[]{:S(2)}) copy-start(f32[2,1,128,128]{3,2,1,0:T(8,128)} %param.13) | copy-start | bytes 393220
  3.0 36.2 %collective-permute-start.1 = (f32[4,128,128]{2,1,0:T(8,128)S(1)}, f32[4,128,128]{2,1,0:T(8,128)S(1)}, u32[]{:S(2)}, u32[]{:S(2)}) collective-permute-start(f32[4,128,128]{2,1,0:T(8,128)S(1)} %get-tuple-element.18.lower), channel_id=1, source_target_pairs={{1,0},{2,1},{3,2},{4,3},{5,4},{6,5},{7,6},{8,7},{9,8},{10,9},{11,1... | collective-permute-start | bytes 786440 | tf_op jit(solution)/shard_map/ppermute | solution.py:170
  18.0 21.1 %collective-permute-start = (f32[4,128,128]{2,1,0:T(8,128)S(1)}, f32[4,128,128]{2,1,0:T(8,128)S(1)}, u32[]{:S(2)}, u32[]{:S(2)}) collective-permute-start(f32[4,128,128]{2,1,0:T(8,128)S(1)} %get-tuple-element.19.upper), channel_id=1, source_target_pairs={{0,1},{1,2},{2,3},{3,4},{4,5},{5,6},{6,7},{7,8},{8,9},{9,10},{10,1... | collective-permute-start | bytes 786440 | tf_op jit(solution)/shard_map/ppermute | solution.py:170
  20.0 10.0 %collective-permute-start.2 = (f32[8,128]{1,0:T(8,128)S(1)}, f32[8,128]{1,0:T(8,128)S(1)}, u32[]{:S(2)}, u32[]{:S(2)}) collective-permute-start(f32[8,128]{1,0:T(8,128)S(1)} %get-tuple-element.20), channel_id=1, source_target_pairs={{0,256},{16,272},{32,288},{48,304},{64,320},{80,336},{96,352},{112... | collective-permute-start | bytes 12296 | tf_op jit(solution)/shard_map/ppermute | solution.py:165
  21.9 16.0 %copy-start.8 = (s32[64,4]{0,1:T(4,128)S(1)}, s32[64,4]{0,1:T(4,128)}, u32[]{:S(2)}) copy-start(s32[64,4]{0,1:T(4,128)} %param.15) | copy-start | bytes 3076
  21.9 16.1 %collective-permute-start.3 = (f32[8,128]{1,0:T(8,128)S(1)}, f32[8,128]{1,0:T(8,128)S(1)}, u32[]{:S(2)}, u32[]{:S(2)}) collective-permute-start(f32[8,128]{1,0:T(8,128)S(1)} %get-tuple-element.21), channel_id=1, source_target_pairs={{0,768},{16,784},{32,800},{48,816},{64,832},{80,848},{96,864},{112... | collective-permute-start | bytes 12296 | tf_op jit(solution)/shard_map/ppermute | solution.py:165
  28.0 9.9 %collective-permute-start.4 = (f32[8,128]{1,0:T(8,128)S(1)}, f32[8,128]{1,0:T(8,128)S(1)}, u32[]{:S(2)}, u32[]{:S(2)}) collective-permute-start(f32[8,128]{1,0:T(8,128)S(1)} %get-tuple-element.22), channel_id=1, source_target_pairs={{0,16},{16,32},{32,48},{48,64},{64,80},{80,96},{96,112},{112,128},... | collective-permute-start | bytes 12296 | tf_op jit(solution)/shard_map/ppermute | solution.py:165
  30.0 9.2 %collective-permute-start.5 = (f32[8,128]{1,0:T(8,128)S(1)}, f32[8,128]{1,0:T(8,128)S(1)}, u32[]{:S(2)}, u32[]{:S(2)}) collective-permute-start(f32[8,128]{1,0:T(8,128)S(1)} %get-tuple-element.23), channel_id=1, source_target_pairs={{0,1008},{16,0},{32,16},{48,32},{64,48},{80,64},{96,80},{112,96},{... | collective-permute-start | bytes 12296 | tf_op jit(solution)/shard_map/ppermute | solution.py:165
  39.2 0.7 copy-start.7
  39.8 1.0 %copy-start.1 = (f32[3,2,1,128,128]{4,3,2,1,0:T(8,128)S(1)}, f32[3,2,1,128,128]{4,3,2,1,0:T(8,128)}, u32[]{:S(2)}) copy-start(f32[3,2,1,128,128]{4,3,2,1,0:T(8,128)} %param.11) | copy-start | bytes 1179652
  40.8 28.0 %copy-start.2 = (f32[3,2,1,128,128]{4,3,2,1,0:T(8,128)S(1)}, f32[3,2,1,128,128]{4,3,2,1,0:T(8,128)}, u32[]{:S(2)}) copy-start(f32[3,2,1,128,128]{4,3,2,1,0:T(8,128)} %param.11) | copy-start | bytes 1179652
  40.8 28.0 %copy-start.5 = (f32[3,2,1,128,128]{4,3,2,1,0:T(8,128)S(1)}, f32[3,2,1,128,128]{4,3,2,1,0:T(8,128)}, u32[]{:S(2)}) copy-start(f32[3,2,1,128,128]{4,3,2,1,0:T(8,128)} %param.12) | copy-start | bytes 1179652
  43.0 25.8 %collective-permute-start.7 = (f32[4,128,128]{2,1,0:T(8,128)S(1)}, f32[4,128,128]{2,1,0:T(8,128)S(1)}, u32[]{:S(2)}, u32[]{:S(2)}) collective-permute-start(f32[4,128,128]{2,1,0:T(8,128)S(1)} %get-tuple-element.24.lower), channel_id=1, source_target_pairs={{1,0},{2,1},{3,2},{4,3},{5,4},{6,5},{7,6},{8,7},{9,8},{10,9},{11,1... | collective-permute-start | bytes 786440 | tf_op jit(solution)/shard_map/ppermute | solution.py:170
  46.9 22.0 %collective-permute-start.6 = (f32[4,128,128]{2,1,0:T(8,128)S(1)}, f32[4,128,128]{2,1,0:T(8,128)S(1)}, u32[]{:S(2)}, u32[]{:S(2)}) collective-permute-start(f32[4,128,128]{2,1,0:T(8,128)S(1)} %get-tuple-element.25.upper), channel_id=1, source_target_pairs={{0,1},{1,2},{2,3},{3,4},{4,5},{5,6},{6,7},{7,8},{8,9},{9,10},{10,1... | collective-permute-start | bytes 786440 | tf_op jit(solution)/shard_map/ppermute | solution.py:170
  49.8 9.9 %collective-permute-start.8 = (f32[8,128]{1,0:T(8,128)S(1)}, f32[8,128]{1,0:T(8,128)S(1)}, u32[]{:S(2)}, u32[]{:S(2)}) collective-permute-start(f32[8,128]{1,0:T(8,128)S(1)} %get-tuple-element.26), channel_id=1, source_target_pairs={{0,256},{16,272},{32,288},{48,304},{64,320},{80,336},{96,352},{112... | collective-permute-start | bytes 12296 | tf_op jit(solution)/shard_map/ppermute | solution.py:165
  51.7 15.8 %collective-permute-start.9 = (f32[8,128]{1,0:T(8,128)S(1)}, f32[8,128]{1,0:T(8,128)S(1)}, u32[]{:S(2)}, u32[]{:S(2)}) collective-permute-start(f32[8,128]{1,0:T(8,128)S(1)} %get-tuple-element.27), channel_id=1, source_target_pairs={{0,768},{16,784},{32,800},{48,816},{64,832},{80,848},{96,864},{112... | collective-permute-start | bytes 12296 | tf_op jit(solution)/shard_map/ppermute | solution.py:165
  57.7 9.8 %collective-permute-start.10 = (f32[8,128]{1,0:T(8,128)S(1)}, f32[8,128]{1,0:T(8,128)S(1)}, u32[]{:S(2)}, u32[]{:S(2)}) collective-permute-start(f32[8,128]{1,0:T(8,128)S(1)} %get-tuple-element.28), channel_id=1, source_target_pairs={{0,16},{16,32},{32,48},{48,64},{64,80},{80,96},{96,112},{112,128},... | collective-permute-start | bytes 12296 | tf_op jit(solution)/shard_map/ppermute | solution.py:165
  59.7 9.2 %collective-permute-start.11 = (f32[8,128]{1,0:T(8,128)S(1)}, f32[8,128]{1,0:T(8,128)S(1)}, u32[]{:S(2)}, u32[]{:S(2)}) collective-permute-start(f32[8,128]{1,0:T(8,128)S(1)} %get-tuple-element.29), channel_id=1, source_target_pairs={{0,1008},{16,0},{32,16},{48,32},{64,48},{80,64},{96,80},{112,96},{... | collective-permute-start | bytes 12296 | tf_op jit(solution)/shard_map/ppermute | solution.py:165

commit v2 on v1

v2 whole, which is shorter than its diff:
```python
import jax
import jax.numpy as jnp
from jax import lax
from jax.experimental import pallas as pl
from jax.experimental.pallas import tpu as pltpu
from jax.sharding import PartitionSpec as P

RELAX = 0.8
STEP = 0.1
VMEM_BYTES = 24 * 1024 * 1024


def lanes(shape):
    return lax.broadcasted_iota(jnp.int32, shape, len(shape) - 1)


def rows(shape):
    return lax.broadcasted_iota(jnp.int32, shape, len(shape) - 2)


def shifted(plane, by, axis):
    return pltpu.roll(plane, by % plane.shape[axis], axis)


def edge_columns(planes):
    count = len(planes)
    shape = planes[0].shape
    lane = lanes(shape)
    gathered = jnp.zeros(shape, jnp.float32)
    for k, plane in enumerate(planes):
        gathered = jnp.where(lane == k, shifted(plane, k, 1), gathered)
        gathered = jnp.where(lane == count + k, shifted(plane, count + k + 1, 1), gathered)
    return gathered.T[: 2 * count]


def pack_rims(planes, row_low, row_high, col_low, col_high):
    for k, plane in enumerate(planes):
        row_low[k : k + 1, :] = plane[0:1, :]
        row_high[k : k + 1, :] = plane[-1:, :]
    columns = edge_columns(planes)
    count = len(planes)
    col_low[...] = columns[:count]
    col_high[...] = columns[count:]


def pack_kernel(
    velocity, heat, mask, flips, lower, upper, row_low, row_high, col_low, col_high, facts,
    mask_here, flips_here, sems,
):
    copies = [
        pltpu.make_async_copy(mask, mask_here, sems.at[0]),
        pltpu.make_async_copy(flips, flips_here, sems.at[1]),
    ]
    for layer, out in enumerate((lower, upper)):
        copies.append(
            pltpu.make_async_copy(
                velocity.at[:, layer], out.at[pl.ds(0, 3)], sems.at[2 + 2 * layer]
            )
        )
        copies.append(
            pltpu.make_async_copy(heat.at[layer], out.at[3], sems.at[3 + 2 * layer])
        )
    for copy in copies:
        copy.start()
    for copy in copies:
        copy.wait()
    pack_rims(
        [ref[k] for ref in (lower, upper) for k in range(4)],
        row_low, row_high, col_low, col_high,
    )
    tile = lax.axis_index("cap")
    bits = flips_here[...]
    mine = jnp.sum(
        jnp.where(lanes(bits.shape) == tile, bits, 0).astype(jnp.float32), axis=1, keepdims=True
    )
    width = facts.shape[1]
    facts[0:4, :] = jnp.broadcast_to(mine, (4, width))
    for layer in range(2):
        scale = 1.0 + 4.0 * mask_here[layer].astype(jnp.float32)
        facts[4 + layer : 5 + layer, :] = jnp.full((1, width), scale, jnp.float32)


def turned(rim, flip):
    lane = lanes(rim.shape)
    picks = jnp.where(jnp.broadcast_to(flip, rim.shape) > 0.5, rim.shape[1] - 1 - lane, lane)
    return jnp.take_along_axis(rim, picks, axis=1)


def halos(facts, from_low_row, from_high_row, from_low_col, from_high_col):
    low_row = turned(from_low_row[...], facts[0:1, :])
    high_row = turned(from_high_row[...], facts[1:2, :])
    low_col = turned(from_low_col[...], facts[2:3, :]).T
    high_col = turned(from_high_col[...], facts[3:4, :]).T
    return low_row, high_row, low_col, high_col


def lateral(plane, k, rims):
    low_row, high_row, low_col, high_col = rims
    size = plane.shape[0]
    row, lane = rows(plane.shape), lanes(plane.shape)
    above = jnp.where(row == 0, low_row[k : k + 1, :], shifted(plane, 1, 0))
    below = jnp.where(row == size - 1, high_row[k : k + 1, :], shifted(plane, -1, 0))
    left = jnp.where(lane == 0, low_col[:, k : k + 1], shifted(plane, 1, 1))
    right = jnp.where(lane == size - 1, high_col[:, k : k + 1], shifted(plane, -1, 1))
    return above, below, left, right


def neighbours(layer, k, state, below_halo, above_halo, rims):
    under = below_halo[k] if layer == 0 else state[0][k]
    over = above_halo[k] if layer == 1 else state[1][k]
    return (*lateral(state[layer][k], layer * 4 + k, rims), under, over)


def moved(layer, state, below_halo, above_halo, forcing, stiffness, rims):
    new = []
    weight = RELAX / (6.0 * stiffness + 1.0)
    for k in range(3):
        plane = state[layer][k]
        total = sum(neighbours(layer, k, state, below_halo, above_halo, rims))
        image = stiffness * (6.0 * plane - total) + plane
        drive = forcing[k, layer]
        if k == 2:
            drive = drive + state[layer][3]
        new.append(plane + weight * (drive - image))
    return new


def warmed(layer, state, below_halo, above_halo, flow, rims):
    plane = state[layer][3]
    up, down, left, right, under, over = neighbours(
        layer, 3, state, below_halo, above_halo, rims
    )
    total = up + down + left + right + under + over
    carried = 0.5 * (
        flow[0, layer] * (down - up)
        + flow[1, layer] * (right - left)
        + flow[2, layer] * (over - under)
    )
    return plane + STEP * (total - 6.0 * plane + carried + state[layer][2])


def stiffness_of(viscosity, facts, layer):
    return viscosity[layer] * facts[4 + layer : 5 + layer, :]


def planes_of(lower, upper):
    return [[ref[k] for k in range(4)] for ref in (lower, upper)]


def first_kernel(
    facts, lower, upper, below_halo, above_halo, lr, hr, lc, hc, forcing, viscosity, flow_far,
    new_lower, new_upper, row_low, row_high, col_low, col_high, flow, sem,
):
    copy = pltpu.make_async_copy(flow_far, flow, sem)
    copy.start()
    rims = halos(facts, lr, hr, lc, hc)
    state = planes_of(lower, upper)
    planes = []
    for layer, out in enumerate((new_lower, new_upper)):
        new = moved(
            layer, state, below_halo, above_halo, forcing,
            stiffness_of(viscosity, facts, layer), rims,
        )
        for k in range(3):
            out[k] = new[k]
    copy.wait()
    for layer, out in enumerate((new_lower, new_upper)):
        out[3] = warmed(layer, state, below_halo, above_halo, flow, rims)
    planes = [ref[k] for ref in (new_lower, new_upper) for k in range(4)]
    pack_rims(planes, row_low, row_high, col_low, col_high)


def last_velocity_kernel(
    facts, lower, upper, below_halo, above_halo, lr, hr, lc, hc, forcing, viscosity, stress,
    new_velocity, partial,
):
    rims = halos(facts, lr, hr, lc, hc)
    state = planes_of(lower, upper)
    for layer in range(2):
        stiffness = stiffness_of(viscosity, facts, layer)
        new = moved(layer, state, below_halo, above_halo, forcing, stiffness, rims)
        for k in range(3):
            new_velocity[k, layer] = new[k]
        share = stiffness * (
            new[0] * stress[0, layer] + new[1] * stress[1, layer] + new[2] * stress[2, layer]
        )
        if layer == 0:
            partial[...] = share
        else:
            partial[...] = (partial[...] + share) * (1.0 / 96.0)


def last_heat_kernel(
    facts, lower, upper, below_halo, above_halo, lr, hr, lc, hc, velocity_near, flow_far,
    new_velocity, new_heat, flow, heat, sems,
):
    copies = [
        pltpu.make_async_copy(flow_far, flow, sems.at[0]),
        pltpu.make_async_copy(velocity_near, new_velocity, sems.at[1]),
    ]
    for copy in copies:
        copy.start()
    rims = halos(facts, lr, hr, lc, hc)
    state = planes_of(lower, upper)
    copies[0].wait()
    for layer in range(2):
        heat[layer] = warmed(layer, state, below_halo, above_halo, flow, rims)
    out = pltpu.make_async_copy(heat, new_heat, sems.at[2])
    out.start()
    copies[1].wait()
    out.wait()


VMEM = pl.BlockSpec(memory_space=pltpu.VMEM)
FAR = pl.BlockSpec(memory_space=pltpu.HBM)


def call(kernel, outs, near, far=(), scratch=(), out_specs=None, flops=0):
    far = [pltpu.with_memory_space_constraint(a, pltpu.HBM) for a in far]
    arrays = (*near, *far)
    moved_bytes = 4 * sum(a.size for a in arrays)
    return pl.pallas_call(
        kernel,
        out_shape=[jax.ShapeDtypeStruct(shape, jnp.float32) for shape in outs],
        in_specs=[VMEM] * len(near) + [FAR] * len(far),
        out_specs=out_specs or [VMEM] * len(outs),
        scratch_shapes=list(scratch),
        compiler_params=pltpu.CompilerParams(vmem_limit_bytes=VMEM_BYTES),
        cost_estimate=pl.CostEstimate(
            flops=flops, bytes_accessed=moved_bytes, transcendentals=0
        ),
    )(*arrays)


def around(array, by):
    count = lax.axis_size("cap")
    return lax.ppermute(array, "cap", [(i, (i + by) % count) for i in range(count)])


def along(array, by):
    count = lax.axis_size("rad")
    return lax.ppermute(
        array, "rad", [(i, i + by) for i in range(count) if 0 <= i + by < count]
    )


def exchange(lower, upper, row_low, row_high, col_low, col_high):
    quarter = lax.axis_size("cap") // 4
    below_halo = along(upper, 1)
    above_halo = along(lower, -1)
    from_low_row = around(row_high, quarter)
    from_high_row = around(row_low, -quarter)
    from_low_col = around(col_high, 1)
    from_high_col = around(col_low, -1)
    return below_halo, above_halo, from_low_row, from_high_row, from_low_col, from_high_col


def shards(
    adjoint_velocity, adjoint_heat, forcing, flow_velocity, forward_stress, viscosity, layer_mask,
    face_flips,
):
    size = adjoint_velocity.shape[-1]
    layer_shape = (4, size, size)
    rim_shape = (8, size)
    packed = [layer_shape] * 2 + [rim_shape] * 4
    velocity, heat = adjoint_velocity[:, :, 0], adjoint_heat[:, 0]
    forces, flow, stress, visc = (
        forcing[:, :, 0], flow_velocity[:, :, 0], forward_stress[:, :, 0], viscosity[:, 0]
    )
    flips = face_flips.T
    flow_here = pltpu.VMEM(flow.shape, jnp.float32)
    *state, facts = call(
        pack_kernel,
        packed + [rim_shape],
        (),
        (velocity, heat, layer_mask, flips),
        (
            pltpu.SMEM(layer_mask.shape, jnp.int32),
            pltpu.VMEM(flips.shape, jnp.int32),
            pltpu.SemaphoreType.DMA((6,)),
        ),
    )
    received = exchange(*state)
    state = call(
        first_kernel,
        packed,
        (facts, *state[:2], *received, forces, visc),
        (flow,),
        (flow_here, pltpu.SemaphoreType.DMA),
    )
    received = exchange(*state)
    near = (facts, *state[:2], *received)
    velocity_near, partial = call(
        last_velocity_kernel, [velocity.shape, (size, size)], (*near, forces, visc, stress)
    )
    pieces = lax.all_to_all(partial, "rad", 0, 0, tiled=True)
    new_velocity, new_heat = call(
        last_heat_kernel,
        [velocity.shape, heat.shape],
        (*near, velocity_near),
        (flow,),
        (flow_here, pltpu.VMEM(heat.shape, jnp.float32), pltpu.SemaphoreType.DMA((3,))),
        [FAR, FAR],
    )
    pieces, new_heat = lax.optimization_barrier((pieces, new_heat))
    count = lax.axis_size("rad")
    gradient = jnp.sum(pieces.reshape(count, size // count, size), axis=0)
    return new_velocity[:, :, None], new_heat[:, None], gradient[None]


def solution(mesh):
    fields = P(None, "rad", "cap", None, None)
    scalar_field = P("rad", "cap", None, None)
    return jax.shard_map(
        shards,
        mesh=mesh,
        in_specs=(
            fields, scalar_field, fields, fields, fields, scalar_field, P("rad"), P(),
        ),
        out_specs=(fields, scalar_field, P("cap", "rad", None)),
        check_vma=False,
    )
```

time: 89.3 us -> 85.2 us (0.954)
  blocking collectives: 16.5 us -> 0 us
  starting transfers between devices: 59.3 us -> 68.5 us
  waiting for transfers between devices: 2.5 us -> 8.14 us
  local copies, waits for them, and re-layouts: 3.7 us -> 0.01 us
  Pallas kernels: 5.26 us -> 6.54 us
    all_to_all x1 -> x0, blocking collectives: 16.5 us -> none  [shards(): pieces = lax.all_to_all(partial, 'rad', 0, 0, tiled=True)]
    all_to_all x0 -> x1, starting transfers between devices: none -> 9.14 us  [shards(): pieces = lax.all_to_all(partial, 'rad', 0, 0, tiled=True)]
    all_to_all x0 -> x1, waiting for transfers between devices: none -> 5.54 us  [shards(): pieces = lax.all_to_all(partial, 'rad', 0, 0, tiled=True)]
    unnamed x19 -> x6, local copies, waits for them, and re-layouts: 3.7 us -> 0.01 us
    pallas_call x3 -> x4, Pallas kernels: 5.26 us -> 6.54 us  [call(): pl.pallas_call(kernel, out_shape=[jax.ShapeDtypeStruct(shape, jnp.float32...]
  transfers between devices with their start and end apart: 12 -> 13, of which waited for: 2 -> 3; matrix products, arithmetic and copies ran while one was open for 0% -> 0% of each run, Pallas kernels for 0% -> 2%
where the time goes in v2:
time: 85.2 us; the launch traced here: 84.6 us
  starting transfers between devices  68.5 us (80%)
  waiting for transfers between devices  8.14 us (10%)
  Pallas kernels  6.54 us (8%)
    ppermute x8, starting transfers between devices, around(): lax.ppermute(array, 'cap', [(i, (i + by) % count) for i in range(count)])  35.6 us
    ppermute x4, starting transfers between devices, along(): lax.ppermute(array, 'rad', [(i, i + by) for i in range(count) if 0 <= i +...  23.8 us
    all_to_all x1, starting transfers between devices, shards(): pieces = lax.all_to_all(partial, 'rad', 0, 0, tiled=True)  9.14 us
    pallas_call x4, Pallas kernels, call(): pl.pallas_call(kernel, out_shape=[jax.ShapeDtypeStruct(shape, jnp.float32...  6.54 us
    all_to_all x1, waiting for transfers between devices, shards(): pieces = lax.all_to_all(partial, 'rad', 0, 0, tiled=True)  5.54 us
    ppermute x8, waiting for transfers between devices, around(): lax.ppermute(array, 'cap', [(i, (i + by) % count) for i in range(count)])  2.59 us
  transfers between devices with their start and end apart: 13, of which 3 were waited for; matrix products, arithmetic and copies ran while one was open for 0% of the time, Pallas kernels for 2%

profile of v2, /device:TPU:2, one launch (start us, length us, event | category | flops | bytes accessed | tf_op | source)
XLA Modules:
  0.0 84.6 jit_solution(5871005785608997442)
XLA Ops:
  0.6 0.0 copy-start
  0.6 0.0 copy-start.1
  0.7 1.5 %shard_map.103 = (f32[4,128,128]{2,1,0:T(8,128)S(1)}, f32[4,128,128]{2,1,0:T(8,128)S(1)}, f32[8,128]{1,0:T(8,128)S(1)}, f32[8,128]{1,0:T(8,128)S(1)}, f32[8,128]...) custom-call(f32[3,2,128,128]{3,2,1,0:T(8,128)} %bitcast.25, f32[2,128,128]{2,1,0:T(8,128)} %bitcast.27, ...), custom_call_target="tpu_custom_call" | custom-call | bytes 525320 | tf_op jit(solution)/shard_map/pallas_call | solution.py:222
  2.2 15.1 %collective-permute-start.1 = (f32[4,128,128]{2,1,0:T(8,128)S(1)}, f32[4,128,128]{2,1,0:T(8,128)S(1)}, u32[]{:S(2)}, u32[]{:S(2)}) collective-permute-start(f32[4,128,128]{2,1,0:T(8,128)S(1)} %get-tuple-element.23.lower), channel_id=1, source_target_pairs={{1,0},{2,1},{3,2},{4,3},{5,4},{6,5},{7,6},{8,7},{9,8},{10,9},{11,1... | collective-permute-start | bytes 786440 | tf_op jit(solution)/shard_map/ppermute | solution.py:242
  17.3 1.9 %collective-permute-start = (f32[4,128,128]{2,1,0:T(8,128)S(1)}, f32[4,128,128]{2,1,0:T(8,128)S(1)}, u32[]{:S(2)}, u32[]{:S(2)}) collective-permute-start(f32[4,128,128]{2,1,0:T(8,128)S(1)} %get-tuple-element.24.upper), channel_id=1, source_target_pairs={{0,1},{1,2},{2,3},{3,4},{4,5},{5,6},{6,7},{7,8},{8,9},{9,10},{10,1... | collective-permute-start | bytes 786440 | tf_op jit(solution)/shard_map/ppermute | solution.py:242
  19.2 1.9 %collective-permute-start.2 = (f32[8,128]{1,0:T(8,128)S(1)}, f32[8,128]{1,0:T(8,128)S(1)}, u32[]{:S(2)}, u32[]{:S(2)}) collective-permute-start(f32[8,128]{1,0:T(8,128)S(1)} %get-tuple-element.25), channel_id=1, source_target_pairs={{0,256},{16,272},{32,288},{48,304},{64,320},{80,336},{96,352},{112... | collective-permute-start | bytes 12296 | tf_op jit(solution)/shard_map/ppermute | solution.py:237
  21.2 6.2 %collective-permute-start.3 = (f32[8,128]{1,0:T(8,128)S(1)}, f32[8,128]{1,0:T(8,128)S(1)}, u32[]{:S(2)}, u32[]{:S(2)}) collective-permute-start(f32[8,128]{1,0:T(8,128)S(1)} %get-tuple-element.26), channel_id=1, source_target_pairs={{0,768},{16,784},{32,800},{48,816},{64,832},{80,848},{96,864},{112... | collective-permute-start | bytes 12296 | tf_op jit(solution)/shard_map/ppermute | solution.py:237
  27.3 1.9 %collective-permute-start.4 = (f32[8,128]{1,0:T(8,128)S(1)}, f32[8,128]{1,0:T(8,128)S(1)}, u32[]{:S(2)}, u32[]{:S(2)}) collective-permute-start(f32[8,128]{1,0:T(8,128)S(1)} %get-tuple-element.27), channel_id=1, source_target_pairs={{0,16},{16,32},{32,48},{48,64},{64,80},{80,96},{96,112},{112,128},... | collective-permute-start | bytes 12296 | tf_op jit(solution)/shard_map/ppermute | solution.py:237
  29.3 0.0 collective-permute-done.2.lr
  29.3 7.9 %collective-permute-start.5 = (f32[8,128]{1,0:T(8,128)S(1)}, f32[8,128]{1,0:T(8,128)S(1)}, u32[]{:S(2)}, u32[]{:S(2)}) collective-permute-start(f32[8,128]{1,0:T(8,128)S(1)} %get-tuple-element.28), channel_id=1, source_target_pairs={{0,1008},{16,0},{32,16},{48,32},{64,48},{80,64},{96,80},{112,96},{... | collective-permute-start | bytes 12296 | tf_op jit(solution)/shard_map/ppermute | solution.py:237
  37.1 0.0 collective-permute-done.3.hr
  37.2 0.0 collective-permute-done.4.lc
  37.2 1.3 %collective-permute-done.5.hc = f32[8,128]{1,0:T(8,128)S(1)} collective-permute-done((f32[8,128]{1,0:T(8,128)S(1)}, f32[8,128]{1,0:T(8,128)S(1)}, u32[]{:S(2)}, u32[]{:S(2)}) %collective-permute-start.5) | collective-permute-done | bytes 4128 | tf_op jit(solution)/shard_map/ppermute | solution.py:237
  38.5 0.0 collective-permute-done.1.above_halo
  38.5 0.0 collective-permute-done.below_halo
  38.5 0.0 copy-done
  38.5 0.0 copy-done.1
  38.5 0.0 copy-start.2
  38.5 1.6 %shard_map.104 = (f32[4,128,128]{2,1,0:T(8,128)S(1)}, f32[4,128,128]{2,1,0:T(8,128)S(1)}, f32[8,128]{1,0:T(8,128)S(1)}, f32[8,128]{1,0:T(8,128)S(1)}, f32[8,128]{1,0:T(8,128)S(1)}, /*index=5*/f32[8,128]{1,0:T(8,128)S(1)}) custom-call(f32[8,128]{1,0:T(8,128)S(1)} %get-tuple-element.22.facts, f32[4,128,128]{2,1,0:T(8,128)S(1)} %get-tuple-element.23.lower, ...), custom_call_target="tpu_custom_call" | custom-call | bytes 1986560 | tf_op jit(solution)/shard_map/pallas_call | solution.py:222
  40.1 3.8 %collective-permute-start.7 = (f32[4,128,128]{2,1,0:T(8,128)S(1)}, f32[4,128,128]{2,1,0:T(8,128)S(1)}, u32[]{:S(2)}, u32[]{:S(2)}) collective-permute-start(f32[4,128,128]{2,1,0:T(8,128)S(1)} %get-tuple-element.29.lower), channel_id=1, source_target_pairs={{1,0},{2,1},{3,2},{4,3},{5,4},{6,5},{7,6},{8,7},{9,8},{10,9},{11,1... | collective-permute-start | bytes 786440 | tf_op jit(solution)/shard_map/ppermute | solution.py:242
  43.9 2.9 %collective-permute-start.6 = (f32[4,128,128]{2,1,0:T(8,128)S(1)}, f32[4,128,128]{2,1,0:T(8,128)S(1)}, u32[]{:S(2)}, u32[]{:S(2)}) collective-permute-start(f32[4,128,128]{2,1,0:T(8,128)S(1)} %get-tuple-element.30.upper), channel_id=1, source_target_pairs={{0,1},{1,2},{2,3},{3,4},{4,5},{5,6},{6,7},{7,8},{8,9},{9,10},{10,1... | collective-permute-start | bytes 786440 | tf_op jit(solution)/shard_map/ppermute | solution.py:242
  46.8 1.9 %collective-permute-start.8 = (f32[8,128]{1,0:T(8,128)S(1)}, f32[8,128]{1,0:T(8,128)S(1)}, u32[]{:S(2)}, u32[]{:S(2)}) collective-permute-start(f32[8,128]{1,0:T(8,128)S(1)} %get-tuple-element.31), channel_id=1, source_target_pairs={{0,256},{16,272},{32,288},{48,304},{64,320},{80,336},{96,352},{112... | collective-permute-start | bytes 12296 | tf_op jit(solution)/shard_map/ppermute | solution.py:237
  48.8 6.0 %collective-permute-start.9 = (f32[8,128]{1,0:T(8,128)S(1)}, f32[8,128]{1,0:T(8,128)S(1)}, u32[]{:S(2)}, u32[]{:S(2)}) collective-permute-start(f32[8,128]{1,0:T(8,128)S(1)} %get-tuple-element.32), channel_id=1, source_target_pairs={{0,768},{16,784},{32,800},{48,816},{64,832},{80,848},{96,864},{112... | collective-permute-start | bytes 12296 | tf_op jit(solution)/shard_map/ppermute | solution.py:237
  54.8 1.9 %collective-permute-start.10 = (f32[8,128]{1,0:T(8,128)S(1)}, f32[8,128]{1,0:T(8,128)S(1)}, u32[]{:S(2)}, u32[]{:S(2)}) collective-permute-start(f32[8,128]{1,0:T(8,128)S(1)} %get-tuple-element.33), channel_id=1, source_target_pairs={{0,16},{16,32},{32,48},{48,64},{64,80},{80,96},{96,112},{112,128},... | collective-permute-start | bytes 12296 | tf_op jit(solution)/shard_map/ppermute | solution.py:237
  56.7 0.0 collective-permute-done.8.lr
  56.7 7.9 %collective-permute-start.11 = (f32[8,128]{1,0:T(8,128)S(1)}, f32[8,128]{1,0:T(8,128)S(1)}, u32[]{:S(2)}, u32[]{:S(2)}) collective-permute-start(f32[8,128]{1,0:T(8,128)S(1)} %get-tuple-element.34), channel_id=1, source_target_pairs={{0,1008},{16,0},{32,16},{48,32},{64,48},{80,64},{96,80},{112,96},{... | collective-permute-start | bytes 12296 | tf_op jit(solution)/shard_map/ppermute | solution.py:237
  64.6 0.0 collective-permute-done.9.hr
  64.6 0.0 collective-permute-done.10.lc
  64.6 1.3 %collective-permute-done.11.hc = f32[8,128]{1,0:T(8,128)S(1)} collective-permute-done((f32[8,128]{1,0:T(8,128)S(1)}, f32[8,128]{1,0:T(8,128)S(1)}, u32[]{:S(2)}, u32[]{:S(2)}) %collective-permute-start.11) | collective-permute-done | bytes 4128 | tf_op jit(solution)/shard_map/ppermute | solution.py:237
  65.9 0.0 collective-permute-done.7.above_halo
  65.9 0.0 collective-permute-done.6.below_halo
  65.9 0.0 copy-done.2
  65.9 1.4 %shard_map.105 = (f32[3,2,128,128]{3,2,1,0:T(8,128)S(1)}, f32[128,128]{1,0:T(8,128)}) custom-call(f32[8,128]{1,0:T(8,128)S(1)} %get-tuple-element.22.facts, f32[4,128,128]{2,1,0:T(8,128)S(1)} %get-tuple-element.29.lower, f32[4,128,128]{2,1,0:T(8,128)S(1)} %get-tuple-element.30.upper, f32[4,128,128]{2,1,0:T(8,128)S(1)} %collective-permute-done.6.below_halo, ...), custom_call_target="tpu_custom_call" | custom-call | bytes 1986560 | tf_op jit(solution)/shard_map/pallas_call | solution.py:222
  67.3 9.1 %all-to-all-start = ((f32[16,8,128]{2,1,0:T(8,128)}), f32[16,8,128]{2,1,0:T(8,128)S(1)}, u32[]{:S(2)}, u32[]{:S(2)}) async-start(f32[16,8,128]{2,1,0:T(8,128)} %bitcast.9), calls=%async_computation | async-start | bytes 131072 | tf_op jit(solution)/shard_map/all_to_all | solution.py:296
  76.4 2.1 %shard_map.106 = (f32[3,2,128,128]{3,2,1,0:T(8,128)}, f32[2,128,128]{2,1,0:T(8,128)}) custom-call(f32[8,128]{1,0:T(8,128)S(1)} %get-tuple-element.22.facts, f32[4,128,128]{2,1,0:T(8,128)S(1)} %get-tuple-element.29.lower, f32[4,128,128]{2,1,0:T(8,128)S(1)} %get-tuple-element.30.upper, f32[4,128,128]{2,1,0:T(8,128)S(1)} %collective-permute-done.6.below_halo, ...), custom_call_target="tpu_custom_call" | custom-call | bytes 1855488 | tf_op jit(solution)/shard_map/pallas_call | solution.py:222
  78.5 5.5 %all-to-all-done = f32[16,8,128]{2,1,0:T(8,128)S(1)} async-done(((f32[16,8,128]{2,1,0:T(8,128)}), f32[16,8,128]{2,1,0:T(8,128)S(1)}, u32[]{:S(2)}, u32[]{:S(2)}) %all-to-all-start) | async-done | bytes 65568 | tf_op jit(solution)/shard_map/all_to_all | solution.py:296
  84.0 0.6 bitcast_reduce_fusion
Async XLA Ops:
  0.6 37.8 %copy-start = (f32[3,2,1,128,128]{4,3,2,1,0:T(8,128)S(1)}, f32[3,2,1,128,128]{4,3,2,1,0:T(8,128)}, u32[]{:S(2)}) copy-start(f32[3,2,1,128,128]{4,3,2,1,0:T(8,128)} %param.10) | copy-start | bytes 1179652
  0.6 37.8 %copy-start.1 = (f32[2,1,128,128]{3,2,1,0:T(8,128)S(1)}, f32[2,1,128,128]{3,2,1,0:T(8,128)}, u32[]{:S(2)}) copy-start(f32[2,1,128,128]{3,2,1,0:T(8,128)} %param.13) | copy-start | bytes 393220
  2.2 36.2 %collective-permute-start.1 = (f32[4,128,128]{2,1,0:T(8,128)S(1)}, f32[4,128,128]{2,1,0:T(8,128)S(1)}, u32[]{:S(2)}, u32[]{:S(2)}) collective-permute-start(f32[4,128,128]{2,1,0:T(8,128)S(1)} %get-tuple-element.23.lower), channel_id=1, source_target_pairs={{1,0},{2,1},{3,2},{4,3},{5,4},{6,5},{7,6},{8,7},{9,8},{10,9},{11,1... | collective-permute-start | bytes 786440 | tf_op jit(solution)/shard_map/ppermute | solution.py:242
  17.3 21.2 %collective-permute-start = (f32[4,128,128]{2,1,0:T(8,128)S(1)}, f32[4,128,128]{2,1,0:T(8,128)S(1)}, u32[]{:S(2)}, u32[]{:S(2)}) collective-permute-start(f32[4,128,128]{2,1,0:T(8,128)S(1)} %get-tuple-element.24.upper), channel_id=1, source_target_pairs={{0,1},{1,2},{2,3},{3,4},{4,5},{5,6},{6,7},{7,8},{8,9},{9,10},{10,1... | collective-permute-start | bytes 786440 | tf_op jit(solution)/shard_map/ppermute | solution.py:242
  19.2 10.0 %collective-permute-start.2 = (f32[8,128]{1,0:T(8,128)S(1)}, f32[8,128]{1,0:T(8,128)S(1)}, u32[]{:S(2)}, u32[]{:S(2)}) collective-permute-start(f32[8,128]{1,0:T(8,128)S(1)} %get-tuple-element.25), channel_id=1, source_target_pairs={{0,256},{16,272},{32,288},{48,304},{64,320},{80,336},{96,352},{112... | collective-permute-start | bytes 12296 | tf_op jit(solution)/shard_map/ppermute | solution.py:237
  21.2 16.0 %collective-permute-start.3 = (f32[8,128]{1,0:T(8,128)S(1)}, f32[8,128]{1,0:T(8,128)S(1)}, u32[]{:S(2)}, u32[]{:S(2)}) collective-permute-start(f32[8,128]{1,0:T(8,128)S(1)} %get-tuple-element.26), channel_id=1, source_target_pairs={{0,768},{16,784},{32,800},{48,816},{64,832},{80,848},{96,864},{112... | collective-permute-start | bytes 12296 | tf_op jit(solution)/shard_map/ppermute | solution.py:237
  27.3 9.8 %collective-permute-start.4 = (f32[8,128]{1,0:T(8,128)S(1)}, f32[8,128]{1,0:T(8,128)S(1)}, u32[]{:S(2)}, u32[]{:S(2)}) collective-permute-start(f32[8,128]{1,0:T(8,128)S(1)} %get-tuple-element.27), channel_id=1, source_target_pairs={{0,16},{16,32},{32,48},{48,64},{64,80},{80,96},{96,112},{112,128},... | collective-permute-start | bytes 12296 | tf_op jit(solution)/shard_map/ppermute | solution.py:237
  29.3 9.2 %collective-permute-start.5 = (f32[8,128]{1,0:T(8,128)S(1)}, f32[8,128]{1,0:T(8,128)S(1)}, u32[]{:S(2)}, u32[]{:S(2)}) collective-permute-start(f32[8,128]{1,0:T(8,128)S(1)} %get-tuple-element.28), channel_id=1, source_target_pairs={{0,1008},{16,0},{32,16},{48,32},{64,48},{80,64},{96,80},{112,96},{... | collective-permute-start | bytes 12296 | tf_op jit(solution)/shard_map/ppermute | solution.py:237
  38.5 27.5 %copy-start.2 = (f32[3,2,1,128,128]{4,3,2,1,0:T(8,128)S(1)}, f32[3,2,1,128,128]{4,3,2,1,0:T(8,128)}, u32[]{:S(2)}) copy-start(f32[3,2,1,128,128]{4,3,2,1,0:T(8,128)} %param.12) | copy-start | bytes 1179652
  40.1 25.8 %collective-permute-start.7 = (f32[4,128,128]{2,1,0:T(8,128)S(1)}, f32[4,128,128]{2,1,0:T(8,128)S(1)}, u32[]{:S(2)}, u32[]{:S(2)}) collective-permute-start(f32[4,128,128]{2,1,0:T(8,128)S(1)} %get-tuple-element.29.lower), channel_id=1, source_target_pairs={{1,0},{2,1},{3,2},{4,3},{5,4},{6,5},{7,6},{8,7},{9,8},{10,9},{11,1... | collective-permute-start | bytes 786440 | tf_op jit(solution)/shard_map/ppermute | solution.py:242
  43.9 22.0 %collective-permute-start.6 = (f32[4,128,128]{2,1,0:T(8,128)S(1)}, f32[4,128,128]{2,1,0:T(8,128)S(1)}, u32[]{:S(2)}, u32[]{:S(2)}) collective-permute-start(f32[4,128,128]{2,1,0:T(8,128)S(1)} %get-tuple-element.30.upper), channel_id=1, source_target_pairs={{0,1},{1,2},{2,3},{3,4},{4,5},{5,6},{6,7},{7,8},{8,9},{9,10},{10,1... | collective-permute-start | bytes 786440 | tf_op jit(solution)/shard_map/ppermute | solution.py:242
  46.8 9.9 %collective-permute-start.8 = (f32[8,128]{1,0:T(8,128)S(1)}, f32[8,128]{1,0:T(8,128)S(1)}, u32[]{:S(2)}, u32[]{:S(2)}) collective-permute-start(f32[8,128]{1,0:T(8,128)S(1)} %get-tuple-element.31), channel_id=1, source_target_pairs={{0,256},{16,272},{32,288},{48,304},{64,320},{80,336},{96,352},{112... | collective-permute-start | bytes 12296 | tf_op jit(solution)/shard_map/ppermute | solution.py:237
  48.8 15.8 %collective-permute-start.9 = (f32[8,128]{1,0:T(8,128)S(1)}, f32[8,128]{1,0:T(8,128)S(1)}, u32[]{:S(2)}, u32[]{:S(2)}) collective-permute-start(f32[8,128]{1,0:T(8,128)S(1)} %get-tuple-element.32), channel_id=1, source_target_pairs={{0,768},{16,784},{32,800},{48,816},{64,832},{80,848},{96,864},{112... | collective-permute-start | bytes 12296 | tf_op jit(solution)/shard_map/ppermute | solution.py:237
  54.8 9.8 %collective-permute-start.10 = (f32[8,128]{1,0:T(8,128)S(1)}, f32[8,128]{1,0:T(8,128)S(1)}, u32[]{:S(2)}, u32[]{:S(2)}) collective-permute-start(f32[8,128]{1,0:T(8,128)S(1)} %get-tuple-element.33), channel_id=1, source_target_pairs={{0,16},{16,32},{32,48},{48,64},{64,80},{80,96},{96,112},{112,128},... | collective-permute-start | bytes 12296 | tf_op jit(solution)/shard_map/ppermute | solution.py:237
  56.7 9.2 %collective-permute-start.11 = (f32[8,128]{1,0:T(8,128)S(1)}, f32[8,128]{1,0:T(8,128)S(1)}, u32[]{:S(2)}, u32[]{:S(2)}) collective-permute-start(f32[8,128]{1,0:T(8,128)S(1)} %get-tuple-element.34), channel_id=1, source_target_pairs={{0,1008},{16,0},{32,16},{48,32},{64,48},{80,64},{96,80},{112,96},{... | collective-permute-start | bytes 12296 | tf_op jit(solution)/shard_map/ppermute | solution.py:237
  67.3 16.7 %all-to-all-start = ((f32[16,8,128]{2,1,0:T(8,128)}), f32[16,8,128]{2,1,0:T(8,128)S(1)}, u32[]{:S(2)}, u32[]{:S(2)}) async-start(f32[16,8,128]{2,1,0:T(8,128)} %bitcast.9), calls=%async_computation | async-start | bytes 131072 | tf_op jit(solution)/shard_map/all_to_all | solution.py:296

commit v3 on v2

--- a/solution.py
+++ b/solution.py
@@ -33,51 +33,101 @@
     return gathered.T[: 2 * count]
 
 
-def pack_rims(planes, row_low, row_high, col_low, col_high):
-    for k, plane in enumerate(planes):
-        row_low[k : k + 1, :] = plane[0:1, :]
-        row_high[k : k + 1, :] = plane[-1:, :]
-    columns = edge_columns(planes)
-    count = len(planes)
-    col_low[...] = columns[:count]
-    col_high[...] = columns[count:]
+def plane_of(ref, k):
+    size = ref.shape[1]
+    return ref[k * size : (k + 1) * size, :]
+
+
+EDGE, SECOND, STIFF, FORCE, FLOW, CORNERS = (slice(8 * n, 8 * n + 8) for n in range(6))
+ROW_MESSAGE = 48
+KEPT = 40
 
 
 def pack_kernel(
-    velocity, heat, mask, flips, lower, upper, row_low, row_high, col_low, col_high, facts,
-    mask_here, flips_here, sems,
+    velocity, heat, mask, flips, forcing, flow, viscosity,
+    lower, upper, row_low, row_high, col_low, col_high, facts,
+    mask_here, flips_here, forcing_rims, flow_rims, viscosity_rims, sems, rim_sem,
 ):
+    size = lower.shape[1]
     copies = [
         pltpu.make_async_copy(mask, mask_here, sems.at[0]),
         pltpu.make_async_copy(flips, flips_here, sems.at[1]),
     ]
     for layer, out in enumerate((lower, upper)):
-        copies.append(
-            pltpu.make_async_copy(
-                velocity.at[:, layer], out.at[pl.ds(0, 3)], sems.at[2 + 2 * layer]
+        for k in range(4):
+            copies.append(
+                pltpu.make_async_copy(
+                    velocity.at[k, layer] if k < 3 else heat.at[layer],
+                    out.at[pl.ds(k * size, size)],
+                    sems.at[2 + 4 * layer + k],
+                )
             )
-        )
-        copies.append(
-            pltpu.make_async_copy(heat.at[layer], out.at[3], sems.at[3 + 2 * layer])
-        )
+    for side, start in enumerate((0, size - 8)):
+        for n, (source, target) in enumerate(
+            ((forcing, forcing_rims), (flow, flow_rims), (viscosity, viscosity_rims))
+        ):
+            here = (slice(None),) * (len(source.shape) - 2) + (pl.ds(start, 8),)
+            copies.append(
+                pltpu.make_async_copy(
+                    source.at[here], target.at[side], rim_sem.at[3 * side + n]
+                )
+            )
     for copy in copies:
         copy.start()
     for copy in copies:
         copy.wait()
-    pack_rims(
-        [ref[k] for ref in (lower, upper) for k in range(4)],
-        row_low, row_high, col_low, col_high,
-    )
+
+    width = facts.shape[1]
+    tiles = lax.axis_size("cap")
     tile = lax.axis_index("cap")
     bits = flips_here[...]
-    mine = jnp.sum(
-        jnp.where(lanes(bits.shape) == tile, bits, 0).astype(jnp.float32), axis=1, keepdims=True
-    )
-    width = facts.shape[1]
-    facts[0:4, :] = jnp.broadcast_to(mine, (4, width))
+    row = rows(bits.shape)
+
+    def bits_of(at):
+        picked = jnp.where(lanes(bits.shape) == lax.rem(at + tiles, tiles), bits, 0)
+        return jnp.sum(picked.astype(jnp.float32), axis=1, keepdims=True)
+
+    facts[0:4, :] = jnp.broadcast_to(bits_of(tile), (4, width))
+    facts[8:12, :] = jnp.broadcast_to(bits_of(tile - tiles // 4), (4, width))
+    facts[12:16, :] = jnp.broadcast_to(bits_of(tile + tiles // 4), (4, width))
     for layer in range(2):
         scale = 1.0 + 4.0 * mask_here[layer].astype(jnp.float32)
         facts[4 + layer : 5 + layer, :] = jnp.full((1, width), scale, jnp.float32)
+
+    planes = [plane_of(ref, k) for ref in (lower, upper) for k in range(4)]
+    for side, (out, edge, second, rim) in enumerate(
+        ((row_low, 0, 1, 0), (row_high, size - 1, size - 2, 7))
+    ):
+        for layer in range(2):
+            scale = facts[4 + layer : 5 + layer, :]
+            for k in range(4):
+                at = 4 * layer + k
+                plane = planes[at]
+                out[at : at + 1, :] = plane[edge : edge + 1, :]
+                out[8 + at : 9 + at, :] = plane[second : second + 1, :]
+                if k < 3:
+                    stiff = viscosity_rims[side, layer, rim : rim + 1, :] * scale
+                    force = forcing_rims[side, k, layer, rim : rim + 1, :]
+                    carry = jnp.zeros((1, width), jnp.float32)
+                else:
+                    stiff = flow_rims[side, 0, layer, rim : rim + 1, :]
+                    force = flow_rims[side, 1, layer, rim : rim + 1, :]
+                    carry = flow_rims[side, 2, layer, rim : rim + 1, :]
+                out[16 + at : 17 + at, :] = stiff
+                out[24 + at : 25 + at, :] = force
+                out[32 + at : 33 + at, :] = carry
+    first, last = row_low[EDGE, :], row_high[EDGE, :]
+    lane = lanes(first.shape)
+    corners = jnp.where(
+        lane < 2,
+        jnp.where(lane == 0, first, shifted(first, 2, 1)),
+        jnp.where(lane == 2, shifted(last, 2, 1), shifted(last, 4, 1)),
+    )
+    row_low[CORNERS, :] = corners
+    row_high[CORNERS, :] = corners
+    columns = edge_columns(planes)
+    col_low[...] = columns[:8]
+    col_high[...] = columns[8:]
 
 
 def turned(rim, flip):
@@ -86,12 +136,8 @@
     return jnp.take_along_axis(rim, picks, axis=1)
 
 
-def halos(facts, from_low_row, from_high_row, from_low_col, from_high_col):
-    low_row = turned(from_low_row[...], facts[0:1, :])
-    high_row = turned(from_high_row[...], facts[1:2, :])
-    low_col = turned(from_low_col[...], facts[2:3, :]).T
-    high_col = turned(from_high_col[...], facts[3:4, :]).T
-    return low_row, high_row, low_col, high_col
+def columns_of(facts, low, high):
+    return turned(low[:8, :], facts[2:3, :]).T, turned(high[:8, :], facts[3:4, :]).T
 
 
 def lateral(plane, k, rims):
@@ -106,8 +152,8 @@
 
 
 def neighbours(layer, k, state, below_halo, above_halo, rims):
-    under = below_halo[k] if layer == 0 else state[0][k]
-    over = above_halo[k] if layer == 1 else state[1][k]
+    under = plane_of(below_halo, k) if layer == 0 else state[0][k]
+    over = plane_of(above_halo, k) if layer == 1 else state[1][k]
     return (*lateral(state[layer][k], layer * 4 + k, rims), under, over)
 
 
@@ -144,37 +190,109 @@
 
 
 def planes_of(lower, upper):
-    return [[ref[k] for k in range(4)] for ref in (lower, upper)]
+    return [[plane_of(ref, k) for k in range(4)] for ref in (lower, upper)]
+
+
+def halo_row(message, own, below, above, left_end, right_end, flip, low):
+    edge, second = message[EDGE], message[SECOND]
+    lane, row = lanes(edge.shape), rows(edge.shape)
+    left = jnp.where(lane == 0, left_end, shifted(edge, 1, 1))
+    right = jnp.where(lane == edge.shape[1] - 1, right_end, shifted(edge, -1, 1))
+    other = shifted(edge, 4, 0)
+    under = jnp.where(row < 4, shifted(below, 4, 0), other)
+    over = jnp.where(row < 4, other, shifted(above, 4, 0))
+    total = own + second + left + right + under + over
+    stiffness = message[STIFF]
+    image = stiffness * (6.0 * edge - total) + edge
+    field = row % 4
+    drive = message[FORCE] + jnp.where(field == 2, shifted(edge, -1, 0), 0.0)
+    velocity = edge + (RELAX / (6.0 * stiffness + 1.0)) * (drive - image)
+    step_i = own - second if low else second - own
+    step_j = (right - left) * (1.0 - 2.0 * flip)
+    carried = 0.5 * (
+        message[STIFF] * step_i + message[FORCE] * step_j + message[FLOW] * (over - under)
+    )
+    heat = edge + STEP * (total - 6.0 * edge + carried + shifted(edge, 1, 0))
+    return jnp.where(field == 3, heat, velocity)
+
+
+def halo_rows(facts, kept, row_low, row_high, below_halo, above_halo, low_col, high_col):
+    size = facts.shape[1]
+    below, above = below_halo[4 * size :, :], above_halo[4 * size :, :]
+    at_low, at_high = low_col[8:16, :], high_col[8:16, :]
+
+    def chosen(flag, corners, one, zero):
+        flag = jnp.broadcast_to(facts[flag : flag + 1, 0:1], (8, 1))
+        return jnp.where(flag > 0.5, corners[:, one : one + 1], corners[:, zero : zero + 1])
+
+    made = []
+    for side, own in enumerate((row_low, row_high)):
+        flip = facts[side : side + 1, :]
+        if side == 0:
+            before = chosen(8 + 2, at_low, 1, 3)
+            after = chosen(8 + 3, at_high, 0, 2)
+        else:
+            before = chosen(12 + 2, at_low, 4 + 3, 4 + 1)
+            after = chosen(12 + 3, at_high, 4 + 2, 4 + 0)
+        swap = jnp.broadcast_to(flip[:, 0:1], (8, 1)) > 0.5
+        made.append(
+            halo_row(
+                kept[KEPT * side : KEPT * (side + 1), :],
+                own[EDGE, :],
+                below[8 * side : 8 * side + 8],
+                above[8 * side : 8 * side + 8],
+                jnp.where(swap, after, before),
+                jnp.where(swap, before, after),
+                flip,
+                side == 0,
+            )
+        )
+    return made
 
 
 def first_kernel(
     facts, lower, upper, below_halo, above_halo, lr, hr, lc, hc, forcing, viscosity, flow_far,
-    new_lower, new_upper, row_low, row_high, col_low, col_high, flow, sem,
+    new_lower, new_upper, col_low, col_high, kept, flow, sem,
 ):
     copy = pltpu.make_async_copy(flow_far, flow, sem)
     copy.start()
-    rims = halos(facts, lr, hr, lc, hc)
+    size = facts.shape[1]
+    for side, message in enumerate((lr, hr)):
+        kept[KEPT * side : KEPT * (side + 1), :] = turned(
+            message[:KEPT, :], facts[side : side + 1, :]
+        )
+    edges = [kept[KEPT * side : KEPT * side + 8, :] for side in range(2)]
+    rims = (*edges, *columns_of(facts, lc, hc))
     state = planes_of(lower, upper)
-    planes = []
-    for layer, out in enumerate((new_lower, new_upper)):
+    outs = (new_lower, new_upper)
+    for layer, out in enumerate(outs):
         new = moved(
             layer, state, below_halo, above_halo, forcing,
             stiffness_of(viscosity, facts, layer), rims,
         )
         for k in range(3):
-            out[k] = new[k]
+            out[k * size : (k + 1) * size, :] = new[k]
+        for side in range(2):
+            out[4 * size + 8 * side : 4 * size + 8 * side + 8, :] = edges[side]
     copy.wait()
-    for layer, out in enumerate((new_lower, new_upper)):
-        out[3] = warmed(layer, state, below_halo, above_halo, flow, rims)
-    planes = [ref[k] for ref in (new_lower, new_upper) for k in range(4)]
-    pack_rims(planes, row_low, row_high, col_low, col_high)
+    for layer, out in enumerate(outs):
+        out[3 * size : 4 * size, :] = warmed(layer, state, below_halo, above_halo, flow, rims)
+    columns = edge_columns([plane_of(ref, k) for ref in outs for k in range(4)])
+    corners = lr[CORNERS, :]
+    corners = jnp.where(lanes(corners.shape) < 4, corners, shifted(hr[CORNERS, :], 4, 1))
+    for n, out in enumerate((col_low, col_high)):
+        out[0:8, :] = columns[8 * n : 8 * n + 8]
+        out[8:16, :] = corners
 
 
 def last_velocity_kernel(
-    facts, lower, upper, below_halo, above_halo, lr, hr, lc, hc, forcing, viscosity, stress,
-    new_velocity, partial,
+    facts, lower, upper, below_halo, above_halo, lc, hc, kept, row_low, row_high, forcing,
+    viscosity, stress, new_velocity, partial, edge_rows,
 ):
-    rims = halos(facts, lr, hr, lc, hc)
+    edges = halo_rows(facts, kept, row_low, row_high, below_halo, above_halo, lc, hc)
+    for side in range(2):
+        edge_rows[8 * side : 8 * side + 8, :] = edges[side]
+    rims = (*edges, *columns_of(facts, lc, hc))
     state = planes_of(lower, upper)
     for layer in range(2):
         stiffness = stiffness_of(viscosity, facts, layer)
@@ -191,7 +309,7 @@
 
 
 def last_heat_kernel(
-    facts, lower, upper, below_halo, above_halo, lr, hr, lc, hc, velocity_near, flow_far,
+    facts, lower, upper, below_halo, above_halo, lc, hc, edge_rows, velocity_near, flow_far,
     new_velocity, new_heat, flow, heat, sems,
 ):
     copies = [
@@ -200,7 +318,7 @@
     ]
     for copy in copies:
         copy.start()
-    rims = halos(facts, lr, hr, lc, hc)
+    rims = (edge_rows[0:8, :], edge_rows[8:16, :], *columns_of(facts, lc, hc))
     state = planes_of(lower, upper)
     copies[0].wait()
     for layer in range(2):
@@ -244,15 +362,12 @@
     )
 
 
-def exchange(lower, upper, row_low, row_high, col_low, col_high):
-    quarter = lax.axis_size("cap") // 4
-    below_halo = along(upper, 1)
-    above_halo = along(lower, -1)
-    from_low_row = around(row_high, quarter)
-    from_high_row = around(row_low, -quarter)
-    from_low_col = around(col_high, 1)
-    from_high_col = around(col_low, -1)
-    return below_halo, above_halo, from_low_row, from_high_row, from_low_col, from_high_col
+def radial(lower, upper):
+    return along(upper, 1), along(lower, -1)
+
+
+def beside(low, high, step):
+    return around(high, step), around(low, -step)
 
 
 def shards(
@@ -260,44 +375,49 @@
     face_flips,
 ):
     size = adjoint_velocity.shape[-1]
-    layer_shape = (4, size, size)
-    rim_shape = (8, size)
-    packed = [layer_shape] * 2 + [rim_shape] * 4
+    quarter = lax.axis_size("cap") // 4
     velocity, heat = adjoint_velocity[:, :, 0], adjoint_heat[:, 0]
     forces, flow, stress, visc = (
         forcing[:, :, 0], flow_velocity[:, :, 0], forward_stress[:, :, 0], viscosity[:, 0]
     )
     flips = face_flips.T
     flow_here = pltpu.VMEM(flow.shape, jnp.float32)
-    *state, facts = call(
+    lower, upper, row_low, row_high, col_low, col_high, facts = call(
         pack_kernel,
-        packed + [rim_shape],
+        [(4 * size, size)] * 2 + [(ROW_MESSAGE, size)] * 2 + [(8, size)] * 2 + [(16, size)],
         (),
-        (velocity, heat, layer_mask, flips),
+        (velocity, heat, layer_mask, flips, forces, flow, visc),
         (
             pltpu.SMEM(layer_mask.shape, jnp.int32),
             pltpu.VMEM(flips.shape, jnp.int32),
+            pltpu.VMEM((2, 3, 2, 8, size), jnp.float32),
+            pltpu.VMEM((2, 3, 2, 8, size), jnp.float32),
+            pltpu.VMEM((2, 2, 8, size), jnp.float32),
+            pltpu.SemaphoreType.DMA((10,)),
             pltpu.SemaphoreType.DMA((6,)),
         ),
     )
-    received = exchange(*state)
-    state = call(
+    halos = radial(lower, upper)
+    rows_beside = beside(row_low, row_high, quarter)
+    columns_beside = beside(col_low, col_high, 1)
+    lower, upper, col_low, col_high, kept = call(
         first_kernel,
-        packed,
-        (facts, *state[:2], *received, forces, visc),
+        [(4 * size + 16, size)] * 2 + [(16, size)] * 2 + [(2 * KEPT, size)],
+        (facts, lower, upper, *halos, *rows_beside, *columns_beside, forces, visc),
         (flow,),
         (flow_here, pltpu.SemaphoreType.DMA),
     )
-    received = exchange(*state)
-    near = (facts, *state[:2], *received)
-    velocity_near, partial = call(
-        last_velocity_kernel, [velocity.shape, (size, size)], (*near, forces, visc, stress)
+    near = (facts, lower, upper, *radial(lower, upper), *beside(col_low, col_high, 1))
+    velocity_near, partial, edge_rows = call(
+        last_velocity_kernel,
+        [velocity.shape, (size, size), (16, size)],
+        (*near, kept, row_low, row_high, forces, visc, stress),
     )
     pieces = lax.all_to_all(partial, "rad", 0, 0, tiled=True)
     new_velocity, new_heat = call(
         last_heat_kernel,
         [velocity.shape, heat.shape],
-        (*near, velocity_near),
+        (*near, edge_rows, velocity_near),
         (flow,),
         (flow_here, pltpu.VMEM(heat.shape, jnp.float32), pltpu.SemaphoreType.DMA((3,))),
         [FAR, FAR],

time: 85.2 us -> 80.7 us (0.947)
  starting transfers between devices: 68.5 us -> 56.1 us
  waiting for transfers between devices: 8.14 us -> 15.4 us
    ppermute x8 -> x6, starting transfers between devices: 35.6 us -> 21.7 us  [around(): lax.ppermute(array, 'cap', [(i, (i + by) % count) for i in range(count)])]
    ppermute x8 -> x6, waiting for transfers between devices: 2.59 us -> 9.87 us  [around(): lax.ppermute(array, 'cap', [(i, (i + by) % count) for i in range(count)])]
    all_to_all x1, starting transfers between devices: 9.14 us -> 10.7 us  [shards(): pieces = lax.all_to_all(partial, 'rad', 0, 0, tiled=True)]
  transfers between devices with their start and end apart: 13 -> 11, of which waited for: 3 -> 4; matrix products, arithmetic and copies ran while one was open for 0% -> 0% of each run, Pallas kernels for 2% -> 3%
where the time goes in v3:
time: 80.7 us; the launch traced here: 80.2 us
  starting transfers between devices  56.1 us (70%)
  waiting for transfers between devices  15.4 us (19%)
  Pallas kernels  7.29 us (9%)
    ppermute x4, starting transfers between devices, along(): lax.ppermute(array, 'rad', [(i, i + by) for i in range(count) if 0 <= i +...  23.8 us
    ppermute x6, starting transfers between devices, around(): lax.ppermute(array, 'cap', [(i, (i + by) % count) for i in range(count)])  21.7 us
    all_to_all x1, starting transfers between devices, shards(): pieces = lax.all_to_all(partial, 'rad', 0, 0, tiled=True)  10.7 us
    ppermute x6, waiting for transfers between devices, around(): lax.ppermute(array, 'cap', [(i, (i + by) % count) for i in range(count)])  9.87 us
    pallas_call x4, Pallas kernels, call(): pl.pallas_call(kernel, out_shape=[jax.ShapeDtypeStruct(shape, jnp.float32...  7.29 us
    all_to_all x1, waiting for transfers between devices, shards(): pieces = lax.all_to_all(partial, 'rad', 0, 0, tiled=True)  5.54 us
  transfers between devices with their start and end apart: 11, of which 4 were waited for; matrix products, arithmetic and copies ran while one was open for 0% of the time, Pallas kernels for 3%

profile of v3, /device:TPU:2, one launch (start us, length us, event | category | flops | bytes accessed | tf_op | source)
XLA Modules:
  0.0 80.2 jit_solution(11218063101563510247)
XLA Ops:
  0.6 0.0 copy-start
  0.6 0.0 copy-start.1
  0.7 1.7 %shard_map.103 = (f32[512,128]{1,0:T(8,128)S(1)}, f32[512,128]{1,0:T(8,128)S(1)}, f32[48,128]{1,0:T(8,128)S(1)}, f32[48,128]{1,0:T(8,128)S(1)}, f32[8,128]{1,0:T...) custom-call(f32[3,2,128,128]{3,2,1,0:T(8,128)} %bitcast.28, f32[2,128,128]{2,1,0:T(8,128)} %bitcast.30, s32[2]{0:T(128)} %mask.1, ...), custom_call_target="tpu_custom_call" | custom-call | bytes 1442824 | tf_op jit(solution)/shard_map/pallas_call | solution.py:340
  2.4 15.1 %collective-permute-start.1 = (f32[512,128]{1,0:T(8,128)S(1)}, f32[512,128]{1,0:T(8,128)S(1)}, u32[]{:S(2)}, u32[]{:S(2)}) collective-permute-start(f32[512,128]{1,0:T(8,128)S(1)} %get-tuple-element.23.lower), channel_id=1, source_target_pairs={{1,0},{2,1},{3,2},{4,3},{5,4},{6,5},{7,6},{8,7},{9,8},{10,9},{11,1... | collective-permute-start | bytes 786440 | tf_op jit(solution)/shard_map/ppermute | solution.py:360
  17.5 1.9 %collective-permute-start = (f32[512,128]{1,0:T(8,128)S(1)}, f32[512,128]{1,0:T(8,128)S(1)}, u32[]{:S(2)}, u32[]{:S(2)}) collective-permute-start(f32[512,128]{1,0:T(8,128)S(1)} %get-tuple-element.24.upper), channel_id=1, source_target_pairs={{0,1},{1,2},{2,3},{3,4},{4,5},{5,6},{6,7},{7,8},{8,9},{9,10},{10,1... | collective-permute-start | bytes 786440 | tf_op jit(solution)/shard_map/ppermute | solution.py:360
  19.4 1.9 %collective-permute-start.2 = (f32[48,128]{1,0:T(8,128)S(1)}, f32[48,128]{1,0:T(8,128)S(1)}, u32[]{:S(2)}, u32[]{:S(2)}) collective-permute-start(f32[48,128]{1,0:T(8,128)S(1)} %get-tuple-element.25.row_high), channel_id=1, source_target_pairs={{0,256},{16,272},{32,288},{48,304},{64,320},{80,336},{96,352},{112... | collective-permute-start | bytes 73736 | tf_op jit(solution)/shard_map/ppermute | solution.py:355
  21.4 6.1 %collective-permute-start.3 = (f32[48,128]{1,0:T(8,128)S(1)}, f32[48,128]{1,0:T(8,128)S(1)}, u32[]{:S(2)}, u32[]{:S(2)}) collective-permute-start(f32[48,128]{1,0:T(8,128)S(1)} %get-tuple-element.26.row_low), channel_id=1, source_target_pairs={{0,768},{16,784},{32,800},{48,816},{64,832},{80,848},{96,864},{112... | collective-permute-start | bytes 73736 | tf_op jit(solution)/shard_map/ppermute | solution.py:355
  27.5 1.9 %collective-permute-start.4 = (f32[8,128]{1,0:T(8,128)S(1)}, f32[8,128]{1,0:T(8,128)S(1)}, u32[]{:S(2)}, u32[]{:S(2)}) collective-permute-start(f32[8,128]{1,0:T(8,128)S(1)} %get-tuple-element.27), channel_id=1, source_target_pairs={{0,16},{16,32},{32,48},{48,64},{64,80},{80,96},{96,112},{112,128},... | collective-permute-start | bytes 12296 | tf_op jit(solution)/shard_map/ppermute | solution.py:355
  29.4 7.2 %collective-permute-done.4.lc = f32[8,128]{1,0:T(8,128)S(1)} collective-permute-done((f32[8,128]{1,0:T(8,128)S(1)}, f32[8,128]{1,0:T(8,128)S(1)}, u32[]{:S(2)}, u32[]{:S(2)}) %collective-permute-start.4) | collective-permute-done | bytes 4128 | tf_op jit(solution)/shard_map/ppermute | solution.py:355
  36.7 1.9 %collective-permute-start.5 = (f32[8,128]{1,0:T(8,128)S(1)}, f32[8,128]{1,0:T(8,128)S(1)}, u32[]{:S(2)}, u32[]{:S(2)}) collective-permute-start(f32[8,128]{1,0:T(8,128)S(1)} %get-tuple-element.28), channel_id=1, source_target_pairs={{0,1008},{16,0},{32,16},{48,32},{64,48},{80,64},{96,80},{112,96},{... | collective-permute-start | bytes 12296 | tf_op jit(solution)/shard_map/ppermute | solution.py:355
  38.6 1.3 %collective-permute-done.5.hc = f32[8,128]{1,0:T(8,128)S(1)} collective-permute-done((f32[8,128]{1,0:T(8,128)S(1)}, f32[8,128]{1,0:T(8,128)S(1)}, u32[]{:S(2)}, u32[]{:S(2)}) %collective-permute-start.5) | collective-permute-done | bytes 4128 | tf_op jit(solution)/shard_map/ppermute | solution.py:355
  39.9 0.0 collective-permute-done.2.lr
  39.9 0.0 collective-permute-done.3.hr
  39.9 0.0 collective-permute-done.1.above_halo
  39.9 0.0 collective-permute-done.below_halo
  39.9 0.0 copy-done
  39.9 0.0 copy-done.1
  39.9 0.0 copy-start.2
  39.9 2.1 %shard_map.104 = (f32[528,128]{1,0:T(8,128)S(1)}, f32[528,128]{1,0:T(8,128)S(1)}, f32[16,128]{1,0:T(8,128)S(1)}, f32[16,128]{1,0:T(8,128)S(1)}, f32[80,128]{1,0:T(8,128)S(1)}) custom-call(f32[16,128]{1,0:T(8,128)S(1)} %get-tuple-element.22.facts, f32[512,128]{1,0:T(8,128)S(1)} %get-tuple-element.23.lower, f32[512,128]{1,0:T(8,128)S(1)} %get-tuple-element.24.upper, ...), custom_call_target="tpu_custom_call" | custom-call | bytes 2031616 | tf_op jit(solution)/shard_map/pallas_call | solution.py:340
  42.0 3.8 %collective-permute-start.7 = (f32[528,128]{1,0:T(8,128)S(1)}, f32[528,128]{1,0:T(8,128)S(1)}, u32[]{:S(2)}, u32[]{:S(2)}) collective-permute-start(f32[528,128]{1,0:T(8,128)S(1)} %get-tuple-element.29.lower), channel_id=1, source_target_pairs={{1,0},{2,1},{3,2},{4,3},{5,4},{6,5},{7,6},{8,7},{9,8},{10,9},{11,1... | collective-permute-start | bytes 811016 | tf_op jit(solution)/shard_map/ppermute | solution.py:360
  45.9 2.9 %collective-permute-start.6 = (f32[528,128]{1,0:T(8,128)S(1)}, f32[528,128]{1,0:T(8,128)S(1)}, u32[]{:S(2)}, u32[]{:S(2)}) collective-permute-start(f32[528,128]{1,0:T(8,128)S(1)} %get-tuple-element.30.upper), channel_id=1, source_target_pairs={{0,1},{1,2},{2,3},{3,4},{4,5},{5,6},{6,7},{7,8},{8,9},{9,10},{10,1... | collective-permute-start | bytes 811016 | tf_op jit(solution)/shard_map/ppermute | solution.py:360
  48.8 1.9 %collective-permute-start.8 = (f32[16,128]{1,0:T(8,128)S(1)}, f32[16,128]{1,0:T(8,128)S(1)}, u32[]{:S(2)}, u32[]{:S(2)}) collective-permute-start(f32[16,128]{1,0:T(8,128)S(1)} %get-tuple-element.31), channel_id=1, source_target_pairs={{0,16},{16,32},{32,48},{48,64},{64,80},{80,96},{96,112},{112,128},... | collective-permute-start | bytes 24584 | tf_op jit(solution)/shard_map/ppermute | solution.py:355
  50.7 7.9 %collective-permute-start.9 = (f32[16,128]{1,0:T(8,128)S(1)}, f32[16,128]{1,0:T(8,128)S(1)}, u32[]{:S(2)}, u32[]{:S(2)}) collective-permute-start(f32[16,128]{1,0:T(8,128)S(1)} %get-tuple-element.32), channel_id=1, source_target_pairs={{0,1008},{16,0},{32,16},{48,32},{64,48},{80,64},{96,80},{112,96},{... | collective-permute-start | bytes 24584 | tf_op jit(solution)/shard_map/ppermute | solution.py:355
  58.6 0.0 collective-permute-done.8.lc
  58.6 1.3 %collective-permute-done.9.hc = f32[16,128]{1,0:T(8,128)S(1)} collective-permute-done((f32[16,128]{1,0:T(8,128)S(1)}, f32[16,128]{1,0:T(8,128)S(1)}, u32[]{:S(2)}, u32[]{:S(2)}) %collective-permute-start.9) | collective-permute-done | bytes 8224 | tf_op jit(solution)/shard_map/ppermute | solution.py:355
  59.9 0.0 collective-permute-done.7.above_halo
  60.0 0.0 collective-permute-done.6.below_halo
  60.0 0.0 copy-done.2
  60.0 1.4 %shard_map.105 = (f32[3,2,128,128]{3,2,1,0:T(8,128)S(1)}, f32[128,128]{1,0:T(8,128)}, f32[16,128]{1,0:T(8,128)S(1)}) custom-call(f32[16,128]{1,0:T(8,128)S(1)} %get-tuple-element.22.facts, f32[528,128]{1,0:T(8,128)S(1)} %get-tuple-element.29.lower, f32[528,128]{1,0:T(8,128)S(1)} %get-tuple-element.30.upper, ...), custom_call_target="tpu_custom_call" | custom-call | bytes 2113536 | tf_op jit(solution)/shard_map/pallas_call | solution.py:340
  61.3 10.7 %all-to-all-start = ((f32[16,8,128]{2,1,0:T(8,128)}), f32[16,8,128]{2,1,0:T(8,128)S(1)}, u32[]{:S(2)}, u32[]{:S(2)}) async-start(f32[16,8,128]{2,1,0:T(8,128)} %bitcast.9), calls=%async_computation | async-start | bytes 131072 | tf_op jit(solution)/shard_map/all_to_all | solution.py:416
  72.0 2.1 %shard_map.106 = (f32[3,2,128,128]{3,2,1,0:T(8,128)}, f32[2,128,128]{2,1,0:T(8,128)}) custom-call(f32[16,128]{1,0:T(8,128)S(1)} %get-tuple-element.22.facts, f32[528,128]{1,0:T(8,128)S(1)} %get-tuple-element.29.lower, f32[528,128]{1,0:T(8,128)S(1)} %get-tuple-element.30.upper, f32[528,128]{1,0:T(8,128)S(1)} %collective-permute-done.6.below_halo, ...), custom_call_target="tpu_custom_call" | custom-call | bytes 1900544 | tf_op jit(solution)/shard_map/pallas_call | solution.py:340
  74.1 5.5 %all-to-all-done = f32[16,8,128]{2,1,0:T(8,128)S(1)} async-done(((f32[16,8,128]{2,1,0:T(8,128)}), f32[16,8,128]{2,1,0:T(8,128)S(1)}, u32[]{:S(2)}, u32[]{:S(2)}) %all-to-all-start) | async-done | bytes 65568 | tf_op jit(solution)/shard_map/all_to_all | solution.py:416
  79.6 0.6 bitcast_reduce_fusion
Async XLA Ops:
  0.6 39.3 %copy-start = (f32[3,2,1,128,128]{4,3,2,1,0:T(8,128)S(1)}, f32[3,2,1,128,128]{4,3,2,1,0:T(8,128)}, u32[]{:S(2)}) copy-start(f32[3,2,1,128,128]{4,3,2,1,0:T(8,128)} %param.10) | copy-start | bytes 1179652
  0.6 39.3 %copy-start.1 = (f32[2,1,128,128]{3,2,1,0:T(8,128)S(1)}, f32[2,1,128,128]{3,2,1,0:T(8,128)}, u32[]{:S(2)}) copy-start(f32[2,1,128,128]{3,2,1,0:T(8,128)} %param.13) | copy-start | bytes 393220
  2.4 37.5 %collective-permute-start.1 = (f32[512,128]{1,0:T(8,128)S(1)}, f32[512,128]{1,0:T(8,128)S(1)}, u32[]{:S(2)}, u32[]{:S(2)}) collective-permute-start(f32[512,128]{1,0:T(8,128)S(1)} %get-tuple-element.23.lower), channel_id=1, source_target_pairs={{1,0},{2,1},{3,2},{4,3},{5,4},{6,5},{7,6},{8,7},{9,8},{10,9},{11,1... | collective-permute-start | bytes 786440 | tf_op jit(solution)/shard_map/ppermute | solution.py:360
  17.5 22.4 %collective-permute-start = (f32[512,128]{1,0:T(8,128)S(1)}, f32[512,128]{1,0:T(8,128)S(1)}, u32[]{:S(2)}, u32[]{:S(2)}) collective-permute-start(f32[512,128]{1,0:T(8,128)S(1)} %get-tuple-element.24.upper), channel_id=1, source_target_pairs={{0,1},{1,2},{2,3},{3,4},{4,5},{5,6},{6,7},{7,8},{8,9},{9,10},{10,1... | collective-permute-start | bytes 786440 | tf_op jit(solution)/shard_map/ppermute | solution.py:360
  19.4 20.4 %collective-permute-start.2 = (f32[48,128]{1,0:T(8,128)S(1)}, f32[48,128]{1,0:T(8,128)S(1)}, u32[]{:S(2)}, u32[]{:S(2)}) collective-permute-start(f32[48,128]{1,0:T(8,128)S(1)} %get-tuple-element.25.row_high), channel_id=1, source_target_pairs={{0,256},{16,272},{32,288},{48,304},{64,320},{80,336},{96,352},{112... | collective-permute-start | bytes 73736 | tf_op jit(solution)/shard_map/ppermute | solution.py:355
  21.4 18.5 %collective-permute-start.3 = (f32[48,128]{1,0:T(8,128)S(1)}, f32[48,128]{1,0:T(8,128)S(1)}, u32[]{:S(2)}, u32[]{:S(2)}) collective-permute-start(f32[48,128]{1,0:T(8,128)S(1)} %get-tuple-element.26.row_low), channel_id=1, source_target_pairs={{0,768},{16,784},{32,800},{48,816},{64,832},{80,848},{96,864},{112... | collective-permute-start | bytes 73736 | tf_op jit(solution)/shard_map/ppermute | solution.py:355
  27.5 9.1 %collective-permute-start.4 = (f32[8,128]{1,0:T(8,128)S(1)}, f32[8,128]{1,0:T(8,128)S(1)}, u32[]{:S(2)}, u32[]{:S(2)}) collective-permute-start(f32[8,128]{1,0:T(8,128)S(1)} %get-tuple-element.27), channel_id=1, source_target_pairs={{0,16},{16,32},{32,48},{48,64},{64,80},{80,96},{96,112},{112,128},... | collective-permute-start | bytes 12296 | tf_op jit(solution)/shard_map/ppermute | solution.py:355
  36.7 3.2 %collective-permute-start.5 = (f32[8,128]{1,0:T(8,128)S(1)}, f32[8,128]{1,0:T(8,128)S(1)}, u32[]{:S(2)}, u32[]{:S(2)}) collective-permute-start(f32[8,128]{1,0:T(8,128)S(1)} %get-tuple-element.28), channel_id=1, source_target_pairs={{0,1008},{16,0},{32,16},{48,32},{64,48},{80,64},{96,80},{112,96},{... | collective-permute-start | bytes 12296 | tf_op jit(solution)/shard_map/ppermute | solution.py:355
  39.9 20.0 %copy-start.2 = (f32[3,2,1,128,128]{4,3,2,1,0:T(8,128)S(1)}, f32[3,2,1,128,128]{4,3,2,1,0:T(8,128)}, u32[]{:S(2)}) copy-start(f32[3,2,1,128,128]{4,3,2,1,0:T(8,128)} %param.12) | copy-start | bytes 1179652
  42.0 17.9 %collective-permute-start.7 = (f32[528,128]{1,0:T(8,128)S(1)}, f32[528,128]{1,0:T(8,128)S(1)}, u32[]{:S(2)}, u32[]{:S(2)}) collective-permute-start(f32[528,128]{1,0:T(8,128)S(1)} %get-tuple-element.29.lower), channel_id=1, source_target_pairs={{1,0},{2,1},{3,2},{4,3},{5,4},{6,5},{7,6},{8,7},{9,8},{10,9},{11,1... | collective-permute-start | bytes 811016 | tf_op jit(solution)/shard_map/ppermute | solution.py:360
  45.9 14.1 %collective-permute-start.6 = (f32[528,128]{1,0:T(8,128)S(1)}, f32[528,128]{1,0:T(8,128)S(1)}, u32[]{:S(2)}, u32[]{:S(2)}) collective-permute-start(f32[528,128]{1,0:T(8,128)S(1)} %get-tuple-element.30.upper), channel_id=1, source_target_pairs={{0,1},{1,2},{2,3},{3,4},{4,5},{5,6},{6,7},{7,8},{8,9},{9,10},{10,1... | collective-permute-start | bytes 811016 | tf_op jit(solution)/shard_map/ppermute | solution.py:360
  48.8 9.8 %collective-permute-start.8 = (f32[16,128]{1,0:T(8,128)S(1)}, f32[16,128]{1,0:T(8,128)S(1)}, u32[]{:S(2)}, u32[]{:S(2)}) collective-permute-start(f32[16,128]{1,0:T(8,128)S(1)} %get-tuple-element.31), channel_id=1, source_target_pairs={{0,16},{16,32},{32,48},{48,64},{64,80},{80,96},{96,112},{112,128},... | collective-permute-start | bytes 24584 | tf_op jit(solution)/shard_map/ppermute | solution.py:355
  50.7 9.2 %collective-permute-start.9 = (f32[16,128]{1,0:T(8,128)S(1)}, f32[16,128]{1,0:T(8,128)S(1)}, u32[]{:S(2)}, u32[]{:S(2)}) collective-permute-start(f32[16,128]{1,0:T(8,128)S(1)} %get-tuple-element.32), channel_id=1, source_target_pairs={{0,1008},{16,0},{32,16},{48,32},{64,48},{80,64},{96,80},{112,96},{... | collective-permute-start | bytes 24584 | tf_op jit(solution)/shard_map/ppermute | solution.py:355
  61.3 18.3 %all-to-all-start = ((f32[16,8,128]{2,1,0:T(8,128)}), f32[16,8,128]{2,1,0:T(8,128)S(1)}, u32[]{:S(2)}, u32[]{:S(2)}) async-start(f32[16,8,128]{2,1,0:T(8,128)} %bitcast.9), calls=%async_computation | async-start | bytes 131072 | tf_op jit(solution)/shard_map/all_to_all | solution.py:416

commit v4 on v3

--- a/solution.py
+++ b/solution.py
@@ -43,12 +43,26 @@
 KEPT = 40
 
 
+def core_index():
+    return lax.rem(lax.axis_index("cap"), 2)
+
+
+def in_order(from_partner, from_outside):
+    second = core_index() == 1
+    return (
+        jnp.where(second, from_partner, from_outside),
+        jnp.where(second, from_outside, from_partner),
+    )
+
+
 def pack_kernel(
     velocity, heat, mask, flips, forcing, flow, viscosity,
-    lower, upper, row_low, row_high, col_low, col_high, facts,
-    mask_here, flips_here, forcing_rims, flow_rims, viscosity_rims, sems, rim_sem,
+    lower, upper, row_own, gift, col_own, facts,
+    mask_here, flips_here, forcing_rims, flow_rims, viscosity_rims, messages, cols, sems, rim_sem,
 ):
     size = lower.shape[1]
+    row_low, row_high = messages.at[0], messages.at[1]
+    core = core_index()
     copies = [
         pltpu.make_async_copy(mask, mask_here, sems.at[0]),
         pltpu.make_async_copy(flips, flips_here, sems.at[1]),
@@ -126,8 +140,12 @@
     row_low[CORNERS, :] = corners
     row_high[CORNERS, :] = corners
     columns = edge_columns(planes)
-    col_low[...] = columns[:8]
-    col_high[...] = columns[8:]
+    cols[0] = columns[:8]
+    cols[1] = columns[8:]
+    row_own[...] = messages[1 - core]
+    gift[:ROW_MESSAGE, :] = messages[core]
+    gift[ROW_MESSAGE:, :] = cols[1 - core]
+    col_own[...] = cols[core]
 
 
 def turned(rim, flip):
@@ -137,7 +155,7 @@
 
 
 def columns_of(facts, low, high):
-    return turned(low[:8, :], facts[2:3, :]).T, turned(high[:8, :], facts[3:4, :]).T
+    return turned(low[:8], facts[2:3, :]).T, turned(high[:8], facts[3:4, :]).T
 
 
 def lateral(plane, k, rims):
@@ -216,17 +234,17 @@
     return jnp.where(field == 3, heat, velocity)
 
 
-def halo_rows(facts, kept, row_low, row_high, below_halo, above_halo, low_col, high_col):
+def halo_rows(facts, kept, below_halo, above_halo, low_col, high_col):
     size = facts.shape[1]
     below, above = below_halo[4 * size :, :], above_halo[4 * size :, :]
-    at_low, at_high = low_col[8:16, :], high_col[8:16, :]
+    at_low, at_high = low_col[8:16], high_col[8:16]
 
     def chosen(flag, corners, one, zero):
         flag = jnp.broadcast_to(facts[flag : flag + 1, 0:1], (8, 1))
         return jnp.where(flag > 0.5, corners[:, one : one + 1], corners[:, zero : zero + 1])
 
     made = []
-    for side, own in enumerate((row_low, row_high)):
+    for side in range(2):
         flip = facts[side : side + 1, :]
         if side == 0:
             before = chosen(8 + 2, at_low, 1, 3)
@@ -238,7 +256,7 @@
         made.append(
             halo_row(
                 kept[KEPT * side : KEPT * (side + 1), :],
-                own[EDGE, :],
+                kept[2 * KEPT + 8 * side : 2 * KEPT + 8 * side + 8, :],
                 below[8 * side : 8 * side + 8],
                 above[8 * side : 8 * side + 8],
                 jnp.where(swap, after, before),
@@ -251,18 +269,26 @@
 
 
 def first_kernel(
-    facts, lower, upper, below_halo, above_halo, lr, hr, lc, hc, forcing, viscosity, flow_far,
-    new_lower, new_upper, col_low, col_high, kept, flow, sem,
+    facts, lower, upper, below_halo, above_halo, gifts, got, passed, outer, forcing, viscosity,
+    flow_far, new_lower, new_upper, col_given, col_own, kept, cols, flow, sem,
 ):
     copy = pltpu.make_async_copy(flow_far, flow, sem)
     copy.start()
     size = facts.shape[1]
-    for side, message in enumerate((lr, hr)):
+    core = core_index()
+    high, low = in_order(passed[1 - core], got[ROW_MESSAGE:, :])
+    messages = (low, high)
+    for side, message in enumerate(messages):
         kept[KEPT * side : KEPT * (side + 1), :] = turned(
-            message[:KEPT, :], facts[side : side + 1, :]
+            message[:KEPT], facts[side : side + 1, :]
         )
+        edge = (size - 1) * side
+        for layer, state in enumerate((lower, upper)):
+            for k in range(4):
+                at = 2 * KEPT + 8 * side + 4 * layer + k
+                kept[at : at + 1, :] = state[k * size + edge : k * size + edge + 1, :]
     edges = [kept[KEPT * side : KEPT * side + 8, :] for side in range(2)]
-    rims = (*edges, *columns_of(facts, lc, hc))
+    rims = (*edges, *columns_of(facts, *in_order(gifts[1 - core, ROW_MESSAGE:], outer[...])))
     state = planes_of(lower, upper)
     outs = (new_lower, new_upper)
     for layer, out in enumerate(outs):
@@ -278,27 +304,39 @@
     for layer, out in enumerate(outs):
         out[3 * size : 4 * size, :] = warmed(layer, state, below_halo, above_halo, flow, rims)
     columns = edge_columns([plane_of(ref, k) for ref in outs for k in range(4)])
-    corners = lr[CORNERS, :]
-    corners = jnp.where(lanes(corners.shape) < 4, corners, shifted(hr[CORNERS, :], 4, 1))
-    for n, out in enumerate((col_low, col_high)):
-        out[0:8, :] = columns[8 * n : 8 * n + 8]
-        out[8:16, :] = corners
-
-
-def last_velocity_kernel(
-    facts, lower, upper, below_halo, above_halo, lc, hc, kept, row_low, row_high, forcing,
-    viscosity, stress, new_velocity, partial, edge_rows,
+    cols[0] = columns[:8]
+    cols[1] = columns[8:]
+    corners = [message[CORNERS] for message in messages]
+    corners = jnp.where(lanes(corners[0].shape) < 4, corners[0], shifted(corners[1], 4, 1))
+    col_given[:8, :] = cols[1 - core]
+    col_own[:8, :] = cols[core]
+    col_given[8:, :] = corners
+    col_own[8:, :] = corners
+
+
+def last_kernel(
+    facts, lower, upper, below_halo, above_halo, gifts, outer, kept, forcing, viscosity, stress,
+    flow, new_velocity, new_heat, partial, velocity, heat, sems,
 ):
-    edges = halo_rows(facts, kept, row_low, row_high, below_halo, above_halo, lc, hc)
-    for side in range(2):
-        edge_rows[8 * side : 8 * side + 8, :] = edges[side]
-    rims = (*edges, *columns_of(facts, lc, hc))
+    sides = in_order(gifts[1 - core_index()], outer[...])
+    edges = halo_rows(facts, kept, below_halo, above_halo, *sides)
+    rims = (*edges, *columns_of(facts, *sides))
     state = planes_of(lower, upper)
+    copies = []
+
+    def send(source, target):
+        copies.append(pltpu.make_async_copy(source, target, sems.at[len(copies)]))
+        copies[-1].start()
+
+    for layer in range(2):
+        heat[layer] = warmed(layer, state, below_halo, above_halo, flow, rims)
+        send(heat.at[layer], new_heat.at[layer])
     for layer in range(2):
         stiffness = stiffness_of(viscosity, facts, layer)
         new = moved(layer, state, below_halo, above_halo, forcing, stiffness, rims)
         for k in range(3):
-            new_velocity[k, layer] = new[k]
+            velocity[k, layer] = new[k]
+            send(velocity.at[k, layer], new_velocity.at[k, layer])
         share = stiffness * (
             new[0] * stress[0, layer] + new[1] * stress[1, layer] + new[2] * stress[2, layer]
         )
@@ -306,27 +344,8 @@
             partial[...] = share
         else:
             partial[...] = (partial[...] + share) * (1.0 / 96.0)
-
-
-def last_heat_kernel(
-    facts, lower, upper, below_halo, above_halo, lc, hc, edge_rows, velocity_near, flow_far,
-    new_velocity, new_heat, flow, heat, sems,
-):
-    copies = [
-        pltpu.make_async_copy(flow_far, flow, sems.at[0]),
-        pltpu.make_async_copy(velocity_near, new_velocity, sems.at[1]),
-    ]
     for copy in copies:
-        copy.start()
-    rims = (edge_rows[0:8, :], edge_rows[8:16, :], *columns_of(facts, lc, hc))
-    state = planes_of(lower, upper)
-    copies[0].wait()
-    for layer in range(2):
-        heat[layer] = warmed(layer, state, below_halo, above_halo, flow, rims)
-    out = pltpu.make_async_copy(heat, new_heat, sems.at[2])
-    out.start()
-    copies[1].wait()
-    out.wait()
+        copy.wait()
 
 
 VMEM = pl.BlockSpec(memory_space=pltpu.VMEM)
@@ -350,9 +369,19 @@
     )(*arrays)
 
 
-def around(array, by):
+def over_tiles(array, to):
     count = lax.axis_size("cap")
-    return lax.ppermute(array, "cap", [(i, (i + by) % count) for i in range(count)])
+    return lax.ppermute(array, "cap", [(i, to(i) % count) for i in range(count)])
+
+
+def of_chip(array):
+    count = lax.axis_size("cap")
+    pairs = [[i, i + 1] for i in range(0, count, 2)]
+    return lax.all_gather(array, "cap", axis_index_groups=pairs)
+
+
+def to_outer(array):
+    return over_tiles(array, lambda i: i + 1 if i % 2 else i - 1)
 
 
 def along(array, by):
@@ -364,10 +393,6 @@
 
 def radial(lower, upper):
     return along(upper, 1), along(lower, -1)
-
-
-def beside(low, high, step):
-    return around(high, step), around(low, -step)
 
 
 def shards(
@@ -381,48 +406,62 @@
         forcing[:, :, 0], flow_velocity[:, :, 0], forward_stress[:, :, 0], viscosity[:, 0]
     )
     flips = face_flips.T
-    flow_here = pltpu.VMEM(flow.shape, jnp.float32)
-    lower, upper, row_low, row_high, col_low, col_high, facts = call(
+    f32 = jnp.float32
+    lower, upper, row_own, gift, col_own, facts = call(
         pack_kernel,
-        [(4 * size, size)] * 2 + [(ROW_MESSAGE, size)] * 2 + [(8, size)] * 2 + [(16, size)],
+        [(4 * size, size)] * 2
+        + [(ROW_MESSAGE, size), (ROW_MESSAGE + 8, size), (8, size), (16, size)],
         (),
         (velocity, heat, layer_mask, flips, forces, flow, visc),
         (
             pltpu.SMEM(layer_mask.shape, jnp.int32),
             pltpu.VMEM(flips.shape, jnp.int32),
-            pltpu.VMEM((2, 3, 2, 8, size), jnp.float32),
-            pltpu.VMEM((2, 3, 2, 8, size), jnp.float32),
-            pltpu.VMEM((2, 2, 8, size), jnp.float32),
+            pltpu.VMEM((2, 3, 2, 8, size), f32),
+            pltpu.VMEM((2, 3, 2, 8, size), f32),
+            pltpu.VMEM((2, 2, 8, size), f32),
+            pltpu.VMEM((2, ROW_MESSAGE, size), f32),
+            pltpu.VMEM((2, 8, size), f32),
             pltpu.SemaphoreType.DMA((10,)),
             pltpu.SemaphoreType.DMA((6,)),
         ),
     )
     halos = radial(lower, upper)
-    rows_beside = beside(row_low, row_high, quarter)
-    columns_beside = beside(col_low, col_high, 1)
-    lower, upper, col_low, col_high, kept = call(
+    gifts = of_chip(gift)
+    core = lax.rem(lax.axis_index("cap"), 2)
+    given = lax.dynamic_index_in_dim(gifts, 1 - core, 0, keepdims=False)[:ROW_MESSAGE]
+    got = over_tiles(
+        jnp.concatenate([row_own, given]),
+        lambda i: i - quarter - 1 if i % 2 else i + quarter + 1,
+    )
+    outer = to_outer(col_own)
+    passed = of_chip(got[:ROW_MESSAGE])
+    lower, upper, col_given, col_own, kept = call(
         first_kernel,
-        [(4 * size + 16, size)] * 2 + [(16, size)] * 2 + [(2 * KEPT, size)],
-        (facts, lower, upper, *halos, *rows_beside, *columns_beside, forces, visc),
+        [(4 * size + 16, size)] * 2 + [(16, size)] * 2 + [(2 * KEPT + 16, size)],
+        (facts, lower, upper, *halos, gifts, got, passed, outer, forces, visc),
         (flow,),
-        (flow_here, pltpu.SemaphoreType.DMA),
-    )
-    near = (facts, lower, upper, *radial(lower, upper), *beside(col_low, col_high, 1))
-    velocity_near, partial, edge_rows = call(
-        last_velocity_kernel,
-        [velocity.shape, (size, size), (16, size)],
-        (*near, kept, row_low, row_high, forces, visc, stress),
+        (
+            pltpu.VMEM((2, 8, size), f32),
+            pltpu.VMEM(flow.shape, f32),
+            pltpu.SemaphoreType.DMA,
+        ),
+    )
+    halos = radial(lower, upper)
+    gifts = of_chip(col_given)
+    outer = to_outer(col_own)
+    new_velocity, new_heat, partial = call(
+        last_kernel,
+        [velocity.shape, heat.shape, (size, size)],
+        (facts, lower, upper, *halos, gifts, outer, kept, forces, visc, stress, flow),
+        (),
+        (
+            pltpu.VMEM(velocity.shape, f32),
+            pltpu.VMEM(heat.shape, f32),
+            pltpu.SemaphoreType.DMA((8,)),
+        ),
+        [FAR, FAR, VMEM],
     )
     pieces = lax.all_to_all(partial, "rad", 0, 0, tiled=True)
-    new_velocity, new_heat = call(
-        last_heat_kernel,
-        [velocity.shape, heat.shape],
-        (*near, edge_rows, velocity_near),
-        (flow,),
-        (flow_here, pltpu.VMEM(heat.shape, jnp.float32), pltpu.SemaphoreType.DMA((3,))),
-        [FAR, FAR],
-    )
-    pieces, new_heat = lax.optimization_barrier((pieces, new_heat))
     count = lax.axis_size("rad")
     gradient = jnp.sum(pieces.reshape(count, size // count, size), axis=0)
     return new_velocity[:, :, None], new_heat[:, None], gradient[None]

time: 80.7 us -> 75.6 us (0.937)
  blocking collectives: 0 us -> 26.6 us
  waiting for transfers between devices: 15.4 us -> 0.68 us
  starting transfers between devices: 56.1 us -> 41.6 us
  Pallas kernels: 7.29 us -> 4.94 us
    all_to_all x0 -> x1, blocking collectives: none -> 21.1 us  [shards(): pieces = lax.all_to_all(partial, 'rad', 0, 0, tiled=True)]
    all_to_all x1 -> x0, starting transfers between devices: 10.7 us -> none  [shards(): pieces = lax.all_to_all(partial, 'rad', 0, 0, tiled=True)]
    ppermute x6 -> x3, waiting for transfers between devices: 9.87 us -> 0.67 us  [over_tiles(): lax.ppermute(array, 'cap', [(i, to(i) % count) for i in range(count)])]
    all_to_all x1 -> x0, waiting for transfers between devices: 5.54 us -> none  [shards(): pieces = lax.all_to_all(partial, 'rad', 0, 0, tiled=True)]
    all_gather x0 -> x3, blocking collectives: none -> 5.5 us  [of_chip(): return lax.all_gather(array, 'cap', axis_index_groups=pairs)]
    ppermute x6 -> x3, starting transfers between devices: 21.7 us -> 17.7 us  [over_tiles(): lax.ppermute(array, 'cap', [(i, to(i) % count) for i in range(count)])]
    pallas_call x4 -> x3, Pallas kernels: 7.29 us -> 4.94 us  [call(): pl.pallas_call(kernel, out_shape=[jax.ShapeDtypeStruct(shape, jnp.float32...]
  transfers between devices with their start and end apart: 11 -> 7, of which waited for: 4 -> 1; matrix products, arithmetic and copies ran while one was open for 0% -> 0% of each run, Pallas kernels for 3% -> 0%
where the time goes in v4:
time: 75.6 us; the launch traced here: 75.3 us
  starting transfers between devices  41.6 us (55%)
  blocking collectives  26.6 us (35%)
  Pallas kernels  4.94 us (7%)
  between operations  0.8 us (1%)
    ppermute x4, starting transfers between devices, along(): lax.ppermute(array, 'rad', [(i, i + by) for i in range(count) if 0 <= i +...  23.9 us
    all_to_all x1, blocking collectives, shards(): pieces = lax.all_to_all(partial, 'rad', 0, 0, tiled=True)  21.1 us
    ppermute x3, starting transfers between devices, over_tiles(): lax.ppermute(array, 'cap', [(i, to(i) % count) for i in range(count)])  17.7 us
    all_gather x3, blocking collectives, of_chip(): return lax.all_gather(array, 'cap', axis_index_groups=pairs)  5.5 us
    pallas_call x3, Pallas kernels, call(): pl.pallas_call(kernel, out_shape=[jax.ShapeDtypeStruct(shape, jnp.float32...  4.94 us
  transfers between devices with their start and end apart: 7, of which 1 were waited for; matrix products, arithmetic and copies ran while one was open for 0% of the time, Pallas kernels for 0%

profile of v4, /device:TPU:2, one launch (start us, length us, event | category | flops | bytes accessed | tf_op | source)
XLA Modules:
  0.0 75.3 jit_solution(17541284761069120884)
XLA Ops:
  0.6 0.0 copy-start.2
  0.6 1.7 %shard_map.103 = (f32[512,128]{1,0:T(8,128)S(1)}, f32[512,128]{1,0:T(8,128)S(1)}, f32[48,128]{1,0:T(8,128)S(1)}, f32[56,128]{1,0:T(8,128)S(1)}, f32[8,128]{1,0:T(8,128)S(1)}, /*index=5*/f32[16,128]{1,0:T(8,128)S(1)}) custom-call(f32[3,2,128,128]{3,2,1,0:T(8,128)} %bitcast.35, f32[2,128,128]{2,1,0:T(8,128)} %bitcast.36, s32[2]{0:T(128)} %mask.1, ...), custom_call_target="tpu_custom_call" | custom-call | bytes 1442824 | tf_op jit(solution)/shard_map/pallas_call | solution.py:359
  2.4 0.0 copy-start
  2.4 15.2 %collective-permute-start.1 = (f32[512,128]{1,0:T(8,128)S(1)}, f32[512,128]{1,0:T(8,128)S(1)}, u32[]{:S(2)}, u32[]{:S(2)}) collective-permute-start(f32[512,128]{1,0:T(8,128)S(1)} %get-tuple-element.18.lower), channel_id=1, source_target_pairs={{1,0},{2,1},{3,2},{4,3},{5,4},{6,5},{7,6},{8,7},{9,8},{10,9},{11,1... | collective-permute-start | bytes 786440 | tf_op jit(solution)/shard_map/ppermute | solution.py:389
  17.6 1.9 %collective-permute-start = (f32[512,128]{1,0:T(8,128)S(1)}, f32[512,128]{1,0:T(8,128)S(1)}, u32[]{:S(2)}, u32[]{:S(2)}) collective-permute-start(f32[512,128]{1,0:T(8,128)S(1)} %get-tuple-element.19.upper), channel_id=1, source_target_pairs={{0,1},{1,2},{2,3},{3,4},{4,5},{5,6},{6,7},{7,8},{8,9},{9,10},{10,1... | collective-permute-start | bytes 786440 | tf_op jit(solution)/shard_map/ppermute | solution.py:389
  19.5 1.8 %all-gather = f32[112,128]{1,0:T(8,128)S(1)} all-gather(f32[56,128]{1,0:T(8,128)S(1)} %get-tuple-element.20), channel_id=2, replica_groups={{0,16},{32,48},{64,80},{96,112},{128,144},{160,176},{192,208},{224,240}..., dimensions={0}, use_global_device_ids=true | all-gather | bytes 86016 | tf_op jit(solution)/shard_map/all_gather | solution.py:380
  21.4 1.9 %collective-permute-start.2 = (f32[96,128]{1,0:T(8,128)S(1)}, f32[96,128]{1,0:T(8,128)S(1)}, u32[]{:S(2)}, u32[]{:S(2)}) collective-permute-start(f32[96,128]{1,0:T(8,128)S(1)} %pad_maximum_fusion), channel_id=1, source_target_pairs={{0,272},{16,768},{32,304},{48,800},{64,336},{80,832},{96,368},{112... | collective-permute-start | bytes 147464 | tf_op jit(solution)/shard_map/ppermute | solution.py:374
  23.3 9.1 %collective-permute-start.3 = (f32[8,128]{1,0:T(8,128)S(1)}, f32[8,128]{1,0:T(8,128)S(1)}, u32[]{:S(2)}, u32[]{:S(2)}) collective-permute-start(f32[8,128]{1,0:T(8,128)S(1)} %get-tuple-element.22), channel_id=1, source_target_pairs={{0,1008},{16,32},{32,16},{48,64},{64,48},{80,96},{96,80},{112,128}... | collective-permute-start | bytes 12296 | tf_op jit(solution)/shard_map/ppermute | solution.py:374
  32.4 0.0 collective-permute-done.2.got
  32.4 1.8 %all-gather.1 = f32[96,128]{1,0:T(8,128)S(1)} all-gather(f32[48,128]{1,0:T(8,128)S(1)} %slice.12), channel_id=3, replica_groups={{0,16},{32,48},{64,80},{96,112},{128,144},{160,176},{192,208},{224,240}..., dimensions={0}, use_global_device_ids=true | all-gather | bytes 73728 | tf_op jit(solution)/shard_map/all_gather | solution.py:380
  34.3 0.0 collective-permute-done.3.outer
  34.3 0.0 collective-permute-done.1.above_halo
  34.3 0.0 collective-permute-done.below_halo
  34.3 0.0 copy-done.2
  34.3 0.0 copy-done
  34.3 0.0 copy-start.1
  34.3 0.0 copy-start.3
  34.3 1.6 %shard_map.104 = (f32[528,128]{1,0:T(8,128)S(1)}, f32[528,128]{1,0:T(8,128)S(1)}, f32[16,128]{1,0:T(8,128)S(1)}, f32[16,128]{1,0:T(8,128)S(1)}, f32[96,128]{1,0:T(8,128)S(1)}) custom-call(f32[16,128]{1,0:T(8,128)S(1)} %get-tuple-element.17.facts, f32[512,128]{1,0:T(8,128)S(1)} %get-tuple-element.18.lower, f32[512,128]{1,0:T(8,128)S(1)} %get-tuple-element.19.upper, ...), custom_call_target="tpu_custom_call" | custom-call | bytes 2134016 | tf_op jit(solution)/shard_map/pallas_call | solution.py:359
  36.0 2.5 %collective-permute-start.5 = (f32[528,128]{1,0:T(8,128)S(1)}, f32[528,128]{1,0:T(8,128)S(1)}, u32[]{:S(2)}, u32[]{:S(2)}) collective-permute-start(f32[528,128]{1,0:T(8,128)S(1)} %get-tuple-element.23.lower), channel_id=1, source_target_pairs={{1,0},{2,1},{3,2},{4,3},{5,4},{6,5},{7,6},{8,7},{9,8},{10,9},{11,1... | collective-permute-start | bytes 811016 | tf_op jit(solution)/shard_map/ppermute | solution.py:389
  38.4 4.3 %collective-permute-start.4 = (f32[528,128]{1,0:T(8,128)S(1)}, f32[528,128]{1,0:T(8,128)S(1)}, u32[]{:S(2)}, u32[]{:S(2)}) collective-permute-start(f32[528,128]{1,0:T(8,128)S(1)} %get-tuple-element.24.upper), channel_id=1, source_target_pairs={{0,1},{1,2},{2,3},{3,4},{4,5},{5,6},{6,7},{7,8},{8,9},{9,10},{10,1... | collective-permute-start | bytes 811016 | tf_op jit(solution)/shard_map/ppermute | solution.py:389
  42.7 6.7 %collective-permute-start.6 = (f32[16,128]{1,0:T(8,128)S(1)}, f32[16,128]{1,0:T(8,128)S(1)}, u32[]{:S(2)}, u32[]{:S(2)}) collective-permute-start(f32[16,128]{1,0:T(8,128)S(1)} %get-tuple-element.26), channel_id=1, source_target_pairs={{0,1008},{16,32},{32,16},{48,64},{64,48},{80,96},{96,80},{112,128}... | collective-permute-start | bytes 24584 | tf_op jit(solution)/shard_map/ppermute | solution.py:374
  49.4 1.8 %all-gather.2 = f32[32,128]{1,0:T(8,128)S(1)} all-gather(f32[16,128]{1,0:T(8,128)S(1)} %get-tuple-element.25), channel_id=4, replica_groups={{0,16},{32,48},{64,80},{96,112},{128,144},{160,176},{192,208},{224,240}..., dimensions={0}, use_global_device_ids=true | all-gather | bytes 24576 | tf_op jit(solution)/shard_map/all_gather | solution.py:380
  51.2 0.7 collective-permute-done.6.outer
  51.9 0.0 collective-permute-done.5.above_halo
  51.9 0.0 collective-permute-done.4.below_halo
  51.9 0.0 copy-done.1
  51.9 0.0 copy-done.3
  51.9 1.6 %shard_map.105 = (f32[3,2,128,128]{3,2,1,0:T(8,128)}, f32[2,128,128]{2,1,0:T(8,128)}, f32[128,128]{1,0:T(8,128)S(1)}) custom-call(f32[16,128]{1,0:T(8,128)S(1)} %get-tuple-element.17.facts, f32[528,128]{1,0:T(8,128)S(1)} %get-tuple-element.23.lower, f32[528,128]{1,0:T(8,128)S(1)} %get-tuple-element.24.upper, ...), custom_call_target="tpu_custom_call" | custom-call | bytes 2473984 | tf_op jit(solution)/shard_map/pallas_call | solution.py:359
  53.5 21.1 %all_to_all.9 = f32[16,8,128]{2,1,0:T(8,128)S(1)} all-to-all(f32[16,8,128]{2,1,0:T(8,128)S(1)} %bitcast.34), channel_id=1, replica_groups=mesh['cap'=64,'rad'=16] {'rad'}, dimensions={0} | all-to-all | bytes 131072 | tf_op jit(solution)/shard_map/all_to_all | solution.py:464
  74.7 0.6 reduce_sum.9
  (3 shorter events, 0.0 us)
Async XLA Ops:
  0.6 33.7 %copy-start.2 = (f32[2,1,128,128]{3,2,1,0:T(8,128)S(1)}, f32[2,1,128,128]{3,2,1,0:T(8,128)}, u32[]{:S(2)}) copy-start(f32[2,1,128,128]{3,2,1,0:T(8,128)} %param.13) | copy-start | bytes 393220
  2.4 31.9 %copy-start = (f32[3,2,1,128,128]{4,3,2,1,0:T(8,128)S(1)}, f32[3,2,1,128,128]{4,3,2,1,0:T(8,128)}, u32[]{:S(2)}) copy-start(f32[3,2,1,128,128]{4,3,2,1,0:T(8,128)} %param.10) | copy-start | bytes 1179652
  2.4 31.9 %collective-permute-start.1 = (f32[512,128]{1,0:T(8,128)S(1)}, f32[512,128]{1,0:T(8,128)S(1)}, u32[]{:S(2)}, u32[]{:S(2)}) collective-permute-start(f32[512,128]{1,0:T(8,128)S(1)} %get-tuple-element.18.lower), channel_id=1, source_target_pairs={{1,0},{2,1},{3,2},{4,3},{5,4},{6,5},{7,6},{8,7},{9,8},{10,9},{11,1... | collective-permute-start | bytes 786440 | tf_op jit(solution)/shard_map/ppermute | solution.py:389
  17.6 16.7 %collective-permute-start = (f32[512,128]{1,0:T(8,128)S(1)}, f32[512,128]{1,0:T(8,128)S(1)}, u32[]{:S(2)}, u32[]{:S(2)}) collective-permute-start(f32[512,128]{1,0:T(8,128)S(1)} %get-tuple-element.19.upper), channel_id=1, source_target_pairs={{0,1},{1,2},{2,3},{3,4},{4,5},{5,6},{6,7},{7,8},{8,9},{9,10},{10,1... | collective-permute-start | bytes 786440 | tf_op jit(solution)/shard_map/ppermute | solution.py:389
  21.4 11.0 %collective-permute-start.2 = (f32[96,128]{1,0:T(8,128)S(1)}, f32[96,128]{1,0:T(8,128)S(1)}, u32[]{:S(2)}, u32[]{:S(2)}) collective-permute-start(f32[96,128]{1,0:T(8,128)S(1)} %pad_maximum_fusion), channel_id=1, source_target_pairs={{0,272},{16,768},{32,304},{48,800},{64,336},{80,832},{96,368},{112... | collective-permute-start | bytes 147464 | tf_op jit(solution)/shard_map/ppermute | solution.py:374
  23.3 11.0 %collective-permute-start.3 = (f32[8,128]{1,0:T(8,128)S(1)}, f32[8,128]{1,0:T(8,128)S(1)}, u32[]{:S(2)}, u32[]{:S(2)}) collective-permute-start(f32[8,128]{1,0:T(8,128)S(1)} %get-tuple-element.22), channel_id=1, source_target_pairs={{0,1008},{16,32},{32,16},{48,64},{64,48},{80,96},{96,80},{112,128}... | collective-permute-start | bytes 12296 | tf_op jit(solution)/shard_map/ppermute | solution.py:374
  34.3 17.6 %copy-start.1 = (f32[3,2,1,128,128]{4,3,2,1,0:T(8,128)S(1)}, f32[3,2,1,128,128]{4,3,2,1,0:T(8,128)}, u32[]{:S(2)}) copy-start(f32[3,2,1,128,128]{4,3,2,1,0:T(8,128)} %param.11) | copy-start | bytes 1179652
  34.3 17.6 %copy-start.3 = (f32[3,2,1,128,128]{4,3,2,1,0:T(8,128)S(1)}, f32[3,2,1,128,128]{4,3,2,1,0:T(8,128)}, u32[]{:S(2)}) copy-start(f32[3,2,1,128,128]{4,3,2,1,0:T(8,128)} %param.12) | copy-start | bytes 1179652
  36.0 15.9 %collective-permute-start.5 = (f32[528,128]{1,0:T(8,128)S(1)}, f32[528,128]{1,0:T(8,128)S(1)}, u32[]{:S(2)}, u32[]{:S(2)}) collective-permute-start(f32[528,128]{1,0:T(8,128)S(1)} %get-tuple-element.23.lower), channel_id=1, source_target_pairs={{1,0},{2,1},{3,2},{4,3},{5,4},{6,5},{7,6},{8,7},{9,8},{10,9},{11,1... | collective-permute-start | bytes 811016 | tf_op jit(solution)/shard_map/ppermute | solution.py:389
  38.4 13.5 %collective-permute-start.4 = (f32[528,128]{1,0:T(8,128)S(1)}, f32[528,128]{1,0:T(8,128)S(1)}, u32[]{:S(2)}, u32[]{:S(2)}) collective-permute-start(f32[528,128]{1,0:T(8,128)S(1)} %get-tuple-element.24.upper), channel_id=1, source_target_pairs={{0,1},{1,2},{2,3},{3,4},{4,5},{5,6},{6,7},{7,8},{8,9},{9,10},{10,1... | collective-permute-start | bytes 811016 | tf_op jit(solution)/shard_map/ppermute | solution.py:389
  42.7 9.2 %collective-permute-start.6 = (f32[16,128]{1,0:T(8,128)S(1)}, f32[16,128]{1,0:T(8,128)S(1)}, u32[]{:S(2)}, u32[]{:S(2)}) collective-permute-start(f32[16,128]{1,0:T(8,128)S(1)} %get-tuple-element.26), channel_id=1, source_target_pairs={{0,1008},{16,32},{32,16},{48,64},{64,48},{80,96},{96,80},{112,128}... | collective-permute-start | bytes 24584 | tf_op jit(solution)/shard_map/ppermute | solution.py:374

commit v5 on v4

--- a/solution.py
+++ b/solution.py
@@ -22,15 +22,22 @@
     return pltpu.roll(plane, by % plane.shape[axis], axis)
 
 
-def edge_columns(planes):
-    count = len(planes)
+def evens(ref):
+    return ref[pl.ds(0, 8, stride=2), :]
+
+
+def odds(ref):
+    return ref[pl.ds(1, 8, stride=2), :]
+
+
+def edge_columns(planes, cols):
     shape = planes[0].shape
-    lane = lanes(shape)
+    half = lanes(shape) >> 1
     gathered = jnp.zeros(shape, jnp.float32)
     for k, plane in enumerate(planes):
-        gathered = jnp.where(lane == k, shifted(plane, k, 1), gathered)
-        gathered = jnp.where(lane == count + k, shifted(plane, count + k + 1, 1), gathered)
-    return gathered.T[: 2 * count]
+        gathered = jnp.where(half == k, shifted(plane, 2 * k + 1, 1), gathered)
+    cols[...] = gathered.T[:16]
+    return odds(cols), evens(cols)
 
 
 def plane_of(ref, k):
@@ -139,13 +146,10 @@
     )
     row_low[CORNERS, :] = corners
     row_high[CORNERS, :] = corners
-    columns = edge_columns(planes)
-    cols[0] = columns[:8]
-    cols[1] = columns[8:]
+    low, high = edge_columns(planes, cols)
     row_own[...] = messages[1 - core]
     gift[:ROW_MESSAGE, :] = messages[core]
-    gift[ROW_MESSAGE:, :] = cols[1 - core]
-    col_own[...] = cols[core]
+    gift[ROW_MESSAGE:, :], col_own[...] = in_order(high, low)[::-1]
 
 
 def turned(rim, flip):
@@ -154,18 +158,23 @@
     return jnp.take_along_axis(rim, picks, axis=1)
 
 
-def columns_of(facts, low, high):
-    return turned(low[:8], facts[2:3, :]).T, turned(high[:8], facts[3:4, :]).T
+def columns_of(facts, low, high, cols):
+    cols[pl.ds(0, 8, stride=2), :] = turned(high[:8], facts[3:4, :])
+    cols[pl.ds(1, 8, stride=2), :] = turned(low[:8], facts[2:3, :])
+    size = facts.shape[1]
+    rest = jnp.zeros((size - 16, size), jnp.float32)
+    return jnp.concatenate([cols[...], rest], 0).T
 
 
 def lateral(plane, k, rims):
-    low_row, high_row, low_col, high_col = rims
+    low_row, high_row, columns = rims
     size = plane.shape[0]
+    ends = shifted(columns, -(2 * k + 1), 1)
     row, lane = rows(plane.shape), lanes(plane.shape)
     above = jnp.where(row == 0, low_row[k : k + 1, :], shifted(plane, 1, 0))
     below = jnp.where(row == size - 1, high_row[k : k + 1, :], shifted(plane, -1, 0))
-    left = jnp.where(lane == 0, low_col[:, k : k + 1], shifted(plane, 1, 1))
-    right = jnp.where(lane == size - 1, high_col[:, k : k + 1], shifted(plane, -1, 1))
+    left = jnp.where(lane == 0, ends, shifted(plane, 1, 1))
+    right = jnp.where(lane == size - 1, ends, shifted(plane, -1, 1))
     return above, below, left, right
 
 
@@ -270,10 +279,8 @@
 
 def first_kernel(
     facts, lower, upper, below_halo, above_halo, gifts, got, passed, outer, forcing, viscosity,
-    flow_far, new_lower, new_upper, col_given, col_own, kept, cols, flow, sem,
+    flow, new_lower, new_upper, col_given, col_own, kept, cols,
 ):
-    copy = pltpu.make_async_copy(flow_far, flow, sem)
-    copy.start()
     size = facts.shape[1]
     core = core_index()
     high, low = in_order(passed[1 - core], got[ROW_MESSAGE:, :])
@@ -288,7 +295,8 @@
                 at = 2 * KEPT + 8 * side + 4 * layer + k
                 kept[at : at + 1, :] = state[k * size + edge : k * size + edge + 1, :]
     edges = [kept[KEPT * side : KEPT * side + 8, :] for side in range(2)]
-    rims = (*edges, *columns_of(facts, *in_order(gifts[1 - core, ROW_MESSAGE:], outer[...])))
+    sides = in_order(gifts[1 - core, ROW_MESSAGE:], outer[...])
+    rims = (*edges, columns_of(facts, *sides, cols))
     state = planes_of(lower, upper)
     outs = (new_lower, new_upper)
     for layer, out in enumerate(outs):
@@ -300,27 +308,23 @@
             out[k * size : (k + 1) * size, :] = new[k]
         for side in range(2):
             out[4 * size + 8 * side : 4 * size + 8 * side + 8, :] = edges[side]
-    copy.wait()
     for layer, out in enumerate(outs):
         out[3 * size : 4 * size, :] = warmed(layer, state, below_halo, above_halo, flow, rims)
-    columns = edge_columns([plane_of(ref, k) for ref in outs for k in range(4)])
-    cols[0] = columns[:8]
-    cols[1] = columns[8:]
+    low, high = edge_columns([plane_of(ref, k) for ref in outs for k in range(4)], cols)
     corners = [message[CORNERS] for message in messages]
     corners = jnp.where(lanes(corners[0].shape) < 4, corners[0], shifted(corners[1], 4, 1))
-    col_given[:8, :] = cols[1 - core]
-    col_own[:8, :] = cols[core]
+    col_given[:8, :], col_own[:8, :] = in_order(high, low)[::-1]
     col_given[8:, :] = corners
     col_own[8:, :] = corners
 
 
 def last_kernel(
     facts, lower, upper, below_halo, above_halo, gifts, outer, kept, forcing, viscosity, stress,
-    flow, new_velocity, new_heat, partial, velocity, heat, sems,
+    flow, new_velocity, new_heat, partial, velocity, heat, cols, sems,
 ):
     sides = in_order(gifts[1 - core_index()], outer[...])
     edges = halo_rows(facts, kept, below_halo, above_halo, *sides)
-    rims = (*edges, *columns_of(facts, *sides))
+    rims = (*edges, columns_of(facts, *sides, cols))
     state = planes_of(lower, upper)
     copies = []
 
@@ -337,13 +341,12 @@
         for k in range(3):
             velocity[k, layer] = new[k]
             send(velocity.at[k, layer], new_velocity.at[k, layer])
-        share = stiffness * (
-            new[0] * stress[0, layer] + new[1] * stress[1, layer] + new[2] * stress[2, layer]
-        )
-        if layer == 0:
-            partial[...] = share
-        else:
-            partial[...] = (partial[...] + share) * (1.0 / 96.0)
+    shares = [
+        stiffness_of(viscosity, facts, layer)
+        * sum(velocity[k, layer] * stress[k, layer] for k in range(3))
+        for layer in range(2)
+    ]
+    partial[...] = (shares[0] + shares[1]) * (1.0 / 96.0)
     for copy in copies:
         copy.wait()
 
@@ -420,7 +423,7 @@
             pltpu.VMEM((2, 3, 2, 8, size), f32),
             pltpu.VMEM((2, 2, 8, size), f32),
             pltpu.VMEM((2, ROW_MESSAGE, size), f32),
-            pltpu.VMEM((2, 8, size), f32),
+            pltpu.VMEM((16, size), f32),
             pltpu.SemaphoreType.DMA((10,)),
             pltpu.SemaphoreType.DMA((6,)),
         ),
@@ -438,13 +441,9 @@
     lower, upper, col_given, col_own, kept = call(
         first_kernel,
         [(4 * size + 16, size)] * 2 + [(16, size)] * 2 + [(2 * KEPT + 16, size)],
-        (facts, lower, upper, *halos, gifts, got, passed, outer, forces, visc),
-        (flow,),
-        (
-            pltpu.VMEM((2, 8, size), f32),
-            pltpu.VMEM(flow.shape, f32),
-            pltpu.SemaphoreType.DMA,
-        ),
+        (facts, lower, upper, *halos, gifts, got, passed, outer, forces, visc, flow),
+        (),
+        (pltpu.VMEM((16, size), f32),),
     )
     halos = radial(lower, upper)
     gifts = of_chip(col_given)
@@ -457,6 +456,7 @@
         (
             pltpu.VMEM(velocity.shape, f32),
             pltpu.VMEM(heat.shape, f32),
+            pltpu.VMEM((16, size), f32),
             pltpu.SemaphoreType.DMA((8,)),
         ),
         [FAR, FAR, VMEM],

time: 75.6 us -> 74.6 us (0.987)
  Pallas kernels: 4.94 us -> 3.93 us
    pallas_call x3, Pallas kernels: 4.94 us -> 3.93 us  [call(): pl.pallas_call(kernel, out_shape=[jax.ShapeDtypeStruct(shape, jnp.float32...]
where the time goes in v5:
time: 74.6 us; the launch traced here: 74.2 us
  starting transfers between devices  41.6 us (56%)
  blocking collectives  26.6 us (36%)
  Pallas kernels  3.93 us (5%)
  between operations  0.79 us (1%)
    ppermute x4, starting transfers between devices, along(): lax.ppermute(array, 'rad', [(i, i + by) for i in range(count) if 0 <= i +...  23.9 us
    all_to_all x1, blocking collectives, shards(): pieces = lax.all_to_all(partial, 'rad', 0, 0, tiled=True)  21.1 us
    ppermute x3, starting transfers between devices, over_tiles(): lax.ppermute(array, 'cap', [(i, to(i) % count) for i in range(count)])  17.7 us
    all_gather x3, blocking collectives, of_chip(): return lax.all_gather(array, 'cap', axis_index_groups=pairs)  5.5 us
    pallas_call x3, Pallas kernels, call(): pl.pallas_call(kernel, out_shape=[jax.ShapeDtypeStruct(shape, jnp.float32...  3.93 us
  transfers between devices with their start and end apart: 7, of which 1 were waited for; matrix products, arithmetic and copies ran while one was open for 0% of the time, Pallas kernels for 0%

profile of v5, /device:TPU:2, one launch (start us, length us, event | category | flops | bytes accessed | tf_op | source)
XLA Modules:
  0.0 74.2 jit_solution(7771720719352002096)
XLA Ops:
  0.6 0.0 copy-start.1
  0.6 0.0 copy-start.2
  0.7 1.6 %shard_map.103 = (f32[512,128]{1,0:T(8,128)S(1)}, f32[512,128]{1,0:T(8,128)S(1)}, f32[48,128]{1,0:T(8,128)S(1)}, f32[56,128]{1,0:T(8,128)S(1)}, f32[8,128]{1,0:T(8,128)S(1)}, /*index=5*/f32[16,128]{1,0:T(8,128)S(1)}) custom-call(f32[3,2,128,128]{3,2,1,0:T(8,128)} %bitcast.35, f32[2,128,128]{2,1,0:T(8,128)} %bitcast.36, s32[2]{0:T(128)} %mask.1, ...), custom_call_target="tpu_custom_call" | custom-call | bytes 1442824 | tf_op jit(solution)/shard_map/pallas_call | solution.py:362
  2.3 0.0 copy-start
  2.3 15.2 %collective-permute-start.1 = (f32[512,128]{1,0:T(8,128)S(1)}, f32[512,128]{1,0:T(8,128)S(1)}, u32[]{:S(2)}, u32[]{:S(2)}) collective-permute-start(f32[512,128]{1,0:T(8,128)S(1)} %get-tuple-element.18.lower), channel_id=1, source_target_pairs={{1,0},{2,1},{3,2},{4,3},{5,4},{6,5},{7,6},{8,7},{9,8},{10,9},{11,1... | collective-permute-start | bytes 786440 | tf_op jit(solution)/shard_map/ppermute | solution.py:392
  17.5 1.9 %collective-permute-start = (f32[512,128]{1,0:T(8,128)S(1)}, f32[512,128]{1,0:T(8,128)S(1)}, u32[]{:S(2)}, u32[]{:S(2)}) collective-permute-start(f32[512,128]{1,0:T(8,128)S(1)} %get-tuple-element.19.upper), channel_id=1, source_target_pairs={{0,1},{1,2},{2,3},{3,4},{4,5},{5,6},{6,7},{7,8},{8,9},{9,10},{10,1... | collective-permute-start | bytes 786440 | tf_op jit(solution)/shard_map/ppermute | solution.py:392
  19.4 1.8 %all-gather = f32[112,128]{1,0:T(8,128)S(1)} all-gather(f32[56,128]{1,0:T(8,128)S(1)} %get-tuple-element.20), channel_id=2, replica_groups={{0,16},{32,48},{64,80},{96,112},{128,144},{160,176},{192,208},{224,240}..., dimensions={0}, use_global_device_ids=true | all-gather | bytes 86016 | tf_op jit(solution)/shard_map/all_gather | solution.py:383
  21.3 1.9 %collective-permute-start.2 = (f32[96,128]{1,0:T(8,128)S(1)}, f32[96,128]{1,0:T(8,128)S(1)}, u32[]{:S(2)}, u32[]{:S(2)}) collective-permute-start(f32[96,128]{1,0:T(8,128)S(1)} %pad_maximum_fusion), channel_id=1, source_target_pairs={{0,272},{16,768},{32,304},{48,800},{64,336},{80,832},{96,368},{112... | collective-permute-start | bytes 147464 | tf_op jit(solution)/shard_map/ppermute | solution.py:377
  23.2 9.1 %collective-permute-start.3 = (f32[8,128]{1,0:T(8,128)S(1)}, f32[8,128]{1,0:T(8,128)S(1)}, u32[]{:S(2)}, u32[]{:S(2)}) collective-permute-start(f32[8,128]{1,0:T(8,128)S(1)} %get-tuple-element.22), channel_id=1, source_target_pairs={{0,1008},{16,32},{32,16},{48,64},{64,48},{80,96},{96,80},{112,128}... | collective-permute-start | bytes 12296 | tf_op jit(solution)/shard_map/ppermute | solution.py:377
  32.3 0.0 collective-permute-done.2.got
  32.3 1.8 %all-gather.1 = f32[96,128]{1,0:T(8,128)S(1)} all-gather(f32[48,128]{1,0:T(8,128)S(1)} %slice.12), channel_id=3, replica_groups={{0,16},{32,48},{64,80},{96,112},{128,144},{160,176},{192,208},{224,240}..., dimensions={0}, use_global_device_ids=true | all-gather | bytes 73728 | tf_op jit(solution)/shard_map/all_gather | solution.py:383
  34.2 0.0 collective-permute-done.3.outer
  34.2 0.0 collective-permute-done.1.above_halo
  34.2 0.0 collective-permute-done.below_halo
  34.2 0.0 copy-done.1
  34.2 0.0 copy-done.2
  34.2 0.0 copy-done
  34.2 0.0 copy-start.3
  34.2 0.9 %shard_map.104 = (f32[528,128]{1,0:T(8,128)S(1)}, f32[528,128]{1,0:T(8,128)S(1)}, f32[16,128]{1,0:T(8,128)S(1)}, f32[16,128]{1,0:T(8,128)S(1)}, f32[96,128]{1,0:T(8,128)S(1)}) custom-call(f32[16,128]{1,0:T(8,128)S(1)} %get-tuple-element.17.facts, f32[512,128]{1,0:T(8,128)S(1)} %get-tuple-element.18.lower, f32[512,128]{1,0:T(8,128)S(1)} %get-tuple-element.19.upper, ...), custom_call_target="tpu_custom_call" | custom-call | bytes 2134016 | tf_op jit(solution)/shard_map/pallas_call | solution.py:362
  35.1 2.4 %collective-permute-start.5 = (f32[528,128]{1,0:T(8,128)S(1)}, f32[528,128]{1,0:T(8,128)S(1)}, u32[]{:S(2)}, u32[]{:S(2)}) collective-permute-start(f32[528,128]{1,0:T(8,128)S(1)} %get-tuple-element.23.lower), channel_id=1, source_target_pairs={{1,0},{2,1},{3,2},{4,3},{5,4},{6,5},{7,6},{8,7},{9,8},{10,9},{11,1... | collective-permute-start | bytes 811016 | tf_op jit(solution)/shard_map/ppermute | solution.py:392
  37.6 4.3 %collective-permute-start.4 = (f32[528,128]{1,0:T(8,128)S(1)}, f32[528,128]{1,0:T(8,128)S(1)}, u32[]{:S(2)}, u32[]{:S(2)}) collective-permute-start(f32[528,128]{1,0:T(8,128)S(1)} %get-tuple-element.24.upper), channel_id=1, source_target_pairs={{0,1},{1,2},{2,3},{3,4},{4,5},{5,6},{6,7},{7,8},{8,9},{9,10},{10,1... | collective-permute-start | bytes 811016 | tf_op jit(solution)/shard_map/ppermute | solution.py:392
  41.9 6.7 %collective-permute-start.6 = (f32[16,128]{1,0:T(8,128)S(1)}, f32[16,128]{1,0:T(8,128)S(1)}, u32[]{:S(2)}, u32[]{:S(2)}) collective-permute-start(f32[16,128]{1,0:T(8,128)S(1)} %get-tuple-element.26), channel_id=1, source_target_pairs={{0,1008},{16,32},{32,16},{48,64},{64,48},{80,96},{96,80},{112,128}... | collective-permute-start | bytes 24584 | tf_op jit(solution)/shard_map/ppermute | solution.py:377
  48.6 1.8 %all-gather.2 = f32[32,128]{1,0:T(8,128)S(1)} all-gather(f32[16,128]{1,0:T(8,128)S(1)} %get-tuple-element.25), channel_id=4, replica_groups={{0,16},{32,48},{64,80},{96,112},{128,144},{160,176},{192,208},{224,240}..., dimensions={0}, use_global_device_ids=true | all-gather | bytes 24576 | tf_op jit(solution)/shard_map/all_gather | solution.py:383
  50.4 0.7 collective-permute-done.6.outer
  51.1 0.0 collective-permute-done.5.above_halo
  51.1 0.0 collective-permute-done.4.below_halo
  51.1 0.0 copy-done.3
  51.1 1.4 %shard_map.105 = (f32[3,2,128,128]{3,2,1,0:T(8,128)}, f32[2,128,128]{2,1,0:T(8,128)}, f32[128,128]{1,0:T(8,128)S(1)}) custom-call(f32[16,128]{1,0:T(8,128)S(1)} %get-tuple-element.17.facts, f32[528,128]{1,0:T(8,128)S(1)} %get-tuple-element.23.lower, f32[528,128]{1,0:T(8,128)S(1)} %get-tuple-element.24.upper, ...), custom_call_target="tpu_custom_call" | custom-call | bytes 2473984 | tf_op jit(solution)/shard_map/pallas_call | solution.py:362
  52.5 21.1 %all_to_all.9 = f32[16,8,128]{2,1,0:T(8,128)S(1)} all-to-all(f32[16,8,128]{2,1,0:T(8,128)S(1)} %bitcast.34), channel_id=1, replica_groups=mesh['cap'=64,'rad'=16] {'rad'}, dimensions={0} | all-to-all | bytes 131072 | tf_op jit(solution)/shard_map/all_to_all | solution.py:464
  73.6 0.6 reduce_sum.9
  (3 shorter events, 0.0 us)
Async XLA Ops:
  0.6 33.6 %copy-start.1 = (f32[3,2,1,128,128]{4,3,2,1,0:T(8,128)S(1)}, f32[3,2,1,128,128]{4,3,2,1,0:T(8,128)}, u32[]{:S(2)}) copy-start(f32[3,2,1,128,128]{4,3,2,1,0:T(8,128)} %param.11) | copy-start | bytes 1179652
  0.6 33.6 %copy-start.2 = (f32[2,1,128,128]{3,2,1,0:T(8,128)S(1)}, f32[2,1,128,128]{3,2,1,0:T(8,128)}, u32[]{:S(2)}) copy-start(f32[2,1,128,128]{3,2,1,0:T(8,128)} %param.13) | copy-start | bytes 393220
  2.3 31.9 %copy-start = (f32[3,2,1,128,128]{4,3,2,1,0:T(8,128)S(1)}, f32[3,2,1,128,128]{4,3,2,1,0:T(8,128)}, u32[]{:S(2)}) copy-start(f32[3,2,1,128,128]{4,3,2,1,0:T(8,128)} %param.10) | copy-start | bytes 1179652
  2.3 31.9 %collective-permute-start.1 = (f32[512,128]{1,0:T(8,128)S(1)}, f32[512,128]{1,0:T(8,128)S(1)}, u32[]{:S(2)}, u32[]{:S(2)}) collective-permute-start(f32[512,128]{1,0:T(8,128)S(1)} %get-tuple-element.18.lower), channel_id=1, source_target_pairs={{1,0},{2,1},{3,2},{4,3},{5,4},{6,5},{7,6},{8,7},{9,8},{10,9},{11,1... | collective-permute-start | bytes 786440 | tf_op jit(solution)/shard_map/ppermute | solution.py:392
  17.5 16.7 %collective-permute-start = (f32[512,128]{1,0:T(8,128)S(1)}, f32[512,128]{1,0:T(8,128)S(1)}, u32[]{:S(2)}, u32[]{:S(2)}) collective-permute-start(f32[512,128]{1,0:T(8,128)S(1)} %get-tuple-element.19.upper), channel_id=1, source_target_pairs={{0,1},{1,2},{2,3},{3,4},{4,5},{5,6},{6,7},{7,8},{8,9},{9,10},{10,1... | collective-permute-start | bytes 786440 | tf_op jit(solution)/shard_map/ppermute | solution.py:392
  21.3 11.0 %collective-permute-start.2 = (f32[96,128]{1,0:T(8,128)S(1)}, f32[96,128]{1,0:T(8,128)S(1)}, u32[]{:S(2)}, u32[]{:S(2)}) collective-permute-start(f32[96,128]{1,0:T(8,128)S(1)} %pad_maximum_fusion), channel_id=1, source_target_pairs={{0,272},{16,768},{32,304},{48,800},{64,336},{80,832},{96,368},{112... | collective-permute-start | bytes 147464 | tf_op jit(solution)/shard_map/ppermute | solution.py:377
  23.2 11.0 %collective-permute-start.3 = (f32[8,128]{1,0:T(8,128)S(1)}, f32[8,128]{1,0:T(8,128)S(1)}, u32[]{:S(2)}, u32[]{:S(2)}) collective-permute-start(f32[8,128]{1,0:T(8,128)S(1)} %get-tuple-element.22), channel_id=1, source_target_pairs={{0,1008},{16,32},{32,16},{48,64},{64,48},{80,96},{96,80},{112,128}... | collective-permute-start | bytes 12296 | tf_op jit(solution)/shard_map/ppermute | solution.py:377
  34.2 16.9 %copy-start.3 = (f32[3,2,1,128,128]{4,3,2,1,0:T(8,128)S(1)}, f32[3,2,1,128,128]{4,3,2,1,0:T(8,128)}, u32[]{:S(2)}) copy-start(f32[3,2,1,128,128]{4,3,2,1,0:T(8,128)} %param.12) | copy-start | bytes 1179652
  35.1 15.9 %collective-permute-start.5 = (f32[528,128]{1,0:T(8,128)S(1)}, f32[528,128]{1,0:T(8,128)S(1)}, u32[]{:S(2)}, u32[]{:S(2)}) collective-permute-start(f32[528,128]{1,0:T(8,128)S(1)} %get-tuple-element.23.lower), channel_id=1, source_target_pairs={{1,0},{2,1},{3,2},{4,3},{5,4},{6,5},{7,6},{8,7},{9,8},{10,9},{11,1... | collective-permute-start | bytes 811016 | tf_op jit(solution)/shard_map/ppermute | solution.py:392
  37.6 13.5 %collective-permute-start.4 = (f32[528,128]{1,0:T(8,128)S(1)}, f32[528,128]{1,0:T(8,128)S(1)}, u32[]{:S(2)}, u32[]{:S(2)}) collective-permute-start(f32[528,128]{1,0:T(8,128)S(1)} %get-tuple-element.24.upper), channel_id=1, source_target_pairs={{0,1},{1,2},{2,3},{3,4},{4,5},{5,6},{6,7},{7,8},{8,9},{9,10},{10,1... | collective-permute-start | bytes 811016 | tf_op jit(solution)/shard_map/ppermute | solution.py:392
  41.9 9.2 %collective-permute-start.6 = (f32[16,128]{1,0:T(8,128)S(1)}, f32[16,128]{1,0:T(8,128)S(1)}, u32[]{:S(2)}, u32[]{:S(2)}) collective-permute-start(f32[16,128]{1,0:T(8,128)S(1)} %get-tuple-element.26), channel_id=1, source_target_pairs={{0,1008},{16,32},{32,16},{48,64},{64,48},{80,96},{96,80},{112,128}... | collective-permute-start | bytes 24584 | tf_op jit(solution)/shard_map/ppermute | solution.py:377

commit v6 on v5

v6 whole, which is shorter than its diff:
```python
import jax
import jax.numpy as jnp
from jax import lax
from jax.experimental import pallas as pl
from jax.experimental.pallas import tpu as pltpu
from jax.sharding import PartitionSpec as P

RELAX = 0.8
STEP = 0.1
VMEM_BYTES = 24 * 1024 * 1024


def lanes(shape):
    return lax.broadcasted_iota(jnp.int32, shape, len(shape) - 1)


def rows(shape):
    return lax.broadcasted_iota(jnp.int32, shape, len(shape) - 2)


def shifted(plane, by, axis):
    return pltpu.roll(plane, by % plane.shape[axis], axis)


def plane_of(ref, k):
    size = ref.shape[1]
    return ref[k * size : (k + 1) * size, :]


EDGE, SECOND, STIFF, FORCE, FLOW, CORNERS = (slice(8 * n, 8 * n + 8) for n in range(6))
MESSAGE = 48
KEPT = 40


def core_index():
    return lax.rem(lax.axis_index("cap"), 2)


def in_order(from_partner, from_outside):
    second = core_index() == 1
    return (
        jnp.where(second, from_partner, from_outside),
        jnp.where(second, from_outside, from_partner),
    )


def pack_kernel(
    velocity, heat, mask, flips, forcing, flow, viscosity,
    lower, upper, row_own, gift, col_own, own_cols, facts,
    mask_here, flips_here, forcing_here, flow_here, viscosity_here, messages, cols, sems,
):
    size = lower.shape[1]
    copies = [
        pltpu.make_async_copy(mask, mask_here, sems.at[0]),
        pltpu.make_async_copy(flips, flips_here, sems.at[1]),
        pltpu.make_async_copy(forcing, forcing_here, sems.at[2]),
        pltpu.make_async_copy(flow, flow_here, sems.at[3]),
        pltpu.make_async_copy(viscosity, viscosity_here, sems.at[4]),
    ]
    for layer, out in enumerate((lower, upper)):
        for k in range(4):
            copies.append(
                pltpu.make_async_copy(
                    velocity.at[k, layer] if k < 3 else heat.at[layer],
                    out.at[pl.ds(k * size, size)],
                    sems.at[5 + 4 * layer + k],
                )
            )
    for copy in copies[5:] + copies[:5]:
        copy.start()
    for copy in copies:
        copy.wait()

    width = facts.shape[1]
    tiles = lax.axis_size("cap")
    tile = lax.axis_index("cap")
    bits = flips_here[...]

    def bits_of(at):
        picked = jnp.where(lanes(bits.shape) == lax.rem(at + tiles, tiles), bits, 0)
        return jnp.sum(picked.astype(jnp.float32), axis=1, keepdims=True)

    facts[0:4, :] = jnp.broadcast_to(bits_of(tile), (4, width))
    facts[8:12, :] = jnp.broadcast_to(bits_of(tile - 1), (4, width))
    facts[12:16, :] = jnp.broadcast_to(bits_of(tile + 1), (4, width))
    for layer in range(2):
        scale = 1.0 + 4.0 * mask_here[layer].astype(jnp.float32)
        facts[4 + layer : 5 + layer, :] = jnp.full((1, width), scale, jnp.float32)

    planes = [plane_of(ref, k) for ref in (lower, upper) for k in range(4)]
    given = [viscosity_here[layer] for layer in range(2)]
    given += [forcing_here[k, layer] for layer in range(2) for k in range(3)]
    given += [flow_here[k, layer] for layer in range(2) for k in range(3)]
    lane = lanes(planes[0].shape)
    gathered = jnp.zeros(planes[0].shape, jnp.float32)
    for k, plane in enumerate(planes):
        gathered = jnp.where((lane >> 2) == k, shifted(plane, 4 * k + 2, 1), gathered)
    for m, plane in enumerate(given):
        gathered = jnp.where((lane >> 1) == 16 + m, shifted(plane, 33 + 2 * m, 1), gathered)
    cols[...] = gathered.T[:64]
    lane = lanes((8, size))
    ends = []
    for edge, row in ((0, 0), (0, size - 1)):
        ends.append([plane[row : row + 1, :] for plane in planes])
    first, last = (jnp.concatenate(end, 0) for end in ends)
    corners = jnp.where(
        lane < 2,
        jnp.where(lane == 0, first, shifted(first, 2, 1)),
        jnp.where(lane == 2, shifted(last, 2, 1), shifted(last, 4, 1)),
    )
    none = jnp.zeros((1, size), jnp.float32)
    for side, (edge, second) in enumerate(((2, 3), (1, 0))):
        out = messages.at[side]
        out[EDGE, :] = cols[pl.ds(edge, 8, stride=4), :]
        out[SECOND, :] = cols[pl.ds(second, 8, stride=4), :]
        out[CORNERS, :] = corners
        own_cols[8 * side : 8 * side + 8, :] = out[EDGE, :]
        start = 33 - side
        for layer in range(2):
            at = 4 * layer
            stiff = cols[start + 2 * layer : start + 2 * layer + 1, :]
            stiff = stiff * facts[4 + layer : 5 + layer, :]
            force = start + 4 + 6 * layer
            carry = start + 16 + 6 * layer
            for k in range(3):
                out[16 + at + k : 17 + at + k, :] = stiff
                out[24 + at + k : 25 + at + k, :] = cols[force + 2 * k : force + 2 * k + 1, :]
                out[32 + at + k : 33 + at + k, :] = none
            out[19 + at : 20 + at, :] = cols[carry + 2 : carry + 3, :]
            out[27 + at : 28 + at, :] = cols[carry : carry + 1, :]
            out[35 + at : 36 + at, :] = cols[carry + 4 : carry + 5, :]
    gift[:8, :], row_own[...] = in_order(first, last)[::-1]
    core = core_index()
    gift[8:, :] = messages[1 - core]
    col_own[...] = messages[core]


def turned(rim, flip):
    lane = lanes(rim.shape)
    picks = jnp.where(jnp.broadcast_to(flip, rim.shape) > 0.5, rim.shape[1] - 1 - lane, lane)
    return jnp.take_along_axis(rim, picks, axis=1)


def columns_of(low, high, cols):
    cols[pl.ds(0, 8, stride=2), :] = high
    cols[pl.ds(1, 8, stride=2), :] = low
    size = low.shape[1]
    rest = jnp.zeros((size - 16, size), jnp.float32)
    return jnp.concatenate([cols[...], rest], 0).T


def lateral(plane, k, rims):
    low_row, high_row, columns = rims
    size = plane.shape[0]
    ends = shifted(columns, -(2 * k + 1), 1)
    row, lane = rows(plane.shape), lanes(plane.shape)
    above = jnp.where(row == 0, low_row[k : k + 1, :], shifted(plane, 1, 0))
    below = jnp.where(row == size - 1, high_row[k : k + 1, :], shifted(plane, -1, 0))
    left = jnp.where(lane == 0, ends, shifted(plane, 1, 1))
    right = jnp.where(lane == size - 1, ends, shifted(plane, -1, 1))
    return above, below, left, right


def neighbours(layer, k, state, below_halo, above_halo, rims):
    under = plane_of(below_halo, k) if layer == 0 else state[0][k]
    over = plane_of(above_halo, k) if layer == 1 else state[1][k]
    return (*lateral(state[layer][k], layer * 4 + k, rims), under, over)


def moved(layer, state, below_halo, above_halo, forcing, stiffness, rims):
    new = []
    weight = RELAX / (6.0 * stiffness + 1.0)
    for k in range(3):
        plane = state[layer][k]
        total = sum(neighbours(layer, k, state, below_halo, above_halo, rims))
        image = stiffness * (6.0 * plane - total) + plane
        drive = forcing[k, layer]
        if k == 2:
            drive = drive + state[layer][3]
        new.append(plane + weight * (drive - image))
    return new


def warmed(layer, state, below_halo, above_halo, flow, rims):
    plane = state[layer][3]
    up, down, left, right, under, over = neighbours(
        layer, 3, state, below_halo, above_halo, rims
    )
    total = up + down + left + right + under + over
    carried = 0.5 * (
        flow[0, layer] * (down - up)
        + flow[1, layer] * (right - left)
        + flow[2, layer] * (over - under)
    )
    return plane + STEP * (total - 6.0 * plane + carried + state[layer][2])


def stiffness_of(viscosity, facts, layer):
    return viscosity[layer] * facts[4 + layer : 5 + layer, :]


def planes_of(lower, upper):
    return [[plane_of(ref, k) for k in range(4)] for ref in (lower, upper)]


def halo_row(message, own, below, above, left_end, right_end, flip, low):
    edge, second = message[EDGE], message[SECOND]
    lane, row = lanes(edge.shape), rows(edge.shape)
    left = jnp.where(lane == 0, left_end, shifted(edge, 1, 1))
    right = jnp.where(lane == edge.shape[1] - 1, right_end, shifted(edge, -1, 1))
    other = shifted(edge, 4, 0)
    under = jnp.where(row < 4, shifted(below, 4, 0), other)
    over = jnp.where(row < 4, other, shifted(above, 4, 0))
    total = own + second + left + right + under + over
    stiffness = message[STIFF]
    image = stiffness * (6.0 * edge - total) + edge
    field = row % 4
    drive = message[FORCE] + jnp.where(field == 2, shifted(edge, -1, 0), 0.0)
    velocity = edge + (RELAX / (6.0 * stiffness + 1.0)) * (drive - image)
    step_i = own - second if low else second - own
    step_j = (right - left) * (1.0 - 2.0 * flip)
    carried = 0.5 * (
        message[STIFF] * step_i + message[FORCE] * step_j + message[FLOW] * (over - under)
    )
    heat = edge + STEP * (total - 6.0 * edge + carried + shifted(edge, 1, 0))
    return jnp.where(field == 3, heat, velocity)


def halo_columns(facts, kept, own_cols, below_halo, above_halo, from_low_row, from_high_row):
    size = facts.shape[1]
    below, above = below_halo[4 * size :, :], above_halo[4 * size :, :]
    at_low, at_high = from_low_row[8:16, :], from_high_row[8:16, :]

    def chosen(flag, corners, one, zero):
        flag = jnp.broadcast_to(facts[flag : flag + 1, 0:1], (8, 1))
        return jnp.where(flag > 0.5, corners[:, one : one + 1], corners[:, zero : zero + 1])

    made = []
    for side in range(2):
        flip = facts[2 + side : 3 + side, :]
        if side == 0:
            before = chosen(8, at_low, 2, 3)
            after = chosen(8 + 1, at_high, 0, 1)
        else:
            before = chosen(12, at_low, 4 + 3, 4 + 2)
            after = chosen(12 + 1, at_high, 4 + 1, 4 + 0)
        swap = jnp.broadcast_to(flip[:, 0:1], (8, 1)) > 0.5
        made.append(
            halo_row(
                kept[KEPT * side : KEPT * (side + 1), :],
                own_cols[8 * side : 8 * side + 8, :],
                below[8 * side : 8 * side + 8],
                above[8 * side : 8 * side + 8],
                jnp.where(swap, after, before),
                jnp.where(swap, before, after),
                flip,
                side == 0,
            )
        )
    return made


def first_kernel(
    facts, lower, upper, below_halo, above_halo, gifts, got, passed, outer, forcing, viscosity,
    flow, new_lower, new_upper, row_low, row_high, kept, cols,
):
    size = facts.shape[1]
    core = core_index()
    high, low = in_order(passed[1 - core], got[8:16, :])
    row_rims = turned(low, facts[0:1, :]), turned(high, facts[1:2, :])
    messages = in_order(gifts[1 - core, 8:], outer[...])
    for side, message in enumerate(messages):
        kept[KEPT * side : KEPT * (side + 1), :] = turned(
            message[:KEPT], facts[2 + side : 3 + side, :]
        )
    edges = [kept[KEPT * side : KEPT * side + 8, :] for side in range(2)]
    rims = (*row_rims, columns_of(*edges, cols))
    state = planes_of(lower, upper)
    outs = (new_lower, new_upper)
    for layer, out in enumerate(outs):
        new = moved(
            layer, state, below_halo, above_halo, forcing,
            stiffness_of(viscosity, facts, layer), rims,
        )
        for k in range(3):
            out[k * size : (k + 1) * size, :] = new[k]
        for side in range(2):
            out[4 * size + 8 * side : 4 * size + 8 * side + 8, :] = edges[side]
    for layer, out in enumerate(outs):
        out[3 * size : 4 * size, :] = warmed(layer, state, below_halo, above_halo, flow, rims)
    corners = [message[CORNERS] for message in messages]
    corners = jnp.where(lanes(corners[0].shape) < 4, corners[0], shifted(corners[1], 4, 1))
    for message, edge in ((row_low, 0), (row_high, size - 1)):
        message[8:, :] = corners
        for layer, out in enumerate(outs):
            for k in range(4):
                at = 4 * layer + k
                message[at : at + 1, :] = out[k * size + edge : k * size + edge + 1, :]


def last_velocity_kernel(
    facts, lower, upper, below_halo, above_halo, lr, hr, kept, own_cols, forcing, viscosity,
    stress, new_velocity, partial, edge_rows, columns, cols,
):
    edge_rows[0:8, :] = turned(lr[0:8, :], facts[0:1, :])
    edge_rows[8:16, :] = turned(hr[0:8, :], facts[1:2, :])
    made = halo_columns(facts, kept, own_cols, below_halo, above_halo, lr, hr)
    columns[...] = columns_of(*made, cols)
    rims = (edge_rows[0:8, :], edge_rows[8:16, :], columns[...])
    state = planes_of(lower, upper)
    for layer in range(2):
        stiffness = stiffness_of(viscosity, facts, layer)
        new = moved(layer, state, below_halo, above_halo, forcing, stiffness, rims)
        for k in range(3):
            new_velocity[k, layer] = new[k]
        share = stiffness * sum(new[k] * stress[k, layer] for k in range(3))
        partial[...] = share if layer == 0 else (partial[...] + share) * (1.0 / 96.0)


def last_heat_kernel(
    lower, upper, below_halo, above_halo, edge_rows, columns, flow, velocity_near,
    new_velocity, new_heat, heat, sems,
):
    copies = []

    def send(source, target):
        copies.append(pltpu.make_async_copy(source, target, sems.at[len(copies)]))
        copies[-1].start()

    send(velocity_near, new_velocity)
    rims = (edge_rows[0:8, :], edge_rows[8:16, :], columns[...])
    state = planes_of(lower, upper)
    for layer in range(2):
        heat[layer] = warmed(layer, state, below_halo, above_halo, flow, rims)
        send(heat.at[layer], new_heat.at[layer])
    for copy in copies:
        copy.wait()


VMEM = pl.BlockSpec(memory_space=pltpu.VMEM)
FAR = pl.BlockSpec(memory_space=pltpu.HBM)


def call(kernel, outs, near, far=(), scratch=(), out_specs=None, flops=0):
    far = [pltpu.with_memory_space_constraint(a, pltpu.HBM) for a in far]
    arrays = (*near, *far)
    moved_bytes = 4 * sum(a.size for a in arrays)
    return pl.pallas_call(
        kernel,
        out_shape=[jax.ShapeDtypeStruct(shape, jnp.float32) for shape in outs],
        in_specs=[VMEM] * len(near) + [FAR] * len(far),
        out_specs=out_specs or [VMEM] * len(outs),
        scratch_shapes=list(scratch),
        compiler_params=pltpu.CompilerParams(vmem_limit_bytes=VMEM_BYTES),
        cost_estimate=pl.CostEstimate(
            flops=flops, bytes_accessed=moved_bytes, transcendentals=0
        ),
    )(*arrays)


def over_tiles(array, to):
    count = lax.axis_size("cap")
    return lax.ppermute(array, "cap", [(i, to(i) % count) for i in range(count)])


def of_chip(array):
    count = lax.axis_size("cap")
    pairs = [[i, i + 1] for i in range(0, count, 2)]
    return lax.all_gather(array, "cap", axis_index_groups=pairs)


def to_outer(array):
    return over_tiles(array, lambda i: i + 1 if i % 2 else i - 1)


def along(array, by):
    count = lax.axis_size("rad")
    return lax.ppermute(
        array, "rad", [(i, i + by) for i in range(count) if 0 <= i + by < count]
    )


def radial(lower, upper):
    return along(upper, 1), along(lower, -1)


def shards(
    adjoint_velocity, adjoint_heat, forcing, flow_velocity, forward_stress, viscosity, layer_mask,
    face_flips,
):
    size = adjoint_velocity.shape[-1]
    quarter = lax.axis_size("cap") // 4
    velocity, heat = adjoint_velocity[:, :, 0], adjoint_heat[:, 0]
    forces, flow, stress, visc = (
        forcing[:, :, 0], flow_velocity[:, :, 0], forward_stress[:, :, 0], viscosity[:, 0]
    )
    flips = face_flips.T
    f32 = jnp.float32
    lower, upper, row_own, gift, col_own, own_cols, facts = call(
        pack_kernel,
        [(4 * size, size)] * 2
        + [(8, size), (MESSAGE + 8, size), (MESSAGE, size), (16, size), (16, size)],
        (),
        (velocity, heat, layer_mask, flips, forces, flow, visc),
        (
            pltpu.SMEM(layer_mask.shape, jnp.int32),
            pltpu.VMEM(flips.shape, jnp.int32),
            pltpu.VMEM(forces.shape, f32),
            pltpu.VMEM(flow.shape, f32),
            pltpu.VMEM(visc.shape, f32),
            pltpu.VMEM((2, MESSAGE, size), f32),
            pltpu.VMEM((64, size), f32),
            pltpu.SemaphoreType.DMA((13,)),
        ),
    )
    halos = radial(lower, upper)
    gifts = of_chip(gift)
    core = lax.rem(lax.axis_index("cap"), 2)
    given = lax.dynamic_index_in_dim(gifts, 1 - core, 0, keepdims=False)[:8]
    got = over_tiles(
        jnp.concatenate([row_own, given]),
        lambda i: i - quarter - 1 if i % 2 else i + quarter + 1,
    )
    outer = to_outer(col_own)
    passed = of_chip(got[:8])
    lower, upper, row_low, row_high, kept = call(
        first_kernel,
        [(4 * size + 16, size)] * 2 + [(16, size)] * 2 + [(2 * KEPT, size)],
        (facts, lower, upper, *halos, gifts, got, passed, outer, forces, visc, flow),
        (),
        (pltpu.VMEM((16, size), f32),),
    )
    halos = radial(lower, upper)
    from_low_row = over_tiles(row_high, lambda i: i + quarter)
    from_high_row = over_tiles(row_low, lambda i: i - quarter)
    velocity_near, partial, edge_rows, columns = call(
        last_velocity_kernel,
        [velocity.shape, (size, size), (16, size), (size, size)],
        (
            facts, lower, upper, *halos, from_low_row, from_high_row, kept, own_cols, forces,
            visc, stress,
        ),
        (),
        (pltpu.VMEM((16, size), f32),),
    )
    pieces = lax.all_to_all(partial, "rad", 0, 0, tiled=True)
    new_velocity, new_heat = call(
        last_heat_kernel,
        [velocity.shape, heat.shape],
        (lower, upper, *halos, edge_rows, columns, flow, velocity_near),
        (),
        (pltpu.VMEM(heat.shape, f32), pltpu.SemaphoreType.DMA((3,))),
        [FAR, FAR],
    )
    pieces, new_heat = lax.optimization_barrier((pieces, new_heat))
    count = lax.axis_size("rad")
    gradient = jnp.sum(pieces.reshape(count, size // count, size), axis=0)
    return new_velocity[:, :, None], new_heat[:, None], gradient[None]


def solution(mesh):
    fields = P(None, "rad", "cap", None, None)
    scalar_field = P("rad", "cap", None, None)
    return jax.shard_map(
        shards,
        mesh=mesh,
        in_specs=(
            fields, scalar_field, fields, fields, fields, scalar_field, P("rad"), P(),
        ),
        out_specs=(fields, scalar_field, P("cap", "rad", None)),
        check_vma=False,
    )
```

time: 74.6 us -> 75.8 us (1.016)
  blocking collectives: 26.6 us -> 4.7 us
  waiting for transfers between devices: 0.68 us -> 12 us
  starting transfers between devices: 41.6 us -> 52.3 us
  Pallas kernels: 3.93 us -> 4.97 us
    all_to_all x1 -> x0, blocking collectives: 21.1 us -> none  [shards(): pieces = lax.all_to_all(partial, 'rad', 0, 0, tiled=True)]
    all_to_all x0 -> x1, starting transfers between devices: none -> 10.3 us  [shards(): pieces = lax.all_to_all(partial, 'rad', 0, 0, tiled=True)]
    all_to_all x0 -> x1, waiting for transfers between devices: none -> 6.71 us  [shards(): pieces = lax.all_to_all(partial, 'rad', 0, 0, tiled=True)]
    ppermute x3 -> x4, waiting for transfers between devices: 0.67 us -> 5.28 us  [over_tiles(): lax.ppermute(array, 'cap', [(i, to(i) % count) for i in range(count)])]
    pallas_call x3 -> x4, Pallas kernels: 3.93 us -> 4.97 us  [call(): pl.pallas_call(kernel, out_shape=[jax.ShapeDtypeStruct(shape, jnp.float32...]
    all_gather x3 -> x2, blocking collectives: 5.5 us -> 4.7 us  [of_chip(): return lax.all_gather(array, 'cap', axis_index_groups=pairs)]
    ppermute x3 -> x4, starting transfers between devices: 17.7 us -> 18.1 us  [over_tiles(): lax.ppermute(array, 'cap', [(i, to(i) % count) for i in range(count)])]
  transfers between devices with their start and end apart: 7 -> 9, of which waited for: 1 -> 3; matrix products, arithmetic and copies ran while one was open for 0% -> 0% of each run, Pallas kernels for 0% -> 1%
where the time goes in v6:
time: 75.8 us; the launch traced here: 75.4 us
  starting transfers between devices  52.3 us (69%)
  waiting for transfers between devices  12 us (16%)
  Pallas kernels  4.97 us (7%)
  blocking collectives  4.7 us (6%)
  between operations  0.8 us (1%)
    ppermute x4, starting transfers between devices, along(): lax.ppermute(array, 'rad', [(i, i + by) for i in range(count) if 0 <= i +...  23.9 us
    ppermute x4, starting transfers between devices, over_tiles(): lax.ppermute(array, 'cap', [(i, to(i) % count) for i in range(count)])  18.1 us
    all_to_all x1, starting transfers between devices, shards(): pieces = lax.all_to_all(partial, 'rad', 0, 0, tiled=True)  10.3 us
    all_to_all x1, waiting for transfers between devices, shards(): pieces = lax.all_to_all(partial, 'rad', 0, 0, tiled=True)  6.71 us
    ppermute x4, waiting for transfers between devices, over_tiles(): lax.ppermute(array, 'cap', [(i, to(i) % count) for i in range(count)])  5.28 us
    pallas_call x4, Pallas kernels, call(): pl.pallas_call(kernel, out_shape=[jax.ShapeDtypeStruct(shape, jnp.float32...  4.97 us
    all_gather x2, blocking collectives, of_chip(): return lax.all_gather(array, 'cap', axis_index_groups=pairs)  4.7 us
  transfers between devices with their start and end apart: 9, of which 3 were waited for; matrix products, arithmetic and copies ran while one was open for 0% of the time, Pallas kernels for 1%

profile of v6, /device:TPU:2, one launch (start us, length us, event | category | flops | bytes accessed | tf_op | source)
XLA Modules:
  0.0 75.4 jit_solution(7480535426797046251)
XLA Ops:
  0.6 0.0 copy-start
  0.6 0.0 copy-start.1
  0.7 2.1 %shard_map.103 = (f32[512,128]{1,0:T(8,128)S(1)}, f32[512,128]{1,0:T(8,128)S(1)}, f32[8,128]{1,0:T(8,128)S(1)}, f32[56,128]{1,0:T(8,128)S(1)}, f32[48,128]{1,0:T...) custom-call(f32[3,2,128,128]{3,2,1,0:T(8,128)} %bitcast.35, f32[2,128,128]{2,1,0:T(8,128)} %bitcast.37, s32[2]{0:T(128)} %mask.1, ...), custom_call_target="tpu_custom_call" | custom-call | bytes 1442824 | tf_op jit(solution)/shard_map/pallas_call | solution.py:348
  2.8 0.0 copy-start.2
  2.8 15.2 %collective-permute-start.1 = (f32[512,128]{1,0:T(8,128)S(1)}, f32[512,128]{1,0:T(8,128)S(1)}, u32[]{:S(2)}, u32[]{:S(2)}) collective-permute-start(f32[512,128]{1,0:T(8,128)S(1)} %get-tuple-element.24.lower), channel_id=1, source_target_pairs={{1,0},{2,1},{3,2},{4,3},{5,4},{6,5},{7,6},{8,7},{9,8},{10,9},{11,1... | collective-permute-start | bytes 786440 | tf_op jit(solution)/shard_map/ppermute | solution.py:378
  18.0 1.9 %collective-permute-start = (f32[512,128]{1,0:T(8,128)S(1)}, f32[512,128]{1,0:T(8,128)S(1)}, u32[]{:S(2)}, u32[]{:S(2)}) collective-permute-start(f32[512,128]{1,0:T(8,128)S(1)} %get-tuple-element.25.upper), channel_id=1, source_target_pairs={{0,1},{1,2},{2,3},{3,4},{4,5},{5,6},{6,7},{7,8},{8,9},{9,10},{10,1... | collective-permute-start | bytes 786440 | tf_op jit(solution)/shard_map/ppermute | solution.py:378
  20.0 8.2 %collective-permute-start.3 = (f32[48,128]{1,0:T(8,128)S(1)}, f32[48,128]{1,0:T(8,128)S(1)}, u32[]{:S(2)}, u32[]{:S(2)}) collective-permute-start(f32[48,128]{1,0:T(8,128)S(1)} %get-tuple-element.28), channel_id=1, source_target_pairs={{0,1008},{16,32},{32,16},{48,64},{64,48},{80,96},{96,80},{112,128}... | collective-permute-start | bytes 73736 | tf_op jit(solution)/shard_map/ppermute | solution.py:363
  28.2 1.8 %all-gather = f32[112,128]{1,0:T(8,128)S(1)} all-gather(f32[56,128]{1,0:T(8,128)S(1)} %get-tuple-element.26), channel_id=2, replica_groups={{0,16},{32,48},{64,80},{96,112},{128,144},{160,176},{192,208},{224,240}..., dimensions={0}, use_global_device_ids=true | all-gather | bytes 86016 | tf_op jit(solution)/shard_map/all_gather | solution.py:369
  30.0 1.9 %collective-permute-start.2 = (f32[16,128]{1,0:T(8,128)S(1)}, f32[16,128]{1,0:T(8,128)S(1)}, u32[]{:S(2)}, u32[]{:S(2)}) collective-permute-start(f32[16,128]{1,0:T(8,128)S(1)} %pad_maximum_fusion), channel_id=1, source_target_pairs={{0,272},{16,768},{32,304},{48,800},{64,336},{80,832},{96,368},{112... | collective-permute-start | bytes 24584 | tf_op jit(solution)/shard_map/ppermute | solution.py:363
  32.0 3.9 %collective-permute-done.2.got = f32[16,128]{1,0:T(8,128)S(1)} collective-permute-done((f32[16,128]{1,0:T(8,128)S(1)}, f32[16,128]{1,0:T(8,128)S(1)}, u32[]{:S(2)}, u32[]{:S(2)}) %collective-permute-start.2) | collective-permute-done | bytes 8224 | tf_op jit(solution)/shard_map/ppermute | solution.py:363
  35.9 2.9 %all-gather.1 = f32[16,128]{1,0:T(8,128)S(1)} all-gather(f32[8,128]{1,0:T(8,128)S(1)} %slice.12), channel_id=3, replica_groups={{0,16},{32,48},{64,80},{96,112},{128,144},{160,176},{192,208},{224,240}..., dimensions={0}, use_global_device_ids=true | all-gather | bytes 12288 | tf_op jit(solution)/shard_map/all_gather | solution.py:369
  38.8 0.0 collective-permute-done.3.outer
  38.8 0.0 collective-permute-done.1.above_halo
  38.8 0.0 collective-permute-done.below_halo
  38.8 0.0 copy-done
  38.8 0.0 copy-done.1
  38.8 0.0 copy-done.2
  38.8 0.0 copy-start.3
  38.8 0.7 shard_map.104
  39.5 2.5 %collective-permute-start.5 = (f32[528,128]{1,0:T(8,128)S(1)}, f32[528,128]{1,0:T(8,128)S(1)}, u32[]{:S(2)}, u32[]{:S(2)}) collective-permute-start(f32[528,128]{1,0:T(8,128)S(1)} %get-tuple-element.29.lower), channel_id=1, source_target_pairs={{1,0},{2,1},{3,2},{4,3},{5,4},{6,5},{7,6},{8,7},{9,8},{10,9},{11,1... | collective-permute-start | bytes 811016 | tf_op jit(solution)/shard_map/ppermute | solution.py:378
  42.0 4.3 %collective-permute-start.4 = (f32[528,128]{1,0:T(8,128)S(1)}, f32[528,128]{1,0:T(8,128)S(1)}, u32[]{:S(2)}, u32[]{:S(2)}) collective-permute-start(f32[528,128]{1,0:T(8,128)S(1)} %get-tuple-element.30.upper), channel_id=1, source_target_pairs={{0,1},{1,2},{2,3},{3,4},{4,5},{5,6},{6,7},{7,8},{8,9},{9,10},{10,1... | collective-permute-start | bytes 811016 | tf_op jit(solution)/shard_map/ppermute | solution.py:378
  46.3 1.9 %collective-permute-start.6 = (f32[16,128]{1,0:T(8,128)S(1)}, f32[16,128]{1,0:T(8,128)S(1)}, u32[]{:S(2)}, u32[]{:S(2)}) collective-permute-start(f32[16,128]{1,0:T(8,128)S(1)} %get-tuple-element.31), channel_id=1, source_target_pairs={{0,256},{16,272},{32,288},{48,304},{64,320},{80,336},{96,352},{112... | collective-permute-start | bytes 24584 | tf_op jit(solution)/shard_map/ppermute | solution.py:363
  48.2 6.0 %collective-permute-start.7 = (f32[16,128]{1,0:T(8,128)S(1)}, f32[16,128]{1,0:T(8,128)S(1)}, u32[]{:S(2)}, u32[]{:S(2)}) collective-permute-start(f32[16,128]{1,0:T(8,128)S(1)} %get-tuple-element.32), channel_id=1, source_target_pairs={{0,768},{16,784},{32,800},{48,816},{64,832},{80,848},{96,864},{112... | collective-permute-start | bytes 24584 | tf_op jit(solution)/shard_map/ppermute | solution.py:363
  54.2 0.0 collective-permute-done.6.lr
  54.2 1.3 %collective-permute-done.7.hr = f32[16,128]{1,0:T(8,128)S(1)} collective-permute-done((f32[16,128]{1,0:T(8,128)S(1)}, f32[16,128]{1,0:T(8,128)S(1)}, u32[]{:S(2)}, u32[]{:S(2)}) %collective-permute-start.7) | collective-permute-done | bytes 8224 | tf_op jit(solution)/shard_map/ppermute | solution.py:363
  55.6 0.0 collective-permute-done.5.above_halo
  55.6 0.0 collective-permute-done.4.below_halo
  55.6 0.0 copy-done.3
  55.6 1.3 %shard_map.105 = (f32[3,2,128,128]{3,2,1,0:T(8,128)S(1)}, f32[128,128]{1,0:T(8,128)}, f32[16,128]{1,0:T(8,128)S(1)}, f32[128,128]{1,0:T(8,128)S(1)}) custom-call(f32[16,128]{1,0:T(8,128)S(1)} %get-tuple-element.23.facts, f32[528,128]{1,0:T(8,128)S(1)} %get-tuple-element.29.lower, f32[528,128]{1,0:T(8,128)S(1)} %get-tuple-element.30.upper, ...), custom_call_target="tpu_custom_call" | custom-call | bytes 2072576 | tf_op jit(solution)/shard_map/pallas_call | solution.py:348
  56.8 10.3 %all-to-all-start = ((f32[16,8,128]{2,1,0:T(8,128)}), f32[16,8,128]{2,1,0:T(8,128)S(1)}, u32[]{:S(2)}, u32[]{:S(2)}) async-start(f32[16,8,128]{2,1,0:T(8,128)} %bitcast.12), calls=%async_computation | async-start | bytes 131072 | tf_op jit(solution)/shard_map/all_to_all | solution.py:446
  67.2 0.9 %shard_map.106 = (f32[3,2,128,128]{3,2,1,0:T(8,128)}, f32[2,128,128]{2,1,0:T(8,128)}) custom-call(f32[528,128]{1,0:T(8,128)S(1)} %get-tuple-element.29.lower, f32[528,128]{1,0:T(8,128)S(1)} %get-tuple-element.30.upper, f32[528,128]{1,0:T(8,128)S(1)} %collective-permute-done.4.below_halo, f32[528,128]{1,0:T(8,128)S(1)} %collective-permute-done.5.above_halo, ...), custom_call_target="tpu_custom_call" | custom-call | bytes 1941504 | tf_op jit(solution)/shard_map/pallas_call | solution.py:348
  68.0 6.7 %all-to-all-done = f32[16,8,128]{2,1,0:T(8,128)S(1)} async-done(((f32[16,8,128]{2,1,0:T(8,128)}), f32[16,8,128]{2,1,0:T(8,128)S(1)}, u32[]{:S(2)}, u32[]{:S(2)}) %all-to-all-start) | async-done | bytes 65568 | tf_op jit(solution)/shard_map/all_to_all | solution.py:446
  74.8 0.6 bitcast_reduce_fusion
  (3 shorter events, 0.0 us)
Async XLA Ops:
  0.6 38.1 %copy-start = (f32[3,2,1,128,128]{4,3,2,1,0:T(8,128)S(1)}, f32[3,2,1,128,128]{4,3,2,1,0:T(8,128)}, u32[]{:S(2)}) copy-start(f32[3,2,1,128,128]{4,3,2,1,0:T(8,128)} %param.10) | copy-start | bytes 1179652
  0.6 38.1 %copy-start.1 = (f32[3,2,1,128,128]{4,3,2,1,0:T(8,128)S(1)}, f32[3,2,1,128,128]{4,3,2,1,0:T(8,128)}, u32[]{:S(2)}) copy-start(f32[3,2,1,128,128]{4,3,2,1,0:T(8,128)} %param.11) | copy-start | bytes 1179652
  2.8 36.0 %copy-start.2 = (f32[2,1,128,128]{3,2,1,0:T(8,128)S(1)}, f32[2,1,128,128]{3,2,1,0:T(8,128)}, u32[]{:S(2)}) copy-start(f32[2,1,128,128]{3,2,1,0:T(8,128)} %param.13) | copy-start | bytes 393220
  2.8 36.0 %collective-permute-start.1 = (f32[512,128]{1,0:T(8,128)S(1)}, f32[512,128]{1,0:T(8,128)S(1)}, u32[]{:S(2)}, u32[]{:S(2)}) collective-permute-start(f32[512,128]{1,0:T(8,128)S(1)} %get-tuple-element.24.lower), channel_id=1, source_target_pairs={{1,0},{2,1},{3,2},{4,3},{5,4},{6,5},{7,6},{8,7},{9,8},{10,9},{11,1... | collective-permute-start | bytes 786440 | tf_op jit(solution)/shard_map/ppermute | solution.py:378
  18.0 20.7 %collective-permute-start = (f32[512,128]{1,0:T(8,128)S(1)}, f32[512,128]{1,0:T(8,128)S(1)}, u32[]{:S(2)}, u32[]{:S(2)}) collective-permute-start(f32[512,128]{1,0:T(8,128)S(1)} %get-tuple-element.25.upper), channel_id=1, source_target_pairs={{0,1},{1,2},{2,3},{3,4},{4,5},{5,6},{6,7},{7,8},{8,9},{9,10},{10,1... | collective-permute-start | bytes 786440 | tf_op jit(solution)/shard_map/ppermute | solution.py:378
  20.0 18.8 %collective-permute-start.3 = (f32[48,128]{1,0:T(8,128)S(1)}, f32[48,128]{1,0:T(8,128)S(1)}, u32[]{:S(2)}, u32[]{:S(2)}) collective-permute-start(f32[48,128]{1,0:T(8,128)S(1)} %get-tuple-element.28), channel_id=1, source_target_pairs={{0,1008},{16,32},{32,16},{48,64},{64,48},{80,96},{96,80},{112,128}... | collective-permute-start | bytes 73736 | tf_op jit(solution)/shard_map/ppermute | solution.py:363
  30.0 5.9 %collective-permute-start.2 = (f32[16,128]{1,0:T(8,128)S(1)}, f32[16,128]{1,0:T(8,128)S(1)}, u32[]{:S(2)}, u32[]{:S(2)}) collective-permute-start(f32[16,128]{1,0:T(8,128)S(1)} %pad_maximum_fusion), channel_id=1, source_target_pairs={{0,272},{16,768},{32,304},{48,800},{64,336},{80,832},{96,368},{112... | collective-permute-start | bytes 24584 | tf_op jit(solution)/shard_map/ppermute | solution.py:363
  38.8 16.8 %copy-start.3 = (f32[3,2,1,128,128]{4,3,2,1,0:T(8,128)S(1)}, f32[3,2,1,128,128]{4,3,2,1,0:T(8,128)}, u32[]{:S(2)}) copy-start(f32[3,2,1,128,128]{4,3,2,1,0:T(8,128)} %param.12) | copy-start | bytes 1179652
  39.5 16.1 %collective-permute-start.5 = (f32[528,128]{1,0:T(8,128)S(1)}, f32[528,128]{1,0:T(8,128)S(1)}, u32[]{:S(2)}, u32[]{:S(2)}) collective-permute-start(f32[528,128]{1,0:T(8,128)S(1)} %get-tuple-element.29.lower), channel_id=1, source_target_pairs={{1,0},{2,1},{3,2},{4,3},{5,4},{6,5},{7,6},{8,7},{9,8},{10,9},{11,1... | collective-permute-start | bytes 811016 | tf_op jit(solution)/shard_map/ppermute | solution.py:378
  42.0 13.6 %collective-permute-start.4 = (f32[528,128]{1,0:T(8,128)S(1)}, f32[528,128]{1,0:T(8,128)S(1)}, u32[]{:S(2)}, u32[]{:S(2)}) collective-permute-start(f32[528,128]{1,0:T(8,128)S(1)} %get-tuple-element.30.upper), channel_id=1, source_target_pairs={{0,1},{1,2},{2,3},{3,4},{4,5},{5,6},{6,7},{7,8},{8,9},{9,10},{10,1... | collective-permute-start | bytes 811016 | tf_op jit(solution)/shard_map/ppermute | solution.py:378
  46.3 8.0 %collective-permute-start.6 = (f32[16,128]{1,0:T(8,128)S(1)}, f32[16,128]{1,0:T(8,128)S(1)}, u32[]{:S(2)}, u32[]{:S(2)}) collective-permute-start(f32[16,128]{1,0:T(8,128)S(1)} %get-tuple-element.31), channel_id=1, source_target_pairs={{0,256},{16,272},{32,288},{48,304},{64,320},{80,336},{96,352},{112... | collective-permute-start | bytes 24584 | tf_op jit(solution)/shard_map/ppermute | solution.py:363
  48.2 7.4 %collective-permute-start.7 = (f32[16,128]{1,0:T(8,128)S(1)}, f32[16,128]{1,0:T(8,128)S(1)}, u32[]{:S(2)}, u32[]{:S(2)}) collective-permute-start(f32[16,128]{1,0:T(8,128)S(1)} %get-tuple-element.32), channel_id=1, source_target_pairs={{0,768},{16,784},{32,800},{48,816},{64,832},{80,848},{96,864},{112... | collective-permute-start | bytes 24584 | tf_op jit(solution)/shard_map/ppermute | solution.py:363
  56.8 17.9 %all-to-all-start = ((f32[16,8,128]{2,1,0:T(8,128)}), f32[16,8,128]{2,1,0:T(8,128)S(1)}, u32[]{:S(2)}, u32[]{:S(2)}) async-start(f32[16,8,128]{2,1,0:T(8,128)} %bitcast.12), calls=%async_computation | async-start | bytes 131072 | tf_op jit(solution)/shard_map/all_to_all | solution.py:446

commit v7 on v5

--- a/solution.py
+++ b/solution.py
@@ -318,35 +318,42 @@
     col_own[8:, :] = corners
 
 
-def last_kernel(
+def last_velocity_kernel(
     facts, lower, upper, below_halo, above_halo, gifts, outer, kept, forcing, viscosity, stress,
-    flow, new_velocity, new_heat, partial, velocity, heat, cols, sems,
+    new_velocity, partial, edge_rows, columns, cols,
 ):
     sides = in_order(gifts[1 - core_index()], outer[...])
     edges = halo_rows(facts, kept, below_halo, above_halo, *sides)
-    rims = (*edges, columns_of(facts, *sides, cols))
+    for side in range(2):
+        edge_rows[8 * side : 8 * side + 8, :] = edges[side]
+    columns[...] = columns_of(facts, *sides, cols)
+    rims = (*edges, columns[...])
     state = planes_of(lower, upper)
-    copies = []
-
-    def send(source, target):
-        copies.append(pltpu.make_async_copy(source, target, sems.at[len(copies)]))
-        copies[-1].start()
-
-    for layer in range(2):
-        heat[layer] = warmed(layer, state, below_halo, above_halo, flow, rims)
-        send(heat.at[layer], new_heat.at[layer])
     for layer in range(2):
         stiffness = stiffness_of(viscosity, facts, layer)
         new = moved(layer, state, below_halo, above_halo, forcing, stiffness, rims)
         for k in range(3):
-            velocity[k, layer] = new[k]
-            send(velocity.at[k, layer], new_velocity.at[k, layer])
-    shares = [
-        stiffness_of(viscosity, facts, layer)
-        * sum(velocity[k, layer] * stress[k, layer] for k in range(3))
-        for layer in range(2)
-    ]
-    partial[...] = (shares[0] + shares[1]) * (1.0 / 96.0)
+            new_velocity[k, layer] = new[k]
+        share = stiffness * sum(new[k] * stress[k, layer] for k in range(3))
+        partial[...] = share if layer == 0 else (partial[...] + share) * (1.0 / 96.0)
+
+
+def last_heat_kernel(
+    lower, upper, below_halo, above_halo, edge_rows, columns, flow, velocity_near,
+    new_velocity, new_heat, heat, sems,
+):
+    copies = []
+
+    def send(source, target):
+        copies.append(pltpu.make_async_copy(source, target, sems.at[len(copies)]))
+        copies[-1].start()
+
+    send(velocity_near, new_velocity)
+    rims = (edge_rows[0:8, :], edge_rows[8:16, :], columns[...])
+    state = planes_of(lower, upper)
+    for layer in range(2):
+        heat[layer] = warmed(layer, state, below_halo, above_halo, flow, rims)
+        send(heat.at[layer], new_heat.at[layer])
     for copy in copies:
         copy.wait()
 
@@ -448,20 +455,23 @@
     halos = radial(lower, upper)
     gifts = of_chip(col_given)
     outer = to_outer(col_own)
-    new_velocity, new_heat, partial = call(
-        last_kernel,
-        [velocity.shape, heat.shape, (size, size)],
-        (facts, lower, upper, *halos, gifts, outer, kept, forces, visc, stress, flow),
+    velocity_near, partial, edge_rows, columns = call(
+        last_velocity_kernel,
+        [velocity.shape, (size, size), (16, size), (size, size)],
+        (facts, lower, upper, *halos, gifts, outer, kept, forces, visc, stress),
         (),
-        (
-            pltpu.VMEM(velocity.shape, f32),
-            pltpu.VMEM(heat.shape, f32),
-            pltpu.VMEM((16, size), f32),
-            pltpu.SemaphoreType.DMA((8,)),
-        ),
-        [FAR, FAR, VMEM],
+        (pltpu.VMEM((16, size), f32),),
     )
     pieces = lax.all_to_all(partial, "rad", 0, 0, tiled=True)
+    new_velocity, new_heat = call(
+        last_heat_kernel,
+        [velocity.shape, heat.shape],
+        (lower, upper, *halos, edge_rows, columns, flow, velocity_near),
+        (),
+        (pltpu.VMEM(heat.shape, f32), pltpu.SemaphoreType.DMA((3,))),
+        [FAR, FAR],
+    )
+    pieces, new_heat = lax.optimization_barrier((pieces, new_heat))
     count = lax.axis_size("rad")
     gradient = jnp.sum(pieces.reshape(count, size // count, size), axis=0)
     return new_velocity[:, :, None], new_heat[:, None], gradient[None]

time: 74.6 us -> 74.6 us (level)
  blocking collectives: 26.6 us -> 5.5 us
  starting transfers between devices: 41.6 us -> 55.3 us
  waiting for transfers between devices: 0.68 us -> 7.39 us
    all_to_all x1 -> x0, blocking collectives: 21.1 us -> none  [shards(): pieces = lax.all_to_all(partial, 'rad', 0, 0, tiled=True)]
    all_to_all x0 -> x1, starting transfers between devices: none -> 13.7 us  [shards(): pieces = lax.all_to_all(partial, 'rad', 0, 0, tiled=True)]
    all_to_all x0 -> x1, waiting for transfers between devices: none -> 6.71 us  [shards(): pieces = lax.all_to_all(partial, 'rad', 0, 0, tiled=True)]
    pallas_call x3 -> x4, Pallas kernels: 3.93 us -> 4.6 us  [call(): pl.pallas_call(kernel, out_shape=[jax.ShapeDtypeStruct(shape, jnp.float32...]
  transfers between devices with their start and end apart: 7 -> 8, of which waited for: 1 -> 2; matrix products, arithmetic and copies ran while one was open for 0% -> 0% of each run, Pallas kernels for 0% -> 1%
where the time goes in v7:
time: 74.6 us; the launch traced here: 74.2 us
  starting transfers between devices  55.3 us (74%)
  waiting for transfers between devices  7.39 us (10%)
  blocking collectives  5.5 us (7%)
  Pallas kernels  4.6 us (6%)
  between operations  0.8 us (1%)
    ppermute x4, starting transfers between devices, along(): lax.ppermute(array, 'rad', [(i, i + by) for i in range(count) if 0 <= i +...  23.9 us
    ppermute x3, starting transfers between devices, over_tiles(): lax.ppermute(array, 'cap', [(i, to(i) % count) for i in range(count)])  17.7 us
    all_to_all x1, starting transfers between devices, shards(): pieces = lax.all_to_all(partial, 'rad', 0, 0, tiled=True)  13.7 us
    all_to_all x1, waiting for transfers between devices, shards(): pieces = lax.all_to_all(partial, 'rad', 0, 0, tiled=True)  6.71 us
    all_gather x3, blocking collectives, of_chip(): return lax.all_gather(array, 'cap', axis_index_groups=pairs)  5.5 us
    pallas_call x4, Pallas kernels, call(): pl.pallas_call(kernel, out_shape=[jax.ShapeDtypeStruct(shape, jnp.float32...  4.6 us
  transfers between devices with their start and end apart: 8, of which 2 were waited for; matrix products, arithmetic and copies ran while one was open for 0% of the time, Pallas kernels for 1%

profile of v7, /device:TPU:2, one launch (start us, length us, event | category | flops | bytes accessed | tf_op | source)
XLA Modules:
  0.0 74.2 jit_solution(7961553903872082743)
XLA Ops:
  0.6 0.0 copy-start.1
  0.6 0.0 copy-start.2
  0.7 1.6 %shard_map.103 = (f32[512,128]{1,0:T(8,128)S(1)}, f32[512,128]{1,0:T(8,128)S(1)}, f32[48,128]{1,0:T(8,128)S(1)}, f32[56,128]{1,0:T(8,128)S(1)}, f32[8,128]{1,0:T(8,128)S(1)}, /*index=5*/f32[16,128]{1,0:T(8,128)S(1)}) custom-call(f32[3,2,128,128]{3,2,1,0:T(8,128)} %bitcast.37, f32[2,128,128]{2,1,0:T(8,128)} %bitcast.39, s32[2]{0:T(128)} %mask.1, ...), custom_call_target="tpu_custom_call" | custom-call | bytes 1442824 | tf_op jit(solution)/shard_map/pallas_call | solution.py:369
  2.3 0.0 copy-start
  2.3 15.2 %collective-permute-start.1 = (f32[512,128]{1,0:T(8,128)S(1)}, f32[512,128]{1,0:T(8,128)S(1)}, u32[]{:S(2)}, u32[]{:S(2)}) collective-permute-start(f32[512,128]{1,0:T(8,128)S(1)} %get-tuple-element.23.lower), channel_id=1, source_target_pairs={{1,0},{2,1},{3,2},{4,3},{5,4},{6,5},{7,6},{8,7},{9,8},{10,9},{11,1... | collective-permute-start | bytes 786440 | tf_op jit(solution)/shard_map/ppermute | solution.py:399
  17.5 1.9 %collective-permute-start = (f32[512,128]{1,0:T(8,128)S(1)}, f32[512,128]{1,0:T(8,128)S(1)}, u32[]{:S(2)}, u32[]{:S(2)}) collective-permute-start(f32[512,128]{1,0:T(8,128)S(1)} %get-tuple-element.24.upper), channel_id=1, source_target_pairs={{0,1},{1,2},{2,3},{3,4},{4,5},{5,6},{6,7},{7,8},{8,9},{9,10},{10,1... | collective-permute-start | bytes 786440 | tf_op jit(solution)/shard_map/ppermute | solution.py:399
  19.4 1.8 %all-gather = f32[112,128]{1,0:T(8,128)S(1)} all-gather(f32[56,128]{1,0:T(8,128)S(1)} %get-tuple-element.25), channel_id=2, replica_groups={{0,16},{32,48},{64,80},{96,112},{128,144},{160,176},{192,208},{224,240}..., dimensions={0}, use_global_device_ids=true | all-gather | bytes 86016 | tf_op jit(solution)/shard_map/all_gather | solution.py:390
  21.3 1.9 %collective-permute-start.2 = (f32[96,128]{1,0:T(8,128)S(1)}, f32[96,128]{1,0:T(8,128)S(1)}, u32[]{:S(2)}, u32[]{:S(2)}) collective-permute-start(f32[96,128]{1,0:T(8,128)S(1)} %pad_maximum_fusion), channel_id=1, source_target_pairs={{0,272},{16,768},{32,304},{48,800},{64,336},{80,832},{96,368},{112... | collective-permute-start | bytes 147464 | tf_op jit(solution)/shard_map/ppermute | solution.py:384
  23.2 9.1 %collective-permute-start.3 = (f32[8,128]{1,0:T(8,128)S(1)}, f32[8,128]{1,0:T(8,128)S(1)}, u32[]{:S(2)}, u32[]{:S(2)}) collective-permute-start(f32[8,128]{1,0:T(8,128)S(1)} %get-tuple-element.27), channel_id=1, source_target_pairs={{0,1008},{16,32},{32,16},{48,64},{64,48},{80,96},{96,80},{112,128}... | collective-permute-start | bytes 12296 | tf_op jit(solution)/shard_map/ppermute | solution.py:384
  32.3 0.0 collective-permute-done.2.got
  32.3 1.8 %all-gather.1 = f32[96,128]{1,0:T(8,128)S(1)} all-gather(f32[48,128]{1,0:T(8,128)S(1)} %slice.12), channel_id=3, replica_groups={{0,16},{32,48},{64,80},{96,112},{128,144},{160,176},{192,208},{224,240}..., dimensions={0}, use_global_device_ids=true | all-gather | bytes 73728 | tf_op jit(solution)/shard_map/all_gather | solution.py:390
  34.2 0.0 collective-permute-done.3.outer
  34.2 0.0 collective-permute-done.1.above_halo
  34.2 0.0 collective-permute-done.below_halo
  34.2 0.0 copy-done.1
  34.2 0.0 copy-done.2
  34.2 0.0 copy-done
  34.2 0.0 copy-start.3
  34.2 0.9 %shard_map.104 = (f32[528,128]{1,0:T(8,128)S(1)}, f32[528,128]{1,0:T(8,128)S(1)}, f32[16,128]{1,0:T(8,128)S(1)}, f32[16,128]{1,0:T(8,128)S(1)}, f32[96,128]{1,0:T(8,128)S(1)}) custom-call(f32[16,128]{1,0:T(8,128)S(1)} %get-tuple-element.22.facts, f32[512,128]{1,0:T(8,128)S(1)} %get-tuple-element.23.lower, f32[512,128]{1,0:T(8,128)S(1)} %get-tuple-element.24.upper, ...), custom_call_target="tpu_custom_call" | custom-call | bytes 2134016 | tf_op jit(solution)/shard_map/pallas_call | solution.py:369
  35.1 2.4 %collective-permute-start.5 = (f32[528,128]{1,0:T(8,128)S(1)}, f32[528,128]{1,0:T(8,128)S(1)}, u32[]{:S(2)}, u32[]{:S(2)}) collective-permute-start(f32[528,128]{1,0:T(8,128)S(1)} %get-tuple-element.28.lower), channel_id=1, source_target_pairs={{1,0},{2,1},{3,2},{4,3},{5,4},{6,5},{7,6},{8,7},{9,8},{10,9},{11,1... | collective-permute-start | bytes 811016 | tf_op jit(solution)/shard_map/ppermute | solution.py:399
  37.6 4.3 %collective-permute-start.4 = (f32[528,128]{1,0:T(8,128)S(1)}, f32[528,128]{1,0:T(8,128)S(1)}, u32[]{:S(2)}, u32[]{:S(2)}) collective-permute-start(f32[528,128]{1,0:T(8,128)S(1)} %get-tuple-element.29.upper), channel_id=1, source_target_pairs={{0,1},{1,2},{2,3},{3,4},{4,5},{5,6},{6,7},{7,8},{8,9},{9,10},{10,1... | collective-permute-start | bytes 811016 | tf_op jit(solution)/shard_map/ppermute | solution.py:399
  41.9 6.7 %collective-permute-start.6 = (f32[16,128]{1,0:T(8,128)S(1)}, f32[16,128]{1,0:T(8,128)S(1)}, u32[]{:S(2)}, u32[]{:S(2)}) collective-permute-start(f32[16,128]{1,0:T(8,128)S(1)} %get-tuple-element.31), channel_id=1, source_target_pairs={{0,1008},{16,32},{32,16},{48,64},{64,48},{80,96},{96,80},{112,128}... | collective-permute-start | bytes 24584 | tf_op jit(solution)/shard_map/ppermute | solution.py:384
  48.6 1.8 %all-gather.2 = f32[32,128]{1,0:T(8,128)S(1)} all-gather(f32[16,128]{1,0:T(8,128)S(1)} %get-tuple-element.30), channel_id=4, replica_groups={{0,16},{32,48},{64,80},{96,112},{128,144},{160,176},{192,208},{224,240}..., dimensions={0}, use_global_device_ids=true | all-gather | bytes 24576 | tf_op jit(solution)/shard_map/all_gather | solution.py:390
  50.4 0.7 collective-permute-done.6.outer
  51.1 0.0 collective-permute-done.5.above_halo
  51.1 0.0 collective-permute-done.4.below_halo
  51.1 0.0 copy-done.3
  51.1 1.2 %shard_map.105 = (f32[3,2,128,128]{3,2,1,0:T(8,128)S(1)}, f32[128,128]{1,0:T(8,128)}, f32[16,128]{1,0:T(8,128)S(1)}, f32[128,128]{1,0:T(8,128)S(1)}) custom-call(f32[16,128]{1,0:T(8,128)S(1)} %get-tuple-element.22.facts, f32[528,128]{1,0:T(8,128)S(1)} %get-tuple-element.28.lower, f32[528,128]{1,0:T(8,128)S(1)} %get-tuple-element.29.upper, ...), custom_call_target="tpu_custom_call" | custom-call | bytes 2080768 | tf_op jit(solution)/shard_map/pallas_call | solution.py:369
  52.3 13.7 %all-to-all-start = ((f32[16,8,128]{2,1,0:T(8,128)}), f32[16,8,128]{2,1,0:T(8,128)S(1)}, u32[]{:S(2)}, u32[]{:S(2)}) async-start(f32[16,8,128]{2,1,0:T(8,128)} %bitcast.13), calls=%async_computation | async-start | bytes 131072 | tf_op jit(solution)/shard_map/all_to_all | solution.py:465
  66.0 0.9 %shard_map.106 = (f32[3,2,128,128]{3,2,1,0:T(8,128)}, f32[2,128,128]{2,1,0:T(8,128)}) custom-call(f32[528,128]{1,0:T(8,128)S(1)} %get-tuple-element.28.lower, f32[528,128]{1,0:T(8,128)S(1)} %get-tuple-element.29.upper, f32[528,128]{1,0:T(8,128)S(1)} %collective-permute-done.4.below_halo, f32[528,128]{1,0:T(8,128)S(1)} %collective-permute-done.5.above_halo, ...), custom_call_target="tpu_custom_call" | custom-call | bytes 1941504 | tf_op jit(solution)/shard_map/pallas_call | solution.py:369
  66.9 6.7 %all-to-all-done = f32[16,8,128]{2,1,0:T(8,128)S(1)} async-done(((f32[16,8,128]{2,1,0:T(8,128)}), f32[16,8,128]{2,1,0:T(8,128)S(1)}, u32[]{:S(2)}, u32[]{:S(2)}) %all-to-all-start) | async-done | bytes 65568 | tf_op jit(solution)/shard_map/all_to_all | solution.py:465
  73.6 0.6 bitcast_reduce_fusion
  (3 shorter events, 0.0 us)
Async XLA Ops:
  0.6 33.6 %copy-start.1 = (f32[3,2,1,128,128]{4,3,2,1,0:T(8,128)S(1)}, f32[3,2,1,128,128]{4,3,2,1,0:T(8,128)}, u32[]{:S(2)}) copy-start(f32[3,2,1,128,128]{4,3,2,1,0:T(8,128)} %param.11) | copy-start | bytes 1179652
  0.6 33.6 %copy-start.2 = (f32[2,1,128,128]{3,2,1,0:T(8,128)S(1)}, f32[2,1,128,128]{3,2,1,0:T(8,128)}, u32[]{:S(2)}) copy-start(f32[2,1,128,128]{3,2,1,0:T(8,128)} %param.13) | copy-start | bytes 393220
  2.3 31.9 %copy-start = (f32[3,2,1,128,128]{4,3,2,1,0:T(8,128)S(1)}, f32[3,2,1,128,128]{4,3,2,1,0:T(8,128)}, u32[]{:S(2)}) copy-start(f32[3,2,1,128,128]{4,3,2,1,0:T(8,128)} %param.10) | copy-start | bytes 1179652
  2.3 31.9 %collective-permute-start.1 = (f32[512,128]{1,0:T(8,128)S(1)}, f32[512,128]{1,0:T(8,128)S(1)}, u32[]{:S(2)}, u32[]{:S(2)}) collective-permute-start(f32[512,128]{1,0:T(8,128)S(1)} %get-tuple-element.23.lower), channel_id=1, source_target_pairs={{1,0},{2,1},{3,2},{4,3},{5,4},{6,5},{7,6},{8,7},{9,8},{10,9},{11,1... | collective-permute-start | bytes 786440 | tf_op jit(solution)/shard_map/ppermute | solution.py:399
  17.5 16.7 %collective-permute-start = (f32[512,128]{1,0:T(8,128)S(1)}, f32[512,128]{1,0:T(8,128)S(1)}, u32[]{:S(2)}, u32[]{:S(2)}) collective-permute-start(f32[512,128]{1,0:T(8,128)S(1)} %get-tuple-element.24.upper), channel_id=1, source_target_pairs={{0,1},{1,2},{2,3},{3,4},{4,5},{5,6},{6,7},{7,8},{8,9},{9,10},{10,1... | collective-permute-start | bytes 786440 | tf_op jit(solution)/shard_map/ppermute | solution.py:399
  21.3 11.0 %collective-permute-start.2 = (f32[96,128]{1,0:T(8,128)S(1)}, f32[96,128]{1,0:T(8,128)S(1)}, u32[]{:S(2)}, u32[]{:S(2)}) collective-permute-start(f32[96,128]{1,0:T(8,128)S(1)} %pad_maximum_fusion), channel_id=1, source_target_pairs={{0,272},{16,768},{32,304},{48,800},{64,336},{80,832},{96,368},{112... | collective-permute-start | bytes 147464 | tf_op jit(solution)/shard_map/ppermute | solution.py:384
  23.2 11.0 %collective-permute-start.3 = (f32[8,128]{1,0:T(8,128)S(1)}, f32[8,128]{1,0:T(8,128)S(1)}, u32[]{:S(2)}, u32[]{:S(2)}) collective-permute-start(f32[8,128]{1,0:T(8,128)S(1)} %get-tuple-element.27), channel_id=1, source_target_pairs={{0,1008},{16,32},{32,16},{48,64},{64,48},{80,96},{96,80},{112,128}... | collective-permute-start | bytes 12296 | tf_op jit(solution)/shard_map/ppermute | solution.py:384
  34.2 16.9 %copy-start.3 = (f32[3,2,1,128,128]{4,3,2,1,0:T(8,128)S(1)}, f32[3,2,1,128,128]{4,3,2,1,0:T(8,128)}, u32[]{:S(2)}) copy-start(f32[3,2,1,128,128]{4,3,2,1,0:T(8,128)} %param.12) | copy-start | bytes 1179652
  35.1 15.9 %collective-permute-start.5 = (f32[528,128]{1,0:T(8,128)S(1)}, f32[528,128]{1,0:T(8,128)S(1)}, u32[]{:S(2)}, u32[]{:S(2)}) collective-permute-start(f32[528,128]{1,0:T(8,128)S(1)} %get-tuple-element.28.lower), channel_id=1, source_target_pairs={{1,0},{2,1},{3,2},{4,3},{5,4},{6,5},{7,6},{8,7},{9,8},{10,9},{11,1... | collective-permute-start | bytes 811016 | tf_op jit(solution)/shard_map/ppermute | solution.py:399
  37.6 13.5 %collective-permute-start.4 = (f32[528,128]{1,0:T(8,128)S(1)}, f32[528,128]{1,0:T(8,128)S(1)}, u32[]{:S(2)}, u32[]{:S(2)}) collective-permute-start(f32[528,128]{1,0:T(8,128)S(1)} %get-tuple-element.29.upper), channel_id=1, source_target_pairs={{0,1},{1,2},{2,3},{3,4},{4,5},{5,6},{6,7},{7,8},{8,9},{9,10},{10,1... | collective-permute-start | bytes 811016 | tf_op jit(solution)/shard_map/ppermute | solution.py:399
  41.9 9.2 %collective-permute-start.6 = (f32[16,128]{1,0:T(8,128)S(1)}, f32[16,128]{1,0:T(8,128)S(1)}, u32[]{:S(2)}, u32[]{:S(2)}) collective-permute-start(f32[16,128]{1,0:T(8,128)S(1)} %get-tuple-element.31), channel_id=1, source_target_pairs={{0,1008},{16,32},{32,16},{48,64},{64,48},{80,96},{96,80},{112,128}... | collective-permute-start | bytes 24584 | tf_op jit(solution)/shard_map/ppermute | solution.py:384
  52.3 21.3 %all-to-all-start = ((f32[16,8,128]{2,1,0:T(8,128)}), f32[16,8,128]{2,1,0:T(8,128)S(1)}, u32[]{:S(2)}, u32[]{:S(2)}) async-start(f32[16,8,128]{2,1,0:T(8,128)} %bitcast.13), calls=%async_computation | async-start | bytes 131072 | tf_op jit(solution)/shard_map/all_to_all | solution.py:465

commit v8 on v7

--- a/solution.py
+++ b/solution.py
@@ -277,41 +277,58 @@
     return made
 
 
-def first_kernel(
-    facts, lower, upper, below_halo, above_halo, gifts, got, passed, outer, forcing, viscosity,
-    flow, new_lower, new_upper, col_given, col_own, kept, cols,
+def cycle_layer(layer, out, facts, state, below_halo, above_halo, forcing, viscosity, flow, rims):
+    size = facts.shape[1]
+    new = moved(
+        layer, state, below_halo, above_halo, forcing, stiffness_of(viscosity, facts, layer), rims
+    )
+    new.append(warmed(layer, state, below_halo, above_halo, flow, rims))
+    for k in range(4):
+        out[k * size : (k + 1) * size, :] = new[k]
+    for side in range(2):
+        out[4 * size + 8 * side : 4 * size + 8 * side + 8, :] = rims[side]
+
+
+def first_upper_kernel(
+    facts, lower, upper, above_halo, gifts, got, passed, outer, forcing, viscosity, flow,
+    new_upper, kept, columns, cols,
 ):
     size = facts.shape[1]
     core = core_index()
     high, low = in_order(passed[1 - core], got[ROW_MESSAGE:, :])
-    messages = (low, high)
-    for side, message in enumerate(messages):
+    for side, message in enumerate((low, high)):
         kept[KEPT * side : KEPT * (side + 1), :] = turned(
             message[:KEPT], facts[side : side + 1, :]
         )
+        kept[2 * KEPT + 16 + 8 * side : 2 * KEPT + 24 + 8 * side, :] = message[CORNERS]
+    edges = [kept[KEPT * side : KEPT * side + 8, :] for side in range(2)]
+    sides = in_order(gifts[1 - core, ROW_MESSAGE:], outer[...])
+    columns[...] = columns_of(facts, *sides, cols)
+    rims = (*edges, columns[...])
+    cycle_layer(
+        1, new_upper, facts, planes_of(lower, upper), None, above_halo, forcing, viscosity, flow,
+        rims,
+    )
+    for side in range(2):
         edge = (size - 1) * side
         for layer, state in enumerate((lower, upper)):
             for k in range(4):
                 at = 2 * KEPT + 8 * side + 4 * layer + k
                 kept[at : at + 1, :] = state[k * size + edge : k * size + edge + 1, :]
+
+
+def first_lower_kernel(
+    facts, lower, upper, below_halo, kept, columns, new_upper, forcing, viscosity, flow,
+    new_lower, col_given, col_own, cols,
+):
     edges = [kept[KEPT * side : KEPT * side + 8, :] for side in range(2)]
-    sides = in_order(gifts[1 - core, ROW_MESSAGE:], outer[...])
-    rims = (*edges, columns_of(facts, *sides, cols))
-    state = planes_of(lower, upper)
-    outs = (new_lower, new_upper)
-    for layer, out in enumerate(outs):
-        new = moved(
-            layer, state, below_halo, above_halo, forcing,
-            stiffness_of(viscosity, facts, layer), rims,
-        )
-        for k in range(3):
-            out[k * size : (k + 1) * size, :] = new[k]
-        for side in range(2):
-            out[4 * size + 8 * side : 4 * size + 8 * side + 8, :] = edges[side]
-    for layer, out in enumerate(outs):
-        out[3 * size : 4 * size, :] = warmed(layer, state, below_halo, above_halo, flow, rims)
-    low, high = edge_columns([plane_of(ref, k) for ref in outs for k in range(4)], cols)
-    corners = [message[CORNERS] for message in messages]
+    rims = (*edges, columns[...])
+    cycle_layer(
+        0, new_lower, facts, planes_of(lower, upper), below_halo, None, forcing, viscosity, flow,
+        rims,
+    )
+    low, high = edge_columns([plane_of(ref, k) for ref in (new_lower, new_upper) for k in range(4)], cols)
+    corners = [kept[2 * KEPT + 16 + 8 * side : 2 * KEPT + 24 + 8 * side, :] for side in range(2)]
     corners = jnp.where(lanes(corners[0].shape) < 4, corners[0], shifted(corners[1], 4, 1))
     col_given[:8, :], col_own[:8, :] = in_order(high, low)[::-1]
     col_given[8:, :] = corners
@@ -445,13 +462,22 @@
     )
     outer = to_outer(col_own)
     passed = of_chip(got[:ROW_MESSAGE])
-    lower, upper, col_given, col_own, kept = call(
-        first_kernel,
-        [(4 * size + 16, size)] * 2 + [(16, size)] * 2 + [(2 * KEPT + 16, size)],
-        (facts, lower, upper, *halos, gifts, got, passed, outer, forces, visc, flow),
+    below_halo, above_halo = halos
+    new_upper, kept, columns = call(
+        first_upper_kernel,
+        [(4 * size + 16, size), (2 * KEPT + 32, size), (size, size)],
+        (facts, lower, upper, above_halo, gifts, got, passed, outer, forces, visc, flow),
         (),
         (pltpu.VMEM((16, size), f32),),
     )
+    lower, col_given, col_own = call(
+        first_lower_kernel,
+        [(4 * size + 16, size), (16, size), (16, size)],
+        (facts, lower, upper, below_halo, kept, columns, new_upper, forces, visc, flow),
+        (),
+        (pltpu.VMEM((16, size), f32),),
+    )
+    upper = new_upper
     halos = radial(lower, upper)
     gifts = of_chip(col_given)
     outer = to_outer(col_own)

time: 74.6 us -> 74.7 us (level)
    pallas_call x4 -> x5, Pallas kernels: 4.6 us -> 4.65 us  [call(): pl.pallas_call(kernel, out_shape=[jax.ShapeDtypeStruct(shape, jnp.float32...]
  transfers between devices with their start and end apart: 8 -> 8, of which waited for: 2 -> 2; matrix products, arithmetic and copies ran while one was open for 0% -> 0% of each run, Pallas kernels for 1% -> 2%
where the time goes in v8:
time: 74.7 us; the launch traced here: 74.3 us
  starting transfers between devices  55.3 us (74%)
  waiting for transfers between devices  7.39 us (10%)
  blocking collectives  5.5 us (7%)
  Pallas kernels  4.65 us (6%)
  between operations  0.8 us (1%)
    ppermute x4, starting transfers between devices, along(): lax.ppermute(array, 'rad', [(i, i + by) for i in range(count) if 0 <= i +...  23.9 us
    ppermute x3, starting transfers between devices, over_tiles(): lax.ppermute(array, 'cap', [(i, to(i) % count) for i in range(count)])  17.7 us
    all_to_all x1, starting transfers between devices, shards(): pieces = lax.all_to_all(partial, 'rad', 0, 0, tiled=True)  13.7 us
    all_to_all x1, waiting for transfers between devices, shards(): pieces = lax.all_to_all(partial, 'rad', 0, 0, tiled=True)  6.71 us
    all_gather x3, blocking collectives, of_chip(): return lax.all_gather(array, 'cap', axis_index_groups=pairs)  5.5 us
    pallas_call x5, Pallas kernels, call(): pl.pallas_call(kernel, out_shape=[jax.ShapeDtypeStruct(shape, jnp.float32...  4.65 us
  transfers between devices with their start and end apart: 8, of which 2 were waited for; matrix products, arithmetic and copies ran while one was open for 0% of the time, Pallas kernels for 2%

profile of v8, /device:TPU:2, one launch (start us, length us, event | category | flops | bytes accessed | tf_op | source)
XLA Modules:
  0.0 74.3 jit_solution(14561538967565879549)
XLA Ops:
  0.6 0.0 copy-start.1
  0.6 0.0 copy-start.2
  0.7 1.6 %shard_map.103 = (f32[512,128]{1,0:T(8,128)S(1)}, f32[512,128]{1,0:T(8,128)S(1)}, f32[48,128]{1,0:T(8,128)S(1)}, f32[56,128]{1,0:T(8,128)S(1)}, f32[8,128]{1,0:T(8,128)S(1)}, /*index=5*/f32[16,128]{1,0:T(8,128)S(1)}) custom-call(f32[3,2,128,128]{3,2,1,0:T(8,128)} %bitcast.40, f32[2,128,128]{2,1,0:T(8,128)} %bitcast.42, s32[2]{0:T(128)} %mask.1, ...), custom_call_target="tpu_custom_call" | custom-call | bytes 1442824 | tf_op jit(solution)/shard_map/pallas_call | solution.py:386
  2.3 0.0 copy-start
  2.3 15.2 %collective-permute-start.1 = (f32[512,128]{1,0:T(8,128)S(1)}, f32[512,128]{1,0:T(8,128)S(1)}, u32[]{:S(2)}, u32[]{:S(2)}) collective-permute-start(f32[512,128]{1,0:T(8,128)S(1)} %get-tuple-element.24.lower), channel_id=1, source_target_pairs={{1,0},{2,1},{3,2},{4,3},{5,4},{6,5},{7,6},{8,7},{9,8},{10,9},{11,1... | collective-permute-start | bytes 786440 | tf_op jit(solution)/shard_map/ppermute | solution.py:416
  17.5 1.9 %collective-permute-start = (f32[512,128]{1,0:T(8,128)S(1)}, f32[512,128]{1,0:T(8,128)S(1)}, u32[]{:S(2)}, u32[]{:S(2)}) collective-permute-start(f32[512,128]{1,0:T(8,128)S(1)} %get-tuple-element.25.upper), channel_id=1, source_target_pairs={{0,1},{1,2},{2,3},{3,4},{4,5},{5,6},{6,7},{7,8},{8,9},{9,10},{10,1... | collective-permute-start | bytes 786440 | tf_op jit(solution)/shard_map/ppermute | solution.py:416
  19.4 1.8 %all-gather = f32[112,128]{1,0:T(8,128)S(1)} all-gather(f32[56,128]{1,0:T(8,128)S(1)} %get-tuple-element.26), channel_id=2, replica_groups={{0,16},{32,48},{64,80},{96,112},{128,144},{160,176},{192,208},{224,240}..., dimensions={0}, use_global_device_ids=true | all-gather | bytes 86016 | tf_op jit(solution)/shard_map/all_gather | solution.py:407
  21.3 1.9 %collective-permute-start.2 = (f32[96,128]{1,0:T(8,128)S(1)}, f32[96,128]{1,0:T(8,128)S(1)}, u32[]{:S(2)}, u32[]{:S(2)}) collective-permute-start(f32[96,128]{1,0:T(8,128)S(1)} %pad_maximum_fusion), channel_id=1, source_target_pairs={{0,272},{16,768},{32,304},{48,800},{64,336},{80,832},{96,368},{112... | collective-permute-start | bytes 147464 | tf_op jit(solution)/shard_map/ppermute | solution.py:401
  23.2 9.1 %collective-permute-start.3 = (f32[8,128]{1,0:T(8,128)S(1)}, f32[8,128]{1,0:T(8,128)S(1)}, u32[]{:S(2)}, u32[]{:S(2)}) collective-permute-start(f32[8,128]{1,0:T(8,128)S(1)} %get-tuple-element.28), channel_id=1, source_target_pairs={{0,1008},{16,32},{32,16},{48,64},{64,48},{80,96},{96,80},{112,128}... | collective-permute-start | bytes 12296 | tf_op jit(solution)/shard_map/ppermute | solution.py:401
  32.3 0.0 collective-permute-done.2.got
  32.3 1.8 %all-gather.1 = f32[96,128]{1,0:T(8,128)S(1)} all-gather(f32[48,128]{1,0:T(8,128)S(1)} %slice.12), channel_id=3, replica_groups={{0,16},{32,48},{64,80},{96,112},{128,144},{160,176},{192,208},{224,240}..., dimensions={0}, use_global_device_ids=true | all-gather | bytes 73728 | tf_op jit(solution)/shard_map/all_gather | solution.py:407
  34.2 0.0 collective-permute-done.3.outer
  34.2 0.0 collective-permute-done.1.above_halo
  34.2 0.0 copy-done.1
  34.2 0.0 copy-done.2
  34.2 0.0 copy-done
  34.2 0.4 shard_map.104
  34.6 0.0 collective-permute-done.below_halo
  34.7 0.0 copy-start.3
  34.7 0.5 shard_map.105
  35.2 2.4 %collective-permute-start.5 = (f32[528,128]{1,0:T(8,128)S(1)}, f32[528,128]{1,0:T(8,128)S(1)}, u32[]{:S(2)}, u32[]{:S(2)}) collective-permute-start(f32[528,128]{1,0:T(8,128)S(1)} %get-tuple-element.32.lower), channel_id=1, source_target_pairs={{1,0},{2,1},{3,2},{4,3},{5,4},{6,5},{7,6},{8,7},{9,8},{10,9},{11,1... | collective-permute-start | bytes 811016 | tf_op jit(solution)/shard_map/ppermute | solution.py:416
  37.6 4.3 %collective-permute-start.4 = (f32[528,128]{1,0:T(8,128)S(1)}, f32[528,128]{1,0:T(8,128)S(1)}, u32[]{:S(2)}, u32[]{:S(2)}) collective-permute-start(f32[528,128]{1,0:T(8,128)S(1)} %get-tuple-element.31.new_upper.upper), channel_id=1, source_target_pairs={{0,1},{1,2},{2,3},{3,4},{4,5},{5,6},{6,7},{7,8},{8,9},{9,10},{10,1... | collective-permute-start | bytes 811016 | tf_op jit(solution)/shard_map/ppermute | solution.py:416
  41.9 6.7 %collective-permute-start.6 = (f32[16,128]{1,0:T(8,128)S(1)}, f32[16,128]{1,0:T(8,128)S(1)}, u32[]{:S(2)}, u32[]{:S(2)}) collective-permute-start(f32[16,128]{1,0:T(8,128)S(1)} %get-tuple-element.34), channel_id=1, source_target_pairs={{0,1008},{16,32},{32,16},{48,64},{64,48},{80,96},{96,80},{112,128}... | collective-permute-start | bytes 24584 | tf_op jit(solution)/shard_map/ppermute | solution.py:401
  48.6 1.8 %all-gather.2 = f32[32,128]{1,0:T(8,128)S(1)} all-gather(f32[16,128]{1,0:T(8,128)S(1)} %get-tuple-element.33), channel_id=4, replica_groups={{0,16},{32,48},{64,80},{96,112},{128,144},{160,176},{192,208},{224,240}..., dimensions={0}, use_global_device_ids=true | all-gather | bytes 24576 | tf_op jit(solution)/shard_map/all_gather | solution.py:407
  50.5 0.7 collective-permute-done.6.outer
  51.1 0.0 collective-permute-done.5.above_halo
  51.1 0.0 collective-permute-done.4.below_halo
  51.1 0.0 copy-done.3
  51.1 1.2 %shard_map.106 = (f32[3,2,128,128]{3,2,1,0:T(8,128)S(1)}, f32[128,128]{1,0:T(8,128)}, f32[16,128]{1,0:T(8,128)S(1)}, f32[128,128]{1,0:T(8,128)S(1)}) custom-call(f32[16,128]{1,0:T(8,128)S(1)} %get-tuple-element.23.facts, f32[528,128]{1,0:T(8,128)S(1)} %get-tuple-element.32.lower, f32[528,128]{1,0:T(8,128)S(1)} %get-tuple-element.31.new_upper.upper, ...), custom_call_target="tpu_custom_call" | custom-call | bytes 2088960 | tf_op jit(solution)/shard_map/pallas_call | solution.py:386
  52.3 13.7 %all-to-all-start = ((f32[16,8,128]{2,1,0:T(8,128)}), f32[16,8,128]{2,1,0:T(8,128)S(1)}, u32[]{:S(2)}, u32[]{:S(2)}) async-start(f32[16,8,128]{2,1,0:T(8,128)} %bitcast.13), calls=%async_computation | async-start | bytes 131072 | tf_op jit(solution)/shard_map/all_to_all | solution.py:491
  66.1 0.9 %shard_map.107 = (f32[3,2,128,128]{3,2,1,0:T(8,128)}, f32[2,128,128]{2,1,0:T(8,128)}) custom-call(f32[528,128]{1,0:T(8,128)S(1)} %get-tuple-element.32.lower, f32[528,128]{1,0:T(8,128)S(1)} %get-tuple-element.31.new_upper.upper, f32[528,128]{1,0:T(8,128)S(1)} %collective-permute-done.4.below_halo, f32[528,128]{1,0:T(8,128)S(1)} %collective-permute-done.5.above_halo, ...), custom_call_target="tpu_custom_call" | custom-call | bytes 1941504 | tf_op jit(solution)/shard_map/pallas_call | solution.py:386
  67.0 6.7 %all-to-all-done = f32[16,8,128]{2,1,0:T(8,128)S(1)} async-done(((f32[16,8,128]{2,1,0:T(8,128)}), f32[16,8,128]{2,1,0:T(8,128)S(1)}, u32[]{:S(2)}, u32[]{:S(2)}) %all-to-all-start) | async-done | bytes 65568 | tf_op jit(solution)/shard_map/all_to_all | solution.py:491
  73.7 0.6 bitcast_reduce_fusion
  (3 shorter events, 0.0 us)
Async XLA Ops:
  0.6 33.6 %copy-start.1 = (f32[3,2,1,128,128]{4,3,2,1,0:T(8,128)S(1)}, f32[3,2,1,128,128]{4,3,2,1,0:T(8,128)}, u32[]{:S(2)}) copy-start(f32[3,2,1,128,128]{4,3,2,1,0:T(8,128)} %param.11) | copy-start | bytes 1179652
  0.6 33.5 %copy-start.2 = (f32[2,1,128,128]{3,2,1,0:T(8,128)S(1)}, f32[2,1,128,128]{3,2,1,0:T(8,128)}, u32[]{:S(2)}) copy-start(f32[2,1,128,128]{3,2,1,0:T(8,128)} %param.13) | copy-start | bytes 393220
  2.3 31.9 %copy-start = (f32[3,2,1,128,128]{4,3,2,1,0:T(8,128)S(1)}, f32[3,2,1,128,128]{4,3,2,1,0:T(8,128)}, u32[]{:S(2)}) copy-start(f32[3,2,1,128,128]{4,3,2,1,0:T(8,128)} %param.10) | copy-start | bytes 1179652
  2.3 31.9 %collective-permute-start.1 = (f32[512,128]{1,0:T(8,128)S(1)}, f32[512,128]{1,0:T(8,128)S(1)}, u32[]{:S(2)}, u32[]{:S(2)}) collective-permute-start(f32[512,128]{1,0:T(8,128)S(1)} %get-tuple-element.24.lower), channel_id=1, source_target_pairs={{1,0},{2,1},{3,2},{4,3},{5,4},{6,5},{7,6},{8,7},{9,8},{10,9},{11,1... | collective-permute-start | bytes 786440 | tf_op jit(solution)/shard_map/ppermute | solution.py:416
  17.5 17.1 %collective-permute-start = (f32[512,128]{1,0:T(8,128)S(1)}, f32[512,128]{1,0:T(8,128)S(1)}, u32[]{:S(2)}, u32[]{:S(2)}) collective-permute-start(f32[512,128]{1,0:T(8,128)S(1)} %get-tuple-element.25.upper), channel_id=1, source_target_pairs={{0,1},{1,2},{2,3},{3,4},{4,5},{5,6},{6,7},{7,8},{8,9},{9,10},{10,1... | collective-permute-start | bytes 786440 | tf_op jit(solution)/shard_map/ppermute | solution.py:416
  21.3 11.0 %collective-permute-start.2 = (f32[96,128]{1,0:T(8,128)S(1)}, f32[96,128]{1,0:T(8,128)S(1)}, u32[]{:S(2)}, u32[]{:S(2)}) collective-permute-start(f32[96,128]{1,0:T(8,128)S(1)} %pad_maximum_fusion), channel_id=1, source_target_pairs={{0,272},{16,768},{32,304},{48,800},{64,336},{80,832},{96,368},{112... | collective-permute-start | bytes 147464 | tf_op jit(solution)/shard_map/ppermute | solution.py:401
  23.2 11.0 %collective-permute-start.3 = (f32[8,128]{1,0:T(8,128)S(1)}, f32[8,128]{1,0:T(8,128)S(1)}, u32[]{:S(2)}, u32[]{:S(2)}) collective-permute-start(f32[8,128]{1,0:T(8,128)S(1)} %get-tuple-element.28), channel_id=1, source_target_pairs={{0,1008},{16,32},{32,16},{48,64},{64,48},{80,96},{96,80},{112,128}... | collective-permute-start | bytes 12296 | tf_op jit(solution)/shard_map/ppermute | solution.py:401
  34.7 16.5 %copy-start.3 = (f32[3,2,1,128,128]{4,3,2,1,0:T(8,128)S(1)}, f32[3,2,1,128,128]{4,3,2,1,0:T(8,128)}, u32[]{:S(2)}) copy-start(f32[3,2,1,128,128]{4,3,2,1,0:T(8,128)} %param.12) | copy-start | bytes 1179652
  35.2 15.9 %collective-permute-start.5 = (f32[528,128]{1,0:T(8,128)S(1)}, f32[528,128]{1,0:T(8,128)S(1)}, u32[]{:S(2)}, u32[]{:S(2)}) collective-permute-start(f32[528,128]{1,0:T(8,128)S(1)} %get-tuple-element.32.lower), channel_id=1, source_target_pairs={{1,0},{2,1},{3,2},{4,3},{5,4},{6,5},{7,6},{8,7},{9,8},{10,9},{11,1... | collective-permute-start | bytes 811016 | tf_op jit(solution)/shard_map/ppermute | solution.py:416
  37.6 13.5 %collective-permute-start.4 = (f32[528,128]{1,0:T(8,128)S(1)}, f32[528,128]{1,0:T(8,128)S(1)}, u32[]{:S(2)}, u32[]{:S(2)}) collective-permute-start(f32[528,128]{1,0:T(8,128)S(1)} %get-tuple-element.31.new_upper.upper), channel_id=1, source_target_pairs={{0,1},{1,2},{2,3},{3,4},{4,5},{5,6},{6,7},{7,8},{8,9},{9,10},{10,1... | collective-permute-start | bytes 811016 | tf_op jit(solution)/shard_map/ppermute | solution.py:416
  41.9 9.2 %collective-permute-start.6 = (f32[16,128]{1,0:T(8,128)S(1)}, f32[16,128]{1,0:T(8,128)S(1)}, u32[]{:S(2)}, u32[]{:S(2)}) collective-permute-start(f32[16,128]{1,0:T(8,128)S(1)} %get-tuple-element.34), channel_id=1, source_target_pairs={{0,1008},{16,32},{32,16},{48,64},{64,48},{80,96},{96,80},{112,128}... | collective-permute-start | bytes 24584 | tf_op jit(solution)/shard_map/ppermute | solution.py:401
  52.3 21.3 %all-to-all-start = ((f32[16,8,128]{2,1,0:T(8,128)}), f32[16,8,128]{2,1,0:T(8,128)S(1)}, u32[]{:S(2)}, u32[]{:S(2)}) async-start(f32[16,8,128]{2,1,0:T(8,128)} %bitcast.13), calls=%async_computation | async-start | bytes 131072 | tf_op jit(solution)/shard_map/all_to_all | solution.py:491

commit v9 on v7

--- a/solution.py
+++ b/solution.py
@@ -70,32 +70,32 @@
     size = lower.shape[1]
     row_low, row_high = messages.at[0], messages.at[1]
     core = core_index()
-    copies = [
+    planes_in = [
+        pltpu.make_async_copy(
+            velocity.at[k, layer] if k < 3 else heat.at[layer],
+            out.at[pl.ds(k * size, size)],
+            sems.at[2 + 4 * layer + k],
+        )
+        for layer, out in enumerate((lower, upper))
+        for k in range(4)
+    ]
+    rims_in = [
         pltpu.make_async_copy(mask, mask_here, sems.at[0]),
         pltpu.make_async_copy(flips, flips_here, sems.at[1]),
     ]
-    for layer, out in enumerate((lower, upper)):
-        for k in range(4):
-            copies.append(
-                pltpu.make_async_copy(
-                    velocity.at[k, layer] if k < 3 else heat.at[layer],
-                    out.at[pl.ds(k * size, size)],
-                    sems.at[2 + 4 * layer + k],
-                )
-            )
     for side, start in enumerate((0, size - 8)):
         for n, (source, target) in enumerate(
             ((forcing, forcing_rims), (flow, flow_rims), (viscosity, viscosity_rims))
         ):
             here = (slice(None),) * (len(source.shape) - 2) + (pl.ds(start, 8),)
-            copies.append(
+            rims_in.append(
                 pltpu.make_async_copy(
                     source.at[here], target.at[side], rim_sem.at[3 * side + n]
                 )
             )
-    for copy in copies:
+    for copy in rims_in + planes_in:
         copy.start()
-    for copy in copies:
+    for copy in rims_in:
         copy.wait()
 
     width = facts.shape[1]
@@ -115,6 +115,24 @@
         scale = 1.0 + 4.0 * mask_here[layer].astype(jnp.float32)
         facts[4 + layer : 5 + layer, :] = jnp.full((1, width), scale, jnp.float32)
 
+    for side, (out, rim) in enumerate(((row_low, 0), (row_high, 7))):
+        for layer in range(2):
+            scale = facts[4 + layer : 5 + layer, :]
+            for k in range(4):
+                at = 4 * layer + k
+                if k < 3:
+                    stiff = viscosity_rims[side, layer, rim : rim + 1, :] * scale
+                    force = forcing_rims[side, k, layer, rim : rim + 1, :]
+                    carry = jnp.zeros((1, width), jnp.float32)
+                else:
+                    stiff = flow_rims[side, 0, layer, rim : rim + 1, :]
+                    force = flow_rims[side, 1, layer, rim : rim + 1, :]
+                    carry = flow_rims[side, 2, layer, rim : rim + 1, :]
+                out[16 + at : 17 + at, :] = stiff
+                out[24 + at : 25 + at, :] = force
+                out[32 + at : 33 + at, :] = carry
+    for copy in planes_in:
+        copy.wait()
     planes = [plane_of(ref, k) for ref in (lower, upper) for k in range(4)]
     for side, (out, edge, second, rim) in enumerate(
         ((row_low, 0, 1, 0), (row_high, size - 1, size - 2, 7))
@@ -126,17 +144,6 @@
                 plane = planes[at]
                 out[at : at + 1, :] = plane[edge : edge + 1, :]
                 out[8 + at : 9 + at, :] = plane[second : second + 1, :]
-                if k < 3:
-                    stiff = viscosity_rims[side, layer, rim : rim + 1, :] * scale
-                    force = forcing_rims[side, k, layer, rim : rim + 1, :]
-                    carry = jnp.zeros((1, width), jnp.float32)
-                else:
-                    stiff = flow_rims[side, 0, layer, rim : rim + 1, :]
-                    force = flow_rims[side, 1, layer, rim : rim + 1, :]
-                    carry = flow_rims[side, 2, layer, rim : rim + 1, :]
-                out[16 + at : 17 + at, :] = stiff
-                out[24 + at : 25 + at, :] = force
-                out[32 + at : 33 + at, :] = carry
     first, last = row_low[EDGE, :], row_high[EDGE, :]
     lane = lanes(first.shape)
     corners = jnp.where(

time: 74.6 us -> 74.6 us (level)
  no operation moved by 1% of the time
where the time goes in v9:
time: 74.6 us; the launch traced here: 74.2 us
  starting transfers between devices  55.3 us (74%)
  waiting for transfers between devices  7.39 us (10%)
  blocking collectives  5.5 us (7%)
  Pallas kernels  4.59 us (6%)
  between operations  0.8 us (1%)
    ppermute x4, starting transfers between devices, along(): lax.ppermute(array, 'rad', [(i, i + by) for i in range(count) if 0 <= i +...  23.9 us
    ppermute x3, starting transfers between devices, over_tiles(): lax.ppermute(array, 'cap', [(i, to(i) % count) for i in range(count)])  17.7 us
    all_to_all x1, starting transfers between devices, shards(): pieces = lax.all_to_all(partial, 'rad', 0, 0, tiled=True)  13.7 us
    all_to_all x1, waiting for transfers between devices, shards(): pieces = lax.all_to_all(partial, 'rad', 0, 0, tiled=True)  6.71 us
    all_gather x3, blocking collectives, of_chip(): return lax.all_gather(array, 'cap', axis_index_groups=pairs)  5.5 us
    pallas_call x4, Pallas kernels, call(): pl.pallas_call(kernel, out_shape=[jax.ShapeDtypeStruct(shape, jnp.float32...  4.59 us
  transfers between devices with their start and end apart: 8, of which 2 were waited for; matrix products, arithmetic and copies ran while one was open for 0% of the time, Pallas kernels for 1%

profile of v9, /device:TPU:2, one launch (start us, length us, event | category | flops | bytes accessed | tf_op | source)
XLA Modules:
  0.0 74.2 jit_solution(2536285157280375891)
XLA Ops:
  0.6 0.0 copy-start.1
  0.6 0.0 copy-start.2
  0.7 1.6 %shard_map.103 = (f32[512,128]{1,0:T(8,128)S(1)}, f32[512,128]{1,0:T(8,128)S(1)}, f32[48,128]{1,0:T(8,128)S(1)}, f32[56,128]{1,0:T(8,128)S(1)}, f32[8,128]{1,0:T(8,128)S(1)}, /*index=5*/f32[16,128]{1,0:T(8,128)S(1)}) custom-call(f32[3,2,128,128]{3,2,1,0:T(8,128)} %bitcast.37, f32[2,128,128]{2,1,0:T(8,128)} %bitcast.39, s32[2]{0:T(128)} %mask.1, ...), custom_call_target="tpu_custom_call" | custom-call | bytes 1442824 | tf_op jit(solution)/shard_map/pallas_call | solution.py:376
  2.3 0.0 copy-start
  2.3 15.2 %collective-permute-start.1 = (f32[512,128]{1,0:T(8,128)S(1)}, f32[512,128]{1,0:T(8,128)S(1)}, u32[]{:S(2)}, u32[]{:S(2)}) collective-permute-start(f32[512,128]{1,0:T(8,128)S(1)} %get-tuple-element.23.lower), channel_id=1, source_target_pairs={{1,0},{2,1},{3,2},{4,3},{5,4},{6,5},{7,6},{8,7},{9,8},{10,9},{11,1... | collective-permute-start | bytes 786440 | tf_op jit(solution)/shard_map/ppermute | solution.py:406
  17.5 1.9 %collective-permute-start = (f32[512,128]{1,0:T(8,128)S(1)}, f32[512,128]{1,0:T(8,128)S(1)}, u32[]{:S(2)}, u32[]{:S(2)}) collective-permute-start(f32[512,128]{1,0:T(8,128)S(1)} %get-tuple-element.24.upper), channel_id=1, source_target_pairs={{0,1},{1,2},{2,3},{3,4},{4,5},{5,6},{6,7},{7,8},{8,9},{9,10},{10,1... | collective-permute-start | bytes 786440 | tf_op jit(solution)/shard_map/ppermute | solution.py:406
  19.4 1.8 %all-gather = f32[112,128]{1,0:T(8,128)S(1)} all-gather(f32[56,128]{1,0:T(8,128)S(1)} %get-tuple-element.25), channel_id=2, replica_groups={{0,16},{32,48},{64,80},{96,112},{128,144},{160,176},{192,208},{224,240}..., dimensions={0}, use_global_device_ids=true | all-gather | bytes 86016 | tf_op jit(solution)/shard_map/all_gather | solution.py:397
  21.3 1.9 %collective-permute-start.2 = (f32[96,128]{1,0:T(8,128)S(1)}, f32[96,128]{1,0:T(8,128)S(1)}, u32[]{:S(2)}, u32[]{:S(2)}) collective-permute-start(f32[96,128]{1,0:T(8,128)S(1)} %pad_maximum_fusion), channel_id=1, source_target_pairs={{0,272},{16,768},{32,304},{48,800},{64,336},{80,832},{96,368},{112... | collective-permute-start | bytes 147464 | tf_op jit(solution)/shard_map/ppermute | solution.py:391
  23.2 9.1 %collective-permute-start.3 = (f32[8,128]{1,0:T(8,128)S(1)}, f32[8,128]{1,0:T(8,128)S(1)}, u32[]{:S(2)}, u32[]{:S(2)}) collective-permute-start(f32[8,128]{1,0:T(8,128)S(1)} %get-tuple-element.27), channel_id=1, source_target_pairs={{0,1008},{16,32},{32,16},{48,64},{64,48},{80,96},{96,80},{112,128}... | collective-permute-start | bytes 12296 | tf_op jit(solution)/shard_map/ppermute | solution.py:391
  32.3 0.0 collective-permute-done.2.got
  32.3 1.8 %all-gather.1 = f32[96,128]{1,0:T(8,128)S(1)} all-gather(f32[48,128]{1,0:T(8,128)S(1)} %slice.12), channel_id=3, replica_groups={{0,16},{32,48},{64,80},{96,112},{128,144},{160,176},{192,208},{224,240}..., dimensions={0}, use_global_device_ids=true | all-gather | bytes 73728 | tf_op jit(solution)/shard_map/all_gather | solution.py:397
  34.2 0.0 collective-permute-done.3.outer
  34.2 0.0 collective-permute-done.1.above_halo
  34.2 0.0 collective-permute-done.below_halo
  34.2 0.0 copy-done.1
  34.2 0.0 copy-done.2
  34.2 0.0 copy-done
  34.2 0.0 copy-start.3
  34.2 0.9 %shard_map.104 = (f32[528,128]{1,0:T(8,128)S(1)}, f32[528,128]{1,0:T(8,128)S(1)}, f32[16,128]{1,0:T(8,128)S(1)}, f32[16,128]{1,0:T(8,128)S(1)}, f32[96,128]{1,0:T(8,128)S(1)}) custom-call(f32[16,128]{1,0:T(8,128)S(1)} %get-tuple-element.22.facts, f32[512,128]{1,0:T(8,128)S(1)} %get-tuple-element.23.lower, f32[512,128]{1,0:T(8,128)S(1)} %get-tuple-element.24.upper, ...), custom_call_target="tpu_custom_call" | custom-call | bytes 2134016 | tf_op jit(solution)/shard_map/pallas_call | solution.py:376
  35.1 2.5 %collective-permute-start.5 = (f32[528,128]{1,0:T(8,128)S(1)}, f32[528,128]{1,0:T(8,128)S(1)}, u32[]{:S(2)}, u32[]{:S(2)}) collective-permute-start(f32[528,128]{1,0:T(8,128)S(1)} %get-tuple-element.28.lower), channel_id=1, source_target_pairs={{1,0},{2,1},{3,2},{4,3},{5,4},{6,5},{7,6},{8,7},{9,8},{10,9},{11,1... | collective-permute-start | bytes 811016 | tf_op jit(solution)/shard_map/ppermute | solution.py:406
  37.6 4.3 %collective-permute-start.4 = (f32[528,128]{1,0:T(8,128)S(1)}, f32[528,128]{1,0:T(8,128)S(1)}, u32[]{:S(2)}, u32[]{:S(2)}) collective-permute-start(f32[528,128]{1,0:T(8,128)S(1)} %get-tuple-element.29.upper), channel_id=1, source_target_pairs={{0,1},{1,2},{2,3},{3,4},{4,5},{5,6},{6,7},{7,8},{8,9},{9,10},{10,1... | collective-permute-start | bytes 811016 | tf_op jit(solution)/shard_map/ppermute | solution.py:406
  41.9 6.7 %collective-permute-start.6 = (f32[16,128]{1,0:T(8,128)S(1)}, f32[16,128]{1,0:T(8,128)S(1)}, u32[]{:S(2)}, u32[]{:S(2)}) collective-permute-start(f32[16,128]{1,0:T(8,128)S(1)} %get-tuple-element.31), channel_id=1, source_target_pairs={{0,1008},{16,32},{32,16},{48,64},{64,48},{80,96},{96,80},{112,128}... | collective-permute-start | bytes 24584 | tf_op jit(solution)/shard_map/ppermute | solution.py:391
  48.6 1.8 %all-gather.2 = f32[32,128]{1,0:T(8,128)S(1)} all-gather(f32[16,128]{1,0:T(8,128)S(1)} %get-tuple-element.30), channel_id=4, replica_groups={{0,16},{32,48},{64,80},{96,112},{128,144},{160,176},{192,208},{224,240}..., dimensions={0}, use_global_device_ids=true | all-gather | bytes 24576 | tf_op jit(solution)/shard_map/all_gather | solution.py:397
  50.4 0.7 collective-permute-done.6.outer
  51.1 0.0 collective-permute-done.5.above_halo
  51.1 0.0 collective-permute-done.4.below_halo
  51.1 0.0 copy-done.3
  51.1 1.2 %shard_map.105 = (f32[3,2,128,128]{3,2,1,0:T(8,128)S(1)}, f32[128,128]{1,0:T(8,128)}, f32[16,128]{1,0:T(8,128)S(1)}, f32[128,128]{1,0:T(8,128)S(1)}) custom-call(f32[16,128]{1,0:T(8,128)S(1)} %get-tuple-element.22.facts, f32[528,128]{1,0:T(8,128)S(1)} %get-tuple-element.28.lower, f32[528,128]{1,0:T(8,128)S(1)} %get-tuple-element.29.upper, ...), custom_call_target="tpu_custom_call" | custom-call | bytes 2080768 | tf_op jit(solution)/shard_map/pallas_call | solution.py:376
  52.3 13.7 %all-to-all-start = ((f32[16,8,128]{2,1,0:T(8,128)}), f32[16,8,128]{2,1,0:T(8,128)S(1)}, u32[]{:S(2)}, u32[]{:S(2)}) async-start(f32[16,8,128]{2,1,0:T(8,128)} %bitcast.13), calls=%async_computation | async-start | bytes 131072 | tf_op jit(solution)/shard_map/all_to_all | solution.py:472
  66.0 0.9 %shard_map.106 = (f32[3,2,128,128]{3,2,1,0:T(8,128)}, f32[2,128,128]{2,1,0:T(8,128)}) custom-call(f32[528,128]{1,0:T(8,128)S(1)} %get-tuple-element.28.lower, f32[528,128]{1,0:T(8,128)S(1)} %get-tuple-element.29.upper, f32[528,128]{1,0:T(8,128)S(1)} %collective-permute-done.4.below_halo, f32[528,128]{1,0:T(8,128)S(1)} %collective-permute-done.5.above_halo, ...), custom_call_target="tpu_custom_call" | custom-call | bytes 1941504 | tf_op jit(solution)/shard_map/pallas_call | solution.py:376
  66.9 6.7 %all-to-all-done = f32[16,8,128]{2,1,0:T(8,128)S(1)} async-done(((f32[16,8,128]{2,1,0:T(8,128)}), f32[16,8,128]{2,1,0:T(8,128)S(1)}, u32[]{:S(2)}, u32[]{:S(2)}) %all-to-all-start) | async-done | bytes 65568 | tf_op jit(solution)/shard_map/all_to_all | solution.py:472
  73.6 0.6 bitcast_reduce_fusion
  (3 shorter events, 0.0 us)
Async XLA Ops:
  0.6 33.6 %copy-start.1 = (f32[3,2,1,128,128]{4,3,2,1,0:T(8,128)S(1)}, f32[3,2,1,128,128]{4,3,2,1,0:T(8,128)}, u32[]{:S(2)}) copy-start(f32[3,2,1,128,128]{4,3,2,1,0:T(8,128)} %param.11) | copy-start | bytes 1179652
  0.6 33.6 %copy-start.2 = (f32[2,1,128,128]{3,2,1,0:T(8,128)S(1)}, f32[2,1,128,128]{3,2,1,0:T(8,128)}, u32[]{:S(2)}) copy-start(f32[2,1,128,128]{3,2,1,0:T(8,128)} %param.13) | copy-start | bytes 393220
  2.3 31.9 %copy-start = (f32[3,2,1,128,128]{4,3,2,1,0:T(8,128)S(1)}, f32[3,2,1,128,128]{4,3,2,1,0:T(8,128)}, u32[]{:S(2)}) copy-start(f32[3,2,1,128,128]{4,3,2,1,0:T(8,128)} %param.10) | copy-start | bytes 1179652
  2.3 31.9 %collective-permute-start.1 = (f32[512,128]{1,0:T(8,128)S(1)}, f32[512,128]{1,0:T(8,128)S(1)}, u32[]{:S(2)}, u32[]{:S(2)}) collective-permute-start(f32[512,128]{1,0:T(8,128)S(1)} %get-tuple-element.23.lower), channel_id=1, source_target_pairs={{1,0},{2,1},{3,2},{4,3},{5,4},{6,5},{7,6},{8,7},{9,8},{10,9},{11,1... | collective-permute-start | bytes 786440 | tf_op jit(solution)/shard_map/ppermute | solution.py:406
  17.5 16.7 %collective-permute-start = (f32[512,128]{1,0:T(8,128)S(1)}, f32[512,128]{1,0:T(8,128)S(1)}, u32[]{:S(2)}, u32[]{:S(2)}) collective-permute-start(f32[512,128]{1,0:T(8,128)S(1)} %get-tuple-element.24.upper), channel_id=1, source_target_pairs={{0,1},{1,2},{2,3},{3,4},{4,5},{5,6},{6,7},{7,8},{8,9},{9,10},{10,1... | collective-permute-start | bytes 786440 | tf_op jit(solution)/shard_map/ppermute | solution.py:406
  21.3 11.0 %collective-permute-start.2 = (f32[96,128]{1,0:T(8,128)S(1)}, f32[96,128]{1,0:T(8,128)S(1)}, u32[]{:S(2)}, u32[]{:S(2)}) collective-permute-start(f32[96,128]{1,0:T(8,128)S(1)} %pad_maximum_fusion), channel_id=1, source_target_pairs={{0,272},{16,768},{32,304},{48,800},{64,336},{80,832},{96,368},{112... | collective-permute-start | bytes 147464 | tf_op jit(solution)/shard_map/ppermute | solution.py:391
  23.2 11.0 %collective-permute-start.3 = (f32[8,128]{1,0:T(8,128)S(1)}, f32[8,128]{1,0:T(8,128)S(1)}, u32[]{:S(2)}, u32[]{:S(2)}) collective-permute-start(f32[8,128]{1,0:T(8,128)S(1)} %get-tuple-element.27), channel_id=1, source_target_pairs={{0,1008},{16,32},{32,16},{48,64},{64,48},{80,96},{96,80},{112,128}... | collective-permute-start | bytes 12296 | tf_op jit(solution)/shard_map/ppermute | solution.py:391
  34.2 16.9 %copy-start.3 = (f32[3,2,1,128,128]{4,3,2,1,0:T(8,128)S(1)}, f32[3,2,1,128,128]{4,3,2,1,0:T(8,128)}, u32[]{:S(2)}) copy-start(f32[3,2,1,128,128]{4,3,2,1,0:T(8,128)} %param.12) | copy-start | bytes 1179652
  35.1 15.9 %collective-permute-start.5 = (f32[528,128]{1,0:T(8,128)S(1)}, f32[528,128]{1,0:T(8,128)S(1)}, u32[]{:S(2)}, u32[]{:S(2)}) collective-permute-start(f32[528,128]{1,0:T(8,128)S(1)} %get-tuple-element.28.lower), channel_id=1, source_target_pairs={{1,0},{2,1},{3,2},{4,3},{5,4},{6,5},{7,6},{8,7},{9,8},{10,9},{11,1... | collective-permute-start | bytes 811016 | tf_op jit(solution)/shard_map/ppermute | solution.py:406
  37.6 13.5 %collective-permute-start.4 = (f32[528,128]{1,0:T(8,128)S(1)}, f32[528,128]{1,0:T(8,128)S(1)}, u32[]{:S(2)}, u32[]{:S(2)}) collective-permute-start(f32[528,128]{1,0:T(8,128)S(1)} %get-tuple-element.29.upper), channel_id=1, source_target_pairs={{0,1},{1,2},{2,3},{3,4},{4,5},{5,6},{6,7},{7,8},{8,9},{9,10},{10,1... | collective-permute-start | bytes 811016 | tf_op jit(solution)/shard_map/ppermute | solution.py:406
  41.9 9.2 %collective-permute-start.6 = (f32[16,128]{1,0:T(8,128)S(1)}, f32[16,128]{1,0:T(8,128)S(1)}, u32[]{:S(2)}, u32[]{:S(2)}) collective-permute-start(f32[16,128]{1,0:T(8,128)S(1)} %get-tuple-element.31), channel_id=1, source_target_pairs={{0,1008},{16,32},{32,16},{48,64},{64,48},{80,96},{96,80},{112,128}... | collective-permute-start | bytes 24584 | tf_op jit(solution)/shard_map/ppermute | solution.py:391
  52.3 21.3 %all-to-all-start = ((f32[16,8,128]{2,1,0:T(8,128)}), f32[16,8,128]{2,1,0:T(8,128)S(1)}, u32[]{:S(2)}, u32[]{:S(2)}) async-start(f32[16,8,128]{2,1,0:T(8,128)} %bitcast.13), calls=%async_computation | async-start | bytes 131072 | tf_op jit(solution)/shard_map/all_to_all | solution.py:472
